TPU v7x, 256 devices: a whole 4x4x8 slice. The times are simulated.
256 devices in a mesh: seq: 128 (over y, z_lo, x, core), batch: 2 (over z_hi).
Axes of the slice: x: 4, y: 4, z: 8 (z_hi: 2, z_lo: 4; z = z_hi * 4 + z_lo), core: 2. Of those that a mesh axis runs over, the one named last changes fastest.
Arguments:
- queries: bfloat16 [2, 16384, 2048], P('batch', 'seq'), may hold values from -8 to 8
- key_rows: bfloat16 [2, 16384, 2048], P('batch', 'seq'), may hold values from -8 to 8
- values: bfloat16 [2, 16384, 2048], P('batch', 'seq'), may hold values from -6 to 6
- cotangent: bfloat16 [2, 16384, 2048], P('batch', 'seq'), may hold values from -6 to 6
- level_bias: float32 [3, 16], replicated, may hold values from -1 to 1
Outputs:
- attended: bfloat16 [2, 16384, 2048], P('batch', 'seq')
- query_grad: bfloat16 [2, 16384, 2048], P('batch', 'seq')
- key_grad: bfloat16 [2, 16384, 2048], P('batch', 'seq')
- value_grad: bfloat16 [2, 16384, 2048], P('batch', 'seq')
- level_grad: float32 [3, 16], replicated
All inputs are finite; a program needn't handle non-finite values.
Results may differ from a plain program's by a relative error of at most 0.0025.
The roundings to bfloat16 on the way count: a program that leaves them out, or rounds other values in their place, can miss the bound.
Values may be sent and summed in bfloat16 or wider, within the bound.
No kernel may reach another device: no remote copies, remote signals or barrier semaphores. Data moves between devices by JAX's collectives and lax.ppermute only.
A program may use at most 128 MiB of HBM per device.

v0:
```python
import math

import jax
import jax.numpy as jnp
from jax import lax
from jax.sharding import PartitionSpec as P

POOL1 = 16
POOL2 = 128
GROUP = 16


NEGATIVE = -1e30


def passed_along(x, axis, by):
    size = lax.axis_size(axis)
    pairs = [(i, i + by) for i in range(size) if 0 <= i + by < size]
    return lax.ppermute(x, axis, pairs)


def partner_2(x, axis, distance):
    return lax.ppermute(x, axis, [(i, i ^ 1 << distance) for i in range(lax.axis_size(axis))])


def pooled(x, factor):
    b, n, d = x.shape
    return (
        jnp.sum(x.reshape(b, n // factor, factor, d), axis=2, dtype=jnp.float32) / factor
    ).astype(jnp.bfloat16)


def spread(x, factor):
    b, n, d = x.shape
    return jnp.broadcast_to((x / factor)[:, :, None, :], (b, n, factor, d)).reshape(
        b, n * factor, d
    )


def offsets(level_bias, fine_ok, group_ok, far_ok):
    fine_part = level_bias[0][:, None] + jnp.where(fine_ok, 0.0, NEGATIVE)[None, :]
    group_part = (
        level_bias[1][:, None] + math.log(POOL1) + jnp.where(group_ok, 0.0, NEGATIVE)[None, :]
    )
    far_part = level_bias[2][:, None] + math.log(POOL2) + jnp.where(far_ok, 0.0, NEGATIVE)[None, :]
    return jnp.concatenate([fine_part, group_part, far_part], axis=1)


def heads_of(x, head_count):
    b, n, d = x.shape
    return x.reshape(b, n, head_count, d // head_count)


def key_grads(score_low, weights_low, head_queries, head_cot, first_col, last_col, score_scale):
    grad_keys = (
        jnp.einsum(
            "bhtk,bthe->bkhe",
            score_low[..., first_col:last_col],
            head_queries,
            preferred_element_type=jnp.float32,
        )
        * score_scale
    )
    grad_values = jnp.einsum(
        "bhtk,bthe->bkhe",
        weights_low[..., first_col:last_col],
        head_cot,
        preferred_element_type=jnp.float32,
    )
    b, n, h, e = grad_keys.shape
    return (grad_keys.reshape(b, n, h * e), grad_values.reshape(b, n, h * e))


def body(queries, key_rows, values, cotangent, level_bias):
    b, block_rows, features = queries.shape
    head_count = level_bias.shape[1]
    score_scale = (features // head_count) ** (-0.5)
    axis_count = lax.axis_size("seq")
    this_index = lax.axis_index("seq")
    bit_count = GROUP.bit_length() - 1
    near_left = passed_along((key_rows, values), "seq", 1)
    near_right = passed_along((key_rows, values), "seq", -1)
    group_rows = block_rows // POOL1
    gathered = jnp.stack([pooled(key_rows, POOL1), pooled(values, POOL1)])
    bit_order = list(range(bit_count))
    for bit_number in bit_order:
        partner = partner_2(gathered, "seq", bit_number)
        upper_side = this_index >> bit_number & 1 == 1
        gathered = jnp.where(
            upper_side,
            jnp.concatenate([partner, gathered], 2),
            jnp.concatenate([gathered, partner], 2),
        )
    distant = lax.all_gather(
        jnp.stack([pooled(key_rows, POOL2), pooled(values, POOL2)]), "seq", axis=2, tiled=True
    )
    far_total = distant.shape[2]
    far_rows = far_total // axis_count
    fine_end = 3 * block_rows
    group_end = fine_end + GROUP * group_rows
    fine_owner = this_index - 1 + jnp.arange(fine_end, dtype=jnp.int32) // block_rows
    fine_ok = (fine_owner >= 0) & (fine_owner < axis_count)
    group_owner = (
        this_index // GROUP * GROUP + jnp.arange(GROUP * group_rows, dtype=jnp.int32) // group_rows
    )
    group_ok = jnp.abs(group_owner - this_index) >= 2
    far_owner = jnp.arange(far_total, dtype=jnp.int32) // far_rows
    far_ok = (far_owner // GROUP != this_index // GROUP) & (jnp.abs(far_owner - this_index) >= 2)
    offset = offsets(level_bias, fine_ok, group_ok, far_ok)
    key_all = jnp.concatenate(
        [near_left[0], key_rows, near_right[0], gathered[0], distant[0]], axis=1
    )
    value_all = jnp.concatenate(
        [near_left[1], values, near_right[1], gathered[1], distant[1]], axis=1
    )
    head_queries = heads_of(queries, head_count)
    head_keys = heads_of(key_all, head_count)
    head_values = heads_of(value_all, head_count)
    head_cot = heads_of(cotangent, head_count)
    scores = (
        jnp.einsum("bthe,bkhe->bhtk", head_queries, head_keys, preferred_element_type=jnp.float32)
        * score_scale
        + offset[None, :, None, :]
    )
    row_top = jnp.max(scores, axis=-1, keepdims=True)
    log_total = row_top + jnp.log(jnp.sum(jnp.exp(scores - row_top), axis=-1, keepdims=True))
    weights = jnp.exp(scores - log_total)
    weights_low = weights.astype(jnp.bfloat16)
    attended = (
        jnp.einsum("bhtk,bkhe->bthe", weights_low, head_values, preferred_element_type=jnp.float32)
        .reshape(b, block_rows, features)
        .astype(jnp.bfloat16)
    )
    weight_grad = jnp.einsum(
        "bthe,bkhe->bhtk", head_cot, head_values, preferred_element_type=jnp.float32
    )
    row_delta = jnp.sum(weights * weight_grad, axis=-1, keepdims=True)
    score_grad = weights * (weight_grad - row_delta)
    score_low = score_grad.astype(jnp.bfloat16)
    query_grad = (
        (
            jnp.einsum("bhtk,bkhe->bthe", score_low, head_keys, preferred_element_type=jnp.float32)
            * score_scale
        )
        .reshape(b, block_rows, features)
        .astype(jnp.bfloat16)
    )
    level_terms = jnp.stack(
        [
            jnp.sum(score_grad[..., :fine_end], axis=(0, 2, 3)),
            jnp.sum(score_grad[..., fine_end:group_end], axis=(0, 2, 3)),
            jnp.sum(score_grad[..., group_end:], axis=(0, 2, 3)),
        ]
    )
    self_keys, self_values = key_grads(
        score_low, weights_low, head_queries, head_cot, block_rows, 2 * block_rows, score_scale
    )
    member_keys, member_values = key_grads(
        score_low, weights_low, head_queries, head_cot, fine_end, group_end, score_scale
    )
    distant_keys, distant_values = key_grads(
        score_low, weights_low, head_queries, head_cot, group_end, key_all.shape[1], score_scale
    )
    before_keys, before_values = key_grads(
        score_low, weights_low, head_queries, head_cot, 0, block_rows, score_scale
    )
    after_keys, after_values = key_grads(
        score_low, weights_low, head_queries, head_cot, 2 * block_rows, fine_end, score_scale
    )
    from_next = passed_along((before_keys, before_values), "seq", -1)
    from_prev = passed_along((after_keys, after_values), "seq", 1)
    fine_keys = self_keys + from_next[0] + from_prev[0]
    fine_values = self_values + from_next[1] + from_prev[1]
    buffer = jnp.stack([member_keys, member_values])
    for bit_number in bit_order[::-1]:
        half_rows = buffer.shape[2] // 2
        low_half = buffer[:, :, :half_rows]
        high_half = buffer[:, :, half_rows:]
        upper_side = this_index >> bit_number & 1 == 1
        outgoing = jnp.where(upper_side, low_half, high_half)
        kept_half = jnp.where(upper_side, high_half, low_half)
        buffer = kept_half + partner_2(outgoing, "seq", bit_number)
    far_sums = (
        lax.psum_scatter(distant_keys, "seq", scatter_dimension=1, tiled=True),
        lax.psum_scatter(distant_values, "seq", scatter_dimension=1, tiled=True),
    )
    key_grad = (fine_keys + spread(buffer[0], POOL1) + spread(far_sums[0], POOL2)).astype(
        jnp.bfloat16
    )
    value_grad = (fine_values + spread(buffer[1], POOL1) + spread(far_sums[1], POOL2)).astype(
        jnp.bfloat16
    )
    level_grad = lax.psum(level_terms, ("seq", "batch"))
    return (attended, query_grad, key_grad, value_grad, level_grad)


def solution(mesh):
    return jax.shard_map(
        body,
        mesh=mesh,
        in_specs=(
            P("batch", "seq", None),
            P("batch", "seq", None),
            P("batch", "seq", None),
            P("batch", "seq", None),
            P(),
        ),
        out_specs=(
            P("batch", "seq", None),
            P("batch", "seq", None),
            P("batch", "seq", None),
            P("batch", "seq", None),
            P(),
        ),
        check_vma=False,
    )
```

profile of v0, /device:TPU:0, one launch (start us, length us, event | category | flops | bytes accessed | tf_op | source)
XLA Modules:
  0.0 1605.4 jit_solution(2246195651047972147)
XLA Ops:
  7.3 2.1 copy.182
  9.4 2.1 collective-permute-start
  12.8 2.0 copy.197
  14.8 3.8 collective-permute-start.6
  24.0 2.0 copy.202
  26.0 2.1 copy.210
  30.6 4.1 collective-permute-done.3
  36.7 4.6 collective-permute-start.4
  42.7 4.6 collective-permute-done.4
  47.8 2.1 fusion.32
  49.9 2.2 maximum_select_fusion
  52.1 2.3 copy.191
  54.4 5.8 collective-permute-start.5
  60.2 1.9 constant_dynamic-update-slice_fusion.4
  66.6 2.0 constant_dynamic-update-slice_fusion.3
  68.6 2.0 constant_dynamic-update-slice_fusion.2
  70.6 2.0 copy.203
  74.9 2.1 constant_dynamic-update-slice_fusion.7
  85.0 142.9 %all-gather.2.cloned.1.call-done = bf16[2,1,128,2048]{3,0,1,2:T(2,128)(2,1)} async-done(((bf16[2,1,1,2048]{3,0,1,2:T(2,128)(2,1)}), bf16[2,1,128,2048]{3,0,1,2:T(2,128)(2,1)}) %all-gather.2.cloned.1.call-update) | async-done | bytes 1048592 | tf_op jit(solution)/shard_map/all_gather | solution.py:94
  228.0 4.1 fusion.58
  232.1 2.4 copy.284
  236.6 3.6 bitcast_reduce_fusion
  243.8 4.6 fusion
  248.6 3.8 convert_bitcast_fusion
  252.4 1.9 fusion.17
  263.9 1.9 fusion.12
  265.8 3.2 copy.235
  270.0 2.2 slice_reduce_fusion
  274.3 3.6 copy.249
  278.0 2.0 copy.262
  280.0 2.7 fusion.40
  282.6 2.5 fusion.42
  285.1 4.4 fusion.22
  289.5 4.5 collective-permute-done.10
  294.0 3.1 copy.236
  297.1 3.6 select_add_fusion.3
  300.7 1.9 slice_select_fusion.2
  302.6 2.2 copy.237
  304.8 2.0 collective-permute-start.11
  306.8 5.8 fusion.27
  312.6 6.5 collective-permute-done.11
  319.1 3.0 copy.238
  322.0 2.2 select_add_fusion.2
  327.6 2.5 fusion.41
  330.2 3.0 collective-permute-done.12
  333.2 2.0 copy.240
  335.2 3.5 select_add_fusion.1
  338.7 1.9 slice_select_fusion
  340.6 2.2 copy.241
  342.9 1.8 slice_reduce_fusion.2
  345.7 2.1 copy.264
  347.9 2.5 copy.228
  350.4 3.6 collective-permute-start.9
  354.0 2.6 copy.224
  359.3 2.6 copy.258
  361.9 4.0 collective-permute-start.15
  367.3 2.6 copy.254
  371.2 92.2 %psum.7 = f32[3,16]{1,0:T(4,128)} all-reduce(f32[3,16]{1,0:T(4,128)S(1)} %pad_maximum_fusion.6), channel_id=1, replica_groups=mesh['seq'=128,'batch'=2] {'seq','batch'}, use_global_device_ids=true, to_apply=%region_12.13 | all-reduce | flops 48 | bytes 384 | tf_op jit(solution)/shard_map/psum | solution.py:193
  463.4 1.9 copy.242
  465.3 2.2 select_add_fusion
  470.9 1117.2 %all-reduce.5.cloned.1.call-done = (f32[1,128,2048]{2,0,1:T(1,128)}, f32[1,128,2048]{2,0,1:T(1,128)}) async-done(((f32[1,128,2048]{2,0,1:T(1,128)}, f32[1,128,2048]{2,0,1:T(1,128)}), (f32[1,128,2048]{2,0,1:T(1,128)}, f32[1,128,2048]{2,0,1:T(1,128)})) %all-reduce.5.cloned.1.call-update) | async-done | bytes 2097168
  1589.5 2.8 fusion.38
  1592.2 2.0 copy.265
  1595.7 2.6 fusion.34
  (149 shorter events, 61.9 us)
Async XLA Ops:
  7.2 14.0 copy-start.6
  7.2 15.6 copy-start.7
  7.2 16.5 %copy-start.20 = (f32[3,16]{1,0:T(4,128)S(1)}, f32[3,16]{1,0:T(4,128)}, u32[]{:S(2)}) copy-start(f32[3,16]{1,0:T(4,128)} %param.9) | copy-start | bytes 580
  7.2 16.5 %copy-start.17 = (bf16[1,128,2048]{2,1,0:T(8,128)(2,1)S(1)}, bf16[1,128,2048]{2,1,0:T(8,128)(2,1)}, u32[]{:S(2)}) copy-start(bf16[1,128,2048]{2,1,0:T(8,128)(2,1)} %param.5) | copy-start | bytes 1572868
  7.2 220.7 %all-gather.2.cloned.1.call-start = ((), (), s32[]{:S(2)}) async-start(), calls=%async_computation | async-start | bytes 1056768 | tf_op jit(solution)/shard_map/all_gather | solution.py:94
  9.4 50.8 %collective-permute-start = (bf16[1,128,2048]{1,2,0:T(8,128)(2,1)}, bf16[1,128,2048]{1,2,0:T(8,128)(2,1)}, u32[]{:S(2)}, u32[]{:S(2)}) collective-permute-start(bf16[1,128,2048]{1,2,0:T(8,128)(2,1)} %copy.182), channel_id=1, source_target_pairs={{0,2},{2,4},{4,6},{6,8},{8,10},{10,12},{12,14},{14,16},{16,18},{18... | collective-permute-start | bytes 1572872 | tf_op jit(solution)/shard_map/ppermute | solution.py:19
  11.5 57.1 %collective-permute-start.1 = (bf16[1,128,2048]{1,2,0:T(8,128)(2,1)}, bf16[1,128,2048]{1,2,0:T(8,128)(2,1)}, u32[]{:S(2)}, u32[]{:S(2)}) collective-permute-start(bf16[1,128,2048]{1,2,0:T(8,128)(2,1)} %copy.182), channel_id=1, source_target_pairs={{2,0},{4,2},{6,4},{8,6},{10,8},{12,10},{14,12},{16,14},{18,16},{20... | collective-permute-start | bytes 1572872 | tf_op jit(solution)/shard_map/ppermute | solution.py:19
  14.8 47.3 %collective-permute-start.6 = (bf16[1,128,2048]{1,2,0:T(8,128)(2,1)}, bf16[1,128,2048]{1,2,0:T(8,128)(2,1)}, u32[]{:S(2)}, u32[]{:S(2)}) collective-permute-start(bf16[1,128,2048]{1,2,0:T(8,128)(2,1)} %copy.197), channel_id=1, source_target_pairs={{0,2},{2,4},{4,6},{6,8},{8,10},{10,12},{12,14},{14,16},{16,18},{18... | collective-permute-start | bytes 1572872 | tf_op jit(solution)/shard_map/ppermute | solution.py:19
  18.7 51.9 %collective-permute-start.7 = (bf16[1,128,2048]{1,2,0:T(8,128)(2,1)}, bf16[1,128,2048]{1,2,0:T(8,128)(2,1)}, u32[]{:S(2)}, u32[]{:S(2)}) collective-permute-start(bf16[1,128,2048]{1,2,0:T(8,128)(2,1)} %copy.197), channel_id=1, source_target_pairs={{2,0},{4,2},{6,4},{8,6},{10,8},{12,10},{14,12},{16,14},{18,16},{20... | collective-permute-start | bytes 1572872 | tf_op jit(solution)/shard_map/ppermute | solution.py:19
  21.2 6.9 copy-start.18
  21.4 7.8 collective-permute-start.2
  22.7 5.8 copy-start.21
  23.6 1564.5 %all-reduce.5.cloned.1.call-start = ((), (), s32[]{:S(2)}) async-start(), calls=%async_computation.1 | async-start | bytes 4194304
  29.2 5.5 collective-permute-start.3
  36.7 10.6 collective-permute-start.4
  54.4 24.5 %collective-permute-start.5 = (bf16[2,1,64,2048]{3,2,1,0:T(8,128)(2,1)}, bf16[2,1,64,2048]{3,2,1,0:T(8,128)(2,1)}, u32[]{:S(2)}, u32[]{:S(2)}) collective-permute-start(bf16[2,1,64,2048]{3,2,1,0:T(8,128)(2,1)} %copy.191), channel_id=1, source_target_pairs={{0,16},{2,18},{4,20},{6,22},{8,24},{10,26},{12,28},{14,30},{16,0},... | collective-permute-start | bytes 1572872 | tf_op jit(solution)/shard_map/ppermute | solution.py:23
  65.7 8.3 copy-start.16
  68.6 8.5 copy-start.15
  74.9 5.5 copy-start.10
  240.2 2.4 copy-start
  243.8 4.6 slice-start
  243.8 4.8 slice-start.1
  252.4 8.4 copy-start.3
  260.8 5.0 copy-start.4
  263.9 5.1 copy-start.5
  269.0 4.1 copy-start.11
  269.0 25.0 %collective-permute-start.10 = (f32[2,1,64,2048]{3,2,1,0:T(8,128)}, f32[2,1,64,2048]{3,2,1,0:T(8,128)}, u32[]{:S(2)}, u32[]{:S(2)}) collective-permute-start(f32[2,1,64,2048]{3,2,1,0:T(8,128)} %copy.235), channel_id=1, source_target_pairs={{0,16},{2,18},{4,20},{6,22},{8,24},{10,26},{12,28},{14,30},{16,0},... | collective-permute-start | bytes 3145736 | tf_op jit(solution)/shard_map/ppermute | solution.py:23
  272.1 5.8 copy-start.12
  280.0 5.2 copy-start.2
  304.8 14.3 collective-permute-start.11
  324.3 1.3 copy-start.1
  326.8 6.4 collective-permute-start.12
  340.6 4.1 copy-start.19
  342.9 120.5 %collective-permute-start.13 = (f32[2,1,8,2048]{3,2,1,0:T(8,128)S(1)}, f32[2,1,8,2048]{3,2,1,0:T(8,128)S(1)}, u32[]{:S(2)}, u32[]{:S(2)}) collective-permute-start(f32[2,1,8,2048]{3,2,1,0:T(8,128)S(1)} %copy.241), channel_id=1, source_target_pairs={{0,2},{2,0},{4,6},{6,4},{8,10},{10,8},{12,14},{14,12},{16,18},{18,... | collective-permute-start | bytes 393224 | tf_op jit(solution)/shard_map/ppermute | solution.py:23
  345.7 12.2 copy-start.8
  350.4 1239.0 %collective-permute-start.9 = (f32[1,128,2048]{1,2,0:T(8,128)}, f32[1,128,2048]{1,2,0:T(8,128)}, u32[]{:S(2)}, u32[]{:S(2)}) collective-permute-start(f32[1,128,2048]{1,2,0:T(8,128)} %bitcast.281), channel_id=1, source_target_pairs={{0,2},{2,4},{4,6},{6,8},{8,10},{10,12},{12,14},{14,16},{16,18},{18... | collective-permute-start | bytes 3145736 | tf_op jit(solution)/shard_map/ppermute | solution.py:19
  356.6 1232.8 %collective-permute-start.8 = (f32[1,128,2048]{1,2,0:T(8,128)}, f32[1,128,2048]{1,2,0:T(8,128)}, u32[]{:S(2)}, u32[]{:S(2)}) collective-permute-start(f32[1,128,2048]{1,2,0:T(8,128)} %bitcast.282), channel_id=1, source_target_pairs={{2,0},{4,2},{6,4},{8,6},{10,8},{12,10},{14,12},{16,14},{18,16},{20... | collective-permute-start | bytes 3145736 | tf_op jit(solution)/shard_map/ppermute | solution.py:19
  359.3 6.6 copy-start.9
  361.9 1233.7 %collective-permute-start.15 = (f32[1,128,2048]{2,1,0:T(8,128)}, f32[1,128,2048]{2,1,0:T(8,128)}, u32[]{:S(2)}, u32[]{:S(2)}) collective-permute-start(f32[1,128,2048]{2,1,0:T(8,128)} %copy.258), channel_id=1, source_target_pairs={{0,2},{2,4},{4,6},{6,8},{8,10},{10,12},{12,14},{14,16},{16,18},{18... | collective-permute-start | bytes 3145736 | tf_op jit(solution)/shard_map/ppermute | solution.py:19
  369.9 1225.7 %collective-permute-start.14 = (f32[1,128,2048]{2,1,0:T(8,128)}, f32[1,128,2048]{2,1,0:T(8,128)}, u32[]{:S(2)}, u32[]{:S(2)}) collective-permute-start(f32[1,128,2048]{2,1,0:T(8,128)} %copy.254), channel_id=1, source_target_pairs={{2,0},{4,2},{6,4},{8,6},{10,8},{12,10},{14,12},{16,14},{18,16},{20... | collective-permute-start | bytes 3145736 | tf_op jit(solution)/shard_map/ppermute | solution.py:19
  468.7 1120.8 %copy-start.14 = (f32[1,128,16,128]{1,3,2,0:T(8,128)S(1)}, f32[1,128,16,128]{1,3,2,0:T(8,128)}, u32[]{:S(2)}) copy-start(f32[1,128,16,128]{1,3,2,0:T(8,128)} %copy.220) | copy-start | bytes 3145732
  1589.5 6.3 copy-start.13
Sparse Core Ops, SparseCore 0:
  23.7 204.2 all-gather.1
  280.1 1307.9 all-reduce.4
where the time goes:
time: 1610 us
  waiting for transfers between devices  1280 us (80%)
  local copies, waits for them, and re-layouts  98.4 us (6%)
  blocking collectives  92.2 us (6%)
  other arithmetic  45.3 us (3%)
  matrix products  35.9 us (2%)
  starting transfers between devices  35.8 us (2%)
    unnamed x3, waiting for transfers between devices  1120 us
    all_gather x1, waiting for transfers between devices, body(): lax.all_gather(jnp.stack([pooled(key_rows, POOL2), pooled(values, POOL2)]...  143 us
    psum x1, blocking collectives, body(): level_grad = lax.psum(level_terms, ('seq', 'batch'))  92.2 us
  transfers between devices with their start and end apart: 18, of which 7 were waited for; matrix products, arithmetic and copies ran while one was open for 8% of the time, Pallas kernels for 0%

commit v1 on v0

v1 whole, which is shorter than its diff:
```python
import functools
import math

import jax
import jax.numpy as jnp
from jax import lax
from jax.experimental import pallas as pl
from jax.experimental.pallas import tpu as pltpu
from jax.sharding import PartitionSpec as P

POOL1 = 16
POOL2 = 128
GROUP = 16
ROWS = 128
HEAD = 128
NEGATIVE = -1e30
LOG1 = math.log(POOL1)
LOG2 = math.log(POOL2)

SIB, Z1, YA, YB = 1, 16, 32, 96

BF = jnp.bfloat16
F32 = jnp.float32


def swap(x, mask):
    return lax.ppermute(x, "seq", [(i, i ^ mask) for i in range(lax.axis_size("seq"))])


def cross(x):
    size = lax.axis_size("seq")
    pairs = [(i, i + 1) for i in range(1, size - 1, 2)]
    return lax.ppermute(x, "seq", pairs + [(j, i) for i, j in pairs])


def in_group(x):
    size = lax.axis_size("seq")
    groups = [[g + i for i in range(GROUP)] for g in range(0, size, GROUP)]
    return lax.all_to_all(x, "seq", 0, 0, axis_index_groups=groups)


def params(limit=24):
    return pltpu.CompilerParams(vmem_limit_bytes=limit * 1024 * 1024)


def cost(us):
    return pl.CostEstimate(flops=0, bytes_accessed=int(us * 3.3e6), transcendentals=0)


def in_hbm(*arrays):
    return [pltpu.with_memory_space_constraint(x, pltpu.HBM) for x in arrays]


def out_hbm(shapes):
    return [pltpu.HBM(s.shape, s.dtype) for s in shapes]


def nt(a, b):
    return lax.dot_general(a, b, (((1,), (1,)), ((), ())), preferred_element_type=F32)


def nn(a, b):
    return lax.dot_general(a, b, (((1,), (0,)), ((), ())), preferred_element_type=F32)


def tn(a, b):
    return lax.dot_general(a, b, (((0,), (0,)), ((), ())), preferred_element_type=F32)


def pool_kernel(k_ref, v_ref, one_ref, two_ref):
    for n, ref in enumerate((k_ref, v_ref)):
        x = ref[...].astype(F32)
        sums = jnp.sum(x.reshape(ROWS // POOL1, POOL1, x.shape[-1]), axis=1)
        one_ref[8 * n : 8 * n + 8, :] = sums / POOL1
        row = jnp.sum(sums, axis=0, keepdims=True) / POOL2
        two_ref[0, n : n + 1, :] = row.astype(BF)


def pool(k, v):
    width = k.shape[1]
    return pl.pallas_call(
        pool_kernel,
        out_shape=(
            jax.ShapeDtypeStruct((16, width), F32),
            jax.ShapeDtypeStruct((1, 2, width), BF),
        ),
        compiler_params=params(),
        cost_estimate=cost(2),
    )(k, v)


def rows_kernel(one_ref, a_ref, b_ref, out_ref, far_ref):
    half = out_ref.shape[-1]
    for m, ref in enumerate((a_ref, b_ref)):
        for r in range(4):
            pair = ref[r].astype(F32)
            for n in range(2):
                to = 8 * n + 4 * m + r
                far_ref[to : to + 1, :] = pair[n : n + 1, :]
    for c in range(2):
        cols = slice(c * half, (c + 1) * half)
        one = one_ref[:, cols].astype(BF)
        far = far_ref[:, cols].astype(BF)
        for p in range(GROUP // 2):
            out_ref[2 * p + c, 0:16] = one
            out_ref[2 * p + c, 16:32] = far


def level_rows(one, a, b):
    width = one.shape[1]
    return pl.pallas_call(
        rows_kernel,
        out_shape=jax.ShapeDtypeStruct((GROUP, 32, width // 2), BF),
        scratch_shapes=[pltpu.VMEM((16, width), F32)],
        compiler_params=params(),
        cost_estimate=cost(1),
    )(one, a, b)


def prepare_kernel(ids_ref, *refs):
    arrays, wholes, halves, sems = refs[:4], refs[4:6], refs[6:10], refs[10]
    half = halves[0].shape[-1]
    start = pl.multiple_of((1 - ids_ref[1]) * half, half)
    copies = []
    for n, (ref, out) in enumerate(zip(arrays, halves)):
        to = wholes[n // 2].at[(n % 2) * ROWS : (n % 2 + 1) * ROWS]
        copies.append(pltpu.make_async_copy(ref, to, sems.at[2 * n]))
        part = ref.at[:, pl.ds(start, half)]
        copies.append(pltpu.make_async_copy(part, out, sems.at[2 * n + 1]))
    for copy in copies:
        copy.start()
    for copy in copies:
        copy.wait()


def prepare(ids, *arrays):
    rows, width = arrays[0].shape
    smem = pl.BlockSpec(memory_space=pltpu.SMEM)
    hbm = pl.BlockSpec(memory_space=pltpu.HBM)
    return pl.pallas_call(
        prepare_kernel,
        in_specs=[smem] + [hbm] * 4,
        out_specs=[hbm] * 6,
        out_shape=[jax.ShapeDtypeStruct((2 * rows, width), BF)] * 2
        + [jax.ShapeDtypeStruct((rows, width // 2), BF)] * 4,
        scratch_shapes=[pltpu.SemaphoreType.DMA((8,))],
        compiler_params=params(),
        cost_estimate=cost(1),
    )(ids, *arrays)


def other_kernel(ids_ref, x_ref, out_ref, sem):
    half = out_ref.shape[-1]
    start = pl.multiple_of((1 - ids_ref[1]) * half, half)
    part = x_ref.at[0 : out_ref.shape[0], pl.ds(start, half)]
    copy = pltpu.make_async_copy(part, out_ref, sem)
    copy.start()
    copy.wait()


def other_half(ids, x, rows):
    smem = pl.BlockSpec(memory_space=pltpu.SMEM)
    hbm = pl.BlockSpec(memory_space=pltpu.HBM)
    return pl.pallas_call(
        other_kernel,
        in_specs=[smem, hbm],
        out_specs=hbm,
        out_shape=jax.ShapeDtypeStruct((rows, x.shape[1] // 2), BF),
        scratch_shapes=[pltpu.SemaphoreType.DMA],
        compiler_params=params(),
        cost_estimate=cost(1),
    )(ids, x)


def split_rows(x):
    wide = x.astype(F32).reshape(GROUP, 16, HEAD)
    keys = wide[:, :8].reshape(ROWS, HEAD).astype(BF)
    return keys, wide[:, 8:].reshape(ROWS, HEAD).astype(BF)


def join_rows(a, b):
    both = [x.reshape(GROUP, 8, HEAD) for x in (a, b)]
    return jnp.concatenate(both, axis=1).astype(BF)


def pieces(sums):
    lane = lax.broadcasted_iota(jnp.int32, (1, HEAD), 1)
    row = jnp.zeros((1, HEAD), F32)
    for n, s in enumerate(sums):
        row = jnp.where(lane % 3 == n, jnp.sum(s, axis=1, keepdims=True), row)
    high = row.astype(BF).astype(F32)
    middle = (row - high).astype(BF).astype(F32)
    rest = row - high - middle
    row = jnp.where(lane < 3, high, jnp.where(lane < 6, middle, rest))
    return jnp.where(lane < 9, row, 0.0)


def attend_kernel(
    steps,
    heads,
    ids_ref,
    bias_ref,
    q_ref,
    k_ref,
    v_ref,
    c_ref,
    sq_ref,
    sk_ref,
    sv_ref,
    sc_ref,
    xk_ref,
    xv_ref,
    sxk_ref,
    sxv_ref,
    level_ref,
    att_ref,
    satt_ref,
    dq_ref,
    sdq_ref,
    dk_ref,
    dv_ref,
    sdk_ref,
    sdv_ref,
    glevel_ref,
    stat_ref,
    sstat_ref,
    mask_ref,
    edge_ref,
):
    step = pl.program_id(0)
    me, core = ids_ref[0], ids_ref[1]
    last = ids_ref[2] - 1
    scale = HEAD**-0.5

    @pl.when(step == 0)
    def _():
        row = lax.broadcasted_iota(jnp.int32, (ROWS, 2 * ROWS), 0)
        lane = lax.broadcasted_iota(jnp.int32, (ROWS, 2 * ROWS), 1)
        block = jnp.where(lane < ROWS, me, me ^ 1)
        group = me // GROUP
        place, which = row // 8, row % 8
        good = jnp.abs(group * GROUP + place - block) >= 2
        mask_ref[0:ROWS] = jnp.where(good, LOG1, NEGATIVE)
        owner = (group ^ (which ^ ((which >> 2) << 1))) * GROUP + place
        good = (which != 0) & (jnp.abs(owner - block) >= 2)
        mask_ref[ROWS:] = jnp.where(good, LOG2, NEGATIVE)
        lane = lane[0:8]
        block = block[0:8]
        edge_ref[...] = jnp.where((block == 0) | (block == last), NEGATIVE, 0.0)

    for j in range(heads):
        cols = slice(j * HEAD, (j + 1) * HEAD)
        head = step * heads + j
        whole_head = core * (steps * heads) + head
        bias = [bias_ref[n, whole_head] for n in range(3)]
        q, sq, c, sc = q_ref[:, cols], sq_ref[:, cols], c_ref[:, cols], sc_ref[:, cols]
        k_near = jnp.concatenate([k_ref[:, cols], sk_ref[:, cols]], axis=0)
        v_near = jnp.concatenate([v_ref[:, cols], sv_ref[:, cols]], axis=0)
        xk, xv, sxk, sxv = (
            ref[:, cols] for ref in (xk_ref, xv_ref, sxk_ref, sxv_ref)
        )
        k_one, v_one = split_rows(level_ref[:, 0:16, cols])
        k_two, v_two = split_rows(level_ref[:, 16:32, cols])
        k_far = jnp.concatenate([k_one, k_two], axis=0)
        v_far = jnp.concatenate([v_one, v_two], axis=0)
        q_both = jnp.concatenate([q, sq], axis=0)
        c_both = jnp.concatenate([c, sc], axis=0)

        s_near = nt(k_near, q_both) * scale + bias[0]
        s_edge = jnp.concatenate([nt(xk, q), nt(sxk, sq)], axis=1) * scale + (
            edge_ref[0:1] + bias[0]
        )
        s_far = nt(k_far, q_both) * scale
        s_one = s_far[0:ROWS] + (mask_ref[0:ROWS] + bias[1])
        s_two = s_far[ROWS:] + (mask_ref[ROWS:] + bias[2])
        scores = [s_near, s_edge, s_one, s_two]
        top = functools.reduce(
            jnp.maximum, [jnp.max(s, axis=0, keepdims=True) for s in scores]
        )
        powers = [jnp.exp(s - top) for s in scores]
        total = sum(jnp.sum(p, axis=0, keepdims=True) for p in powers)
        share = 1.0 / total
        weights = [p * share for p in powers]

        g_far = nt(v_far, c_both)
        grads = [
            nt(v_near, c_both),
            jnp.concatenate([nt(xv, c), nt(sxv, sc)], axis=1),
            g_far[0:ROWS],
            g_far[ROWS:],
        ]
        delta = sum(
            jnp.sum(w * g, axis=0, keepdims=True) for w, g in zip(weights, grads)
        )
        score_grads = [w * (g - delta) for w, g in zip(weights, grads)]
        w_near, w_edge, w_one, w_two = [w.astype(BF) for w in weights]
        d_near, d_edge, d_one, d_two = [d.astype(BF) for d in score_grads]
        w_far = jnp.concatenate([w_one, w_two], axis=0)
        d_far = jnp.concatenate([d_one, d_two], axis=0)

        att = tn(w_near, v_near) + tn(w_far, v_far)
        att_ref[:, cols] = (att[0:ROWS] + tn(w_edge[:, 0:ROWS], xv)).astype(BF)
        satt_ref[:, cols] = (att[ROWS:] + tn(w_edge[:, ROWS:], sxv)).astype(BF)
        dq = tn(d_near, k_near) + tn(d_far, k_far)
        dq_ref[:, cols] = ((dq[0:ROWS] + tn(d_edge[:, 0:ROWS], xk)) * scale).astype(BF)
        sdq_ref[:, cols] = ((dq[ROWS:] + tn(d_edge[:, ROWS:], sxk)) * scale).astype(BF)

        dk = nn(d_near, q_both) * scale
        dk_ref[:, cols] = dk[0:ROWS]
        sdk_ref[:, cols] = dk[ROWS:]
        dv = nn(w_near, c_both)
        dv_ref[:, cols] = dv[0:ROWS]
        sdv_ref[:, cols] = dv[ROWS:]
        dk = nn(d_far, q_both) * scale
        dv = nn(w_far, c_both)
        glevel_ref[:, 0:16, cols] = join_rows(dk[0:ROWS], dv[0:ROWS])
        sums = [jnp.sum(d, axis=0, keepdims=True) for d in score_grads]
        level = pieces([sums[0] + sums[1], sums[2], sums[3]])
        first = lax.broadcasted_iota(jnp.int32, (ROWS, HEAD), 0) % 8 == 0
        glevel_ref[:, 16:32, cols] = join_rows(
            jnp.where(first, level, dk[ROWS:]), dv[ROWS:]
        )

        log_total = top + jnp.log(total)
        row = pl.ds(head, 1)
        low = pl.ds(head + 8, 1)
        stat_ref[row] = log_total[:, 0:ROWS]
        sstat_ref[row] = log_total[:, ROWS:]
        stat_ref[low] = delta[:, 0:ROWS]
        sstat_ref[low] = delta[:, ROWS:]


def attend(ids, bias, own, sib, x, sx, level):
    width = own[0].shape[1]
    half = width // 2
    heads = 2
    block = heads * HEAD
    steps = half // block
    rows = ROWS

    def mine(n, at=0):
        return pl.BlockSpec((n, block), lambda i, ids: (at, ids[1] * steps + i))

    def part(n, at=0):
        return pl.BlockSpec((n, block), lambda i, ids: (at, i))

    rows_of = pl.BlockSpec((GROUP, 32, block), lambda i, ids: (0, 0, i))
    stat = pl.BlockSpec((16, rows), lambda i, ids: (0, 0))
    low = jax.ShapeDtypeStruct((rows, half), BF)
    high = jax.ShapeDtypeStruct((rows, half), F32)
    stats = jax.ShapeDtypeStruct((16, rows), F32)
    return pl.pallas_call(
        functools.partial(attend_kernel, steps, heads),
        grid_spec=pltpu.PrefetchScalarGridSpec(
            num_scalar_prefetch=1,
            grid=(steps,),
            in_specs=[pl.BlockSpec(memory_space=pltpu.SMEM)]
            + [mine(rows)] * 4
            + [part(rows)] * 4
            + [mine(rows), mine(rows, 1), part(rows), part(rows, 1)]
            + [rows_of],
            out_specs=[part(rows)] * 8 + [rows_of] + [stat] * 2,
            scratch_shapes=[
                pltpu.VMEM((2 * rows, 2 * rows), F32),
                pltpu.VMEM((8, 2 * rows), F32),
            ],
        ),
        out_shape=out_hbm(
            [low] * 4
            + [high] * 4
            + [jax.ShapeDtypeStruct((GROUP, 32, half), BF)]
            + [stats] * 2
        ),
        compiler_params=params(),
        cost_estimate=cost(9),
    )(ids, bias, *in_hbm(*own, *sib, x, x, sx, sx, level))


def edge_kernel(
    per_half,
    heads,
    ids_ref,
    bias_ref,
    k_ref,
    v_ref,
    q_ref,
    c_ref,
    stat_ref,
    att_ref,
    satt_ref,
    dq_ref,
    sdq_ref,
    dk_ref,
    sdk_ref,
    dv_ref,
    sdv_ref,
    out_att_ref,
    out_dq_ref,
    out_dk_ref,
    out_dv_ref,
):
    step = pl.program_id(0)
    mine = step // per_half == ids_ref[1]
    scale = HEAD**-0.5
    out_att_ref[...] = jnp.where(mine, att_ref[...], satt_ref[...])
    out_dq_ref[...] = jnp.where(mine, dq_ref[...], sdq_ref[...])
    for j in range(heads):
        cols = slice(j * HEAD, (j + 1) * HEAD)
        bias = bias_ref[0, step * heads + j]
        row = lax.rem(step, per_half) * heads + j
        log_total = stat_ref[0, pl.ds(row, 1)]
        delta = stat_ref[0, pl.ds(row + 8, 1)]
        q, c = q_ref[:, cols], c_ref[:, cols]
        weights = jnp.exp(nt(k_ref[:, cols], q) * scale + (bias - log_total))
        score_grad = weights * (nt(v_ref[:, cols], c) - delta)
        dk = jnp.where(mine, dk_ref[:, cols], sdk_ref[:, cols])
        dv = jnp.where(mine, dv_ref[:, cols], sdv_ref[:, cols])
        out_dk_ref[:, cols] = dk + nn(score_grad.astype(BF), q) * scale
        out_dv_ref[:, cols] = dv + nn(weights.astype(BF), c)


def edge(ids, bias, k, v, x, stat, parts):
    rows, width = k.shape
    heads = 4
    block = heads * HEAD
    per_half = width // 2 // block
    whole = pl.BlockSpec((rows, block), lambda i, ids: (0, i))
    part = pl.BlockSpec((rows, block), lambda i, ids: (0, lax.rem(i, per_half)))
    return pl.pallas_call(
        functools.partial(edge_kernel, per_half, heads),
        grid_spec=pltpu.PrefetchScalarGridSpec(
            num_scalar_prefetch=1,
            grid=(2 * per_half,),
            in_specs=[
                pl.BlockSpec(memory_space=pltpu.SMEM),
                whole,
                whole,
                pl.BlockSpec((rows, block), lambda i, ids: (0, i)),
                pl.BlockSpec((rows, block), lambda i, ids: (1, i)),
                pl.BlockSpec((1, 16, rows), lambda i, ids: (i // per_half, 0, 0)),
            ]
            + [part] * 8,
            out_specs=[whole] * 4,
        ),
        out_shape=out_hbm(
            [jax.ShapeDtypeStruct((rows, width), t) for t in (BF, BF, F32, F32)]
        ),
        compiler_params=params(),
        cost_estimate=cost(4),
    )(ids, bias, *in_hbm(k, v, x, x, stat, *parts))


def sums_kernel(x_ref, one_ref, low_ref, high_ref, level_ref):
    total = jnp.sum(x_ref[:, 0].astype(F32), axis=0)
    one_ref[...] = total[0:16]
    zero = jnp.zeros((1, total.shape[-1]), F32)
    for n in range(2):
        at = 16 + 8 * n
        for r in range(4):
            row = total[at + r : at + r + 1]
            low_ref[r, n : n + 1, :] = row if r else zero
            high_ref[r, n : n + 1, :] = total[at + 4 + r : at + 5 + r]
        row = total[at : at + 1]
        high_ref[4, n : n + 1, :] = row
        level_ref[0, n : n + 1, :] = row


def sums(x):
    half = x.shape[-1]
    block = 512
    per_half = half // block
    x = x.reshape(GROUP // 2, 2, 32, half)
    return pl.pallas_call(
        sums_kernel,
        grid=(2 * per_half,),
        in_specs=[
            pl.BlockSpec(
                (GROUP // 2, 1, 32, block),
                lambda i: (0, i // per_half, 0, lax.rem(i, per_half)),
            )
        ],
        out_specs=[pl.BlockSpec((16, block), lambda i: (0, i))]
        + [pl.BlockSpec((n, 2, block), lambda i: (0, 0, i)) for n in (4, 5, 1)],
        out_shape=[jax.ShapeDtypeStruct((16, 2 * half), F32)]
        + [jax.ShapeDtypeStruct((n, 2, 2 * half), F32) for n in (4, 5, 1)],
        compiler_params=params(),
        cost_estimate=cost(1),
    )(x)


def final_kernel(one_ref, far_ref, dk_ref, dv_ref, out_dk_ref, out_dv_ref):
    total = one_ref[...] / POOL1
    for n, (ref, out) in enumerate(((dk_ref, out_dk_ref), (dv_ref, out_dv_ref))):
        rows = total[8 * n : 8 * n + 8] + far_ref[0, n : n + 1, :] / POOL2
        for r in range(8):
            at = slice(r * POOL1, (r + 1) * POOL1)
            out[at] = (ref[at] + rows[r : r + 1]).astype(BF)


def final(one, far, dk, dv):
    rows, width = dk.shape
    block = 512
    whole = pl.BlockSpec((rows, block), lambda i: (0, i))
    return pl.pallas_call(
        final_kernel,
        grid=(width // block,),
        in_specs=[
            pl.BlockSpec((16, block), lambda i: (0, i)),
            pl.BlockSpec((1, 2, block), lambda i: (0, 0, i)),
            whole,
            whole,
        ],
        out_specs=[whole] * 2,
        out_shape=[jax.ShapeDtypeStruct((rows, width), BF)] * 2,
        compiler_params=params(),
        cost_estimate=cost(2),
    )(one, far, dk, dv)


def body(queries, key_rows, values, cotangent, level_bias):
    q, k, v, c = queries[0], key_rows[0], values[0], cotangent[0]
    heads = level_bias.shape[1]
    size = lax.axis_size("seq")
    me = lax.axis_index("seq")
    core = me % 2
    ids = jnp.stack([me, core, size]).astype(jnp.int32)

    one, far = pool(k, v)
    far = jnp.concatenate([far, swap(far, Z1)], axis=0)
    far = jnp.concatenate([far, swap(far, YA)], axis=0)
    rows = level_rows(one, far, swap(far, YB))

    kv, qc, *sends = prepare(ids, k, v, q, c)
    sk, sv, sq, sc = [swap(s, SIB) for s in sends]
    x = cross(kv)
    rows, x = lax.optimization_barrier((rows, x))
    rows = in_group(rows)
    sx = swap(other_half(ids, x, 2 * ROWS), SIB)
    late, rows = lax.optimization_barrier((qc, rows))
    x_qc = cross(late)

    att, satt, dq, sdq, dk, dv, sdk, sdv, grads, stat, sstat = attend(
        ids, level_bias, (q, k, v, c), (sq, sk, sv, sc), x, sx, rows
    )

    grads, x_qc = lax.optimization_barrier((grads, x_qc))
    one, low, high, level = sums(in_group(grads))
    for mask in (YB, YA, Z1):
        got = swap(high, mask)
        low = low + got[:-1]
        level = level + got[-1:]
        half = low.shape[0] // 2
        high = jnp.concatenate([low[half:], level], axis=0)
        low = low[:half] if half else low

    rstat = swap(sstat, SIB)
    stats = jnp.where(core == 0, jnp.stack([stat, rstat]), jnp.stack([rstat, stat]))
    x_stats = cross(stats)
    ratt, rdq, rdk, rdv = [swap(s, SIB) for s in (satt, sdq, sdk, sdv)]
    att, dq, dk, dv = edge(
        ids,
        level_bias,
        k,
        v,
        x_qc,
        x_stats,
        (att, ratt, dq, rdq, dk, rdk, dv, rdv),
    )

    level = level + lax.ppermute(level, "batch", [(0, 1), (1, 0)])
    dk, dv = final(one, low, dk, dv)
    level = level[0, 0].reshape(heads, HEAD)[:, :9].reshape(heads, 3, 3).sum(1).T
    return att[None], dq[None], dk[None], dv[None], level


def solution(mesh):
    rows = P("batch", "seq", None)
    return jax.shard_map(
        body,
        mesh=mesh,
        in_specs=(rows, rows, rows, rows, P()),
        out_specs=(rows, rows, rows, rows, P()),
        check_vma=False,
    )
```

time: 1610 us -> 144 us (0.09)
  the two profiles are of different devices: /device:TPU:0 before, /device:TPU:24 now
where the time goes in v1:
time: 144 us; the launch traced here: 143 us
  waiting for transfers between devices  43.6 us (30%)
  blocking collectives  40.9 us (28%)
  starting transfers between devices  22.9 us (16%)
  Pallas kernels  22.5 us (16%)
  local copies, waits for them, and re-layouts  11.3 us (8%)
    all_to_all x2, blocking collectives, in_group(): return lax.all_to_all(x, 'seq', 0, 0, axis_index_groups=groups)  40.9 us
    ppermute x16, waiting for transfers between devices, swap(): lax.ppermute(x, 'seq', [(i, i ^ mask) for i in range(lax.axis_size('seq'))])  35.1 us
    ppermute x3, starting transfers between devices, cross(): return lax.ppermute(x, 'seq', pairs + [(j, i) for i, j in pairs])  14.5 us
    pallas_call x1, Pallas kernels, attend(): pl.pallas_call(functools.partial(attend_kernel, steps, heads), grid_spec=...  10.6 us
    unnamed x61, local copies, waits for them, and re-layouts  10.5 us
    ppermute x3, waiting for transfers between devices, cross(): return lax.ppermute(x, 'seq', pairs + [(j, i) for i, j in pairs])  8.47 us
    pallas_call x1, Pallas kernels, edge(): pl.pallas_call(functools.partial(edge_kernel, per_half, heads), grid_spec...  7.67 us
    ppermute x1, starting transfers between devices, body(): level = level + lax.ppermute(level, 'batch', [(0, 1), (1, 0)])  4.58 us
  transfers between devices with their start and end apart: 20, of which 11 were waited for; matrix products, arithmetic and copies ran while one was open for 0% of the time, Pallas kernels for 15%

profile of v1, /device:TPU:24, one launch (start us, length us, event | category | flops | bytes accessed | tf_op | source)
XLA Modules:
  0.0 143.0 jit_solution(9040234191131558207)
XLA Ops:
  0.6 0.1 pad_add_fusion.ids_ref
  0.7 1.0 copy-done.1
  1.8 1.0 copy-done.3
  2.8 1.0 copy-done.5
  3.8 1.0 copy-done.6
  4.9 0.8 shard_map.92
  5.7 8.3 %collective-permute-start.7 = (bf16[256,2048]{1,0:T(8,128)(2,1)S(1)}, bf16[256,2048]{1,0:T(8,128)(2,1)S(1)}, u32[]{:S(2)}, u32[]{:S(2)}) collective-permute-start(bf16[256,2048]{1,0:T(8,128)(2,1)S(1)} %get-tuple-element.46), channel_id=1, source_target_pairs={{2,4},{6,8},{10,12},{14,16},{18,20},{22,24},{26,28},{30,32},{34,36... | collective-permute-start | bytes 3145736 | tf_op jit(solution)/shard_map/ppermute | solution.py:33
  14.1 0.5 shard_map.93
  14.6 0.1 collective-permute-start.4
  14.8 11.7 %collective-permute-done.4 = bf16[1,2,2048]{2,1,0:T(2,128)(2,1)S(1)} collective-permute-done((bf16[1,2,2048]{2,1,0:T(2,128)(2,1)S(1)}, bf16[1,2,2048]{2,1,0:T(2,128)(2,1)S(1)}, u32[]{:S(2)}, u32[]{:S(2)}) %collective-permute-start.4) | collective-permute-done | bytes 8224 | tf_op jit(solution)/shard_map/ppermute | solution.py:27
  26.5 0.5 collective-permute-start.5
  27.1 3.3 %collective-permute-done.5 = bf16[2,2,2048]{2,1,0:T(2,128)(2,1)S(1)} collective-permute-done((bf16[2,2,2048]{2,1,0:T(2,128)(2,1)S(1)}, bf16[2,2,2048]{2,1,0:T(2,128)(2,1)S(1)}, u32[]{:S(2)}, u32[]{:S(2)}) %collective-permute-start.5) | collective-permute-done | bytes 16416 | tf_op jit(solution)/shard_map/ppermute | solution.py:27
  30.4 0.1 collective-permute-start.6
  30.5 5.1 %collective-permute-done.6.b_ref = bf16[4,2,2048]{2,1,0:T(2,128)(2,1)S(1)} collective-permute-done((bf16[4,2,2048]{2,1,0:T(2,128)(2,1)S(1)}, bf16[4,2,2048]{2,1,0:T(2,128)(2,1)S(1)}, u32[]{:S(2)}, u32[]{:S(2)}) %collective-permute-start.6) | collective-permute-done | bytes 32800 | tf_op jit(solution)/shard_map/ppermute | solution.py:27
  35.6 0.1 shard_map.94
  35.7 0.0 collective-permute-done.7.x_ref.xk_ref.xv_ref
  35.7 19.8 %all_to_all.10.level_ref = bf16[16,32,1024]{2,1,0:T(8,128)(2,1)} all-to-all(bf16[16,32,1024]{2,1,0:T(8,128)(2,1)S(1)} %shard_map.94), channel_id=1, replica_groups={{0,2,4,6,8,10,12,14,16,18,20,22,24,26,28,30},{32,34,36,38,40,42,44,46,4..., dimensions={0} | all-to-all | bytes 2097152 | tf_op jit(solution)/shard_map/all_to_all | solution.py:39
  55.5 4.2 %collective-permute-start.9 = (bf16[256,2048]{1,0:T(8,128)(2,1)S(1)}, bf16[256,2048]{1,0:T(8,128)(2,1)S(1)}, u32[]{:S(2)}, u32[]{:S(2)}) collective-permute-start(bf16[256,2048]{1,0:T(8,128)(2,1)S(1)} %get-tuple-element.52), channel_id=1, source_target_pairs={{2,4},{6,8},{10,12},{14,16},{18,20},{22,24},{26,28},{30,32},{34,36... | collective-permute-start | bytes 3145736 | tf_op jit(solution)/shard_map/ppermute | solution.py:33
  59.7 0.1 collective-permute-start
  59.8 0.6 shard_map.95
  60.5 0.6 collective-permute-start.8
  61.0 0.1 collective-permute-start.1
  61.1 0.4 collective-permute-start.2
  61.5 0.0 collective-permute-done.sq_ref
  61.6 0.1 collective-permute-start.3
  61.7 1.3 collective-permute-done.1.sk_ref
  62.9 0.4 collective-permute-done.2.sv_ref
  63.3 0.4 collective-permute-done.3.sc_ref
  63.7 0.3 copy-done.18
  64.0 0.4 copy-done.19
  64.4 0.8 copy-done.11
  65.2 10.6 %shard_map.96 = (bf16[128,1024]{1,0:T(8,128)(2,1)}, bf16[128,1024]{1,0:T(8,128)(2,1)}, bf16[128,1024]{1,0:T(8,128)(2,1)}, bf16[128,1024]{1,0:T(8,128)(2,1)}, f32...) custom-call(s32[3]{0:T(128)S(1)} %pad_add_fusion.ids_ref, ...), custom_call_target="tpu_custom_call" | custom-call | bytes 29700000 | tf_op jit(solution)/shard_map/pallas_call | solution.py:352
  75.8 0.6 collective-permute-done.9.q_ref.c_ref
  76.4 21.2 %all_to_all.11 = bf16[16,32,1024]{2,1,0:T(8,128)(2,1)S(1)} all-to-all(bf16[16,32,1024]{2,1,0:T(8,128)(2,1)} %get-tuple-element.66), channel_id=1, replica_groups={{0,2,4,6,8,10,12,14,16,18,20,22,24,26,28,30},{32,34,36,38,40,42,44,46,4..., dimensions={0} | all-to-all | bytes 2097152 | tf_op jit(solution)/shard_map/all_to_all | solution.py:39
  97.6 0.4 shard_map.98
  98.0 0.1 collective-permute-start.16
  98.1 5.6 %collective-permute-done.16 = f32[5,2,2048]{2,1,0:T(2,128)S(1)} collective-permute-done((f32[5,2,2048]{2,1,0:T(2,128)S(1)}, f32[5,2,2048]{2,1,0:T(2,128)S(1)}, u32[]{:S(2)}, u32[]{:S(2)}) %collective-permute-start.16) | collective-permute-done | bytes 81952 | tf_op jit(solution)/shard_map/ppermute | solution.py:27
  103.8 0.0 copy-start.20
  103.8 0.6 copy-done.20
  104.4 0.7 slice-done
  105.2 0.1 collective-permute-start.17
  105.3 0.6 copy-done.28
  105.9 0.0 collective-permute-start.10
  105.9 0.5 collective-permute-start.12
  106.4 0.1 collective-permute-start.13
  106.5 0.4 collective-permute-start.14
  106.9 2.5 %collective-permute-done.17 = f32[3,2,2048]{2,1,0:T(2,128)S(1)} collective-permute-done((f32[3,2,2048]{2,1,0:T(2,128)S(1)}, f32[3,2,2048]{2,1,0:T(2,128)S(1)}, u32[]{:S(2)}, u32[]{:S(2)}) %collective-permute-start.17) | collective-permute-done | bytes 49184 | tf_op jit(solution)/shard_map/ppermute | solution.py:27
  109.5 0.6 collective-permute-start.18
  110.1 0.0 copy-done.23
  110.1 4.8 %collective-permute-done.18 = f32[2,2,2048]{2,1,0:T(2,128)S(1)} collective-permute-done((f32[2,2,2048]{2,1,0:T(2,128)S(1)}, f32[2,2,2048]{2,1,0:T(2,128)S(1)}, u32[]{:S(2)}, u32[]{:S(2)}) %collective-permute-start.18) | collective-permute-done | bytes 32800 | tf_op jit(solution)/shard_map/ppermute | solution.py:27
  115.0 1.9 %collective-permute-start.11 = (f32[2,16,128]{2,1,0:T(8,128)S(1)}, f32[2,16,128]{2,1,0:T(8,128)S(1)}, u32[]{:S(2)}, u32[]{:S(2)}) collective-permute-start(f32[2,16,128]{2,1,0:T(8,128)S(1)} %maximum_select_fusion), channel_id=1, source_target_pairs={{2,4},{6,8},{10,12},{14,16},{18,20},{22,24},{26,28},{30,32},{34,36... | collective-permute-start | bytes 49160 | tf_op jit(solution)/shard_map/ppermute | solution.py:33
  116.9 7.9 %collective-permute-done.11.stat_ref = f32[2,16,128]{2,1,0:T(8,128)S(1)} collective-permute-done((f32[2,16,128]{2,1,0:T(8,128)S(1)}, f32[2,16,128]{2,1,0:T(8,128)S(1)}, u32[]{:S(2)}, u32[]{:S(2)}) %collective-permute-start.11) | collective-permute-done | bytes 16416 | tf_op jit(solution)/shard_map/ppermute | solution.py:33
  124.8 4.6 %collective-permute-start.19 = (f32[1,2,2048]{2,1,0:T(2,128)S(1)}, f32[1,2,2048]{2,1,0:T(2,128)S(1)}, u32[]{:S(2)}, u32[]{:S(2)}) collective-permute-start(f32[1,2,2048]{2,1,0:T(2,128)S(1)} %get-tuple-element.75), channel_id=1, source_target_pairs={{0,1},{1,0},{2,3},{3,2},{4,5},{5,4},{6,7},{7,6},{8,9},{9,8},{10,11... | collective-permute-start | bytes 49160 | tf_op jit(solution)/shard_map/ppermute | solution.py:570
  129.4 0.0 copy-start.12
  129.5 0.6 copy-done.14
  130.1 0.1 copy-done.15
  130.2 0.2 copy-done.12
  130.4 0.2 copy-done.13
  130.5 7.7 %shard_map.97 = (bf16[128,2048]{1,0:T(8,128)(2,1)}, bf16[128,2048]{1,0:T(8,128)(2,1)}, f32[128,2048]{1,0:T(8,128)}, f32[128,2048]{1,0:T(8,128)}) custom-call(s32[3]{0:T(128)S(1)} %pad_add_fusion.ids_ref, f32[3,16]{1,0:T(4,128)S(1)} %copy-done.9, bf16[128,2048]{1,0:T(8,128)(2,1)} %bitcast.19, bf16[128,2048]{1,0:T(8,128)(2,1)} %bitcast.23, ...), custom_call_target="tpu_custom_call" | custom-call | bytes 13200000 | tf_op jit(solution)/shard_map/pallas_call | solution.py:429
  138.2 1.2 copy-done.7
  139.4 1.2 copy-done.8
  140.7 1.7 %shard_map.99 = (bf16[128,2048]{1,0:T(8,128)(2,1)}, bf16[128,2048]{1,0:T(8,128)(2,1)}) custom-call(f32[16,2048]{1,0:T(8,128)S(1)} %get-tuple-element.67.one_ref, f32[1,2,2048]{2,1,0:T(2,128)S(1)} %get-tuple-element.76.far_ref, f32[128,2048]{1,0:T(8,128)S(1)} %copy-done.7, f32[128,2048]{1,0:T(8,128)S(1)} %copy-done.8), custom_call_target="tpu_custom_call" | custom-call | bytes 6600000 | tf_op jit(solution)/shard_map/pallas_call | solution.py:504
  142.4 0.1 copy.11
  142.5 0.6 reduce_sum.9
  (64 shorter events, 0.3 us)
Async XLA Ops:
  0.7 1.0 copy-start.1
  1.8 1.0 copy-start.3
  2.8 1.0 copy-start.5
  3.8 1.0 copy-start.6
  4.9 9.2 %copy-start.2 = (bf16[1,128,2048]{2,1,0:T(8,128)(2,1)S(1)}, bf16[1,128,2048]{2,1,0:T(8,128)(2,1)}, u32[]{:S(2)}) copy-start(bf16[1,128,2048]{2,1,0:T(8,128)(2,1)} %param.6) | copy-start | bytes 1572868
  4.9 9.2 %copy-start.4 = (bf16[1,128,2048]{2,1,0:T(8,128)(2,1)S(1)}, bf16[1,128,2048]{2,1,0:T(8,128)(2,1)}, u32[]{:S(2)}) copy-start(bf16[1,128,2048]{2,1,0:T(8,128)(2,1)} %param.7) | copy-start | bytes 1572868
  5.7 29.9 %collective-permute-start.7 = (bf16[256,2048]{1,0:T(8,128)(2,1)S(1)}, bf16[256,2048]{1,0:T(8,128)(2,1)S(1)}, u32[]{:S(2)}, u32[]{:S(2)}) collective-permute-start(bf16[256,2048]{1,0:T(8,128)(2,1)S(1)} %get-tuple-element.46), channel_id=1, source_target_pairs={{2,4},{6,8},{10,12},{14,16},{18,20},{22,24},{26,28},{30,32},{34,36... | collective-permute-start | bytes 3145736 | tf_op jit(solution)/shard_map/ppermute | solution.py:33
  14.6 11.8 %collective-permute-start.4 = (bf16[1,2,2048]{2,1,0:T(2,128)(2,1)S(1)}, bf16[1,2,2048]{2,1,0:T(2,128)(2,1)S(1)}, u32[]{:S(2)}, u32[]{:S(2)}) collective-permute-start(bf16[1,2,2048]{2,1,0:T(2,128)(2,1)S(1)} %get-tuple-element.45), channel_id=1, source_target_pairs={{0,32},{2,34},{4,36},{6,38},{8,40},{10,42},{12,44},{14,46},{16,48}... | collective-permute-start | bytes 24584 | tf_op jit(solution)/shard_map/ppermute | solution.py:27
  26.5 3.8 %collective-permute-start.5 = (bf16[2,2,2048]{2,1,0:T(2,128)(2,1)S(1)}, bf16[2,2,2048]{2,1,0:T(2,128)(2,1)S(1)}, u32[]{:S(2)}, u32[]{:S(2)}) collective-permute-start(bf16[2,2,2048]{2,1,0:T(2,128)(2,1)S(1)} %pad_maximum_fusion.2), channel_id=1, source_target_pairs={{0,64},{2,66},{4,68},{6,70},{8,72},{10,74},{12,76},{14,78},{16,80}... | collective-permute-start | bytes 49160 | tf_op jit(solution)/shard_map/ppermute | solution.py:27
  30.4 5.2 %collective-permute-start.6 = (bf16[4,2,2048]{2,1,0:T(2,128)(2,1)S(1)}, bf16[4,2,2048]{2,1,0:T(2,128)(2,1)S(1)}, u32[]{:S(2)}, u32[]{:S(2)}) collective-permute-start(bf16[4,2,2048]{2,1,0:T(2,128)(2,1)S(1)} %constant_dynamic-update-slice_fusion.a_ref), channel_id=1, source_target_pairs={{0,192},{2,194},{4,196},{6,198},{8,200},{10,202},{12,204},{14,206}... | collective-permute-start | bytes 98312 | tf_op jit(solution)/shard_map/ppermute | solution.py:27
  35.7 24.1 %copy-start = (bf16[256,2048]{1,0:T(8,128)(2,1)}, bf16[256,2048]{1,0:T(8,128)(2,1)S(1)}, u32[]{:S(2)}) copy-start(bf16[256,2048]{1,0:T(8,128)(2,1)S(1)} %collective-permute-done.7.x_ref.xk_ref.xv_ref) | copy-start | bytes 3145732
  55.5 20.9 %collective-permute-start.9 = (bf16[256,2048]{1,0:T(8,128)(2,1)S(1)}, bf16[256,2048]{1,0:T(8,128)(2,1)S(1)}, u32[]{:S(2)}, u32[]{:S(2)}) collective-permute-start(bf16[256,2048]{1,0:T(8,128)(2,1)S(1)} %get-tuple-element.52), channel_id=1, source_target_pairs={{2,4},{6,8},{10,12},{14,16},{18,20},{22,24},{26,28},{30,32},{34,36... | collective-permute-start | bytes 3145736 | tf_op jit(solution)/shard_map/ppermute | solution.py:33
  59.7 1.8 %collective-permute-start = (bf16[128,1024]{1,0:T(8,128)(2,1)S(1)}, bf16[128,1024]{1,0:T(8,128)(2,1)S(1)}, u32[]{:S(2)}, u32[]{:S(2)}) collective-permute-start(bf16[128,1024]{1,0:T(8,128)(2,1)S(1)} %get-tuple-element.40), channel_id=1, source_target_pairs={{0,2},{2,0},{4,6},{6,4},{8,10},{10,8},{12,14},{14,12},{16,18},{18,... | collective-permute-start | bytes 786440 | tf_op jit(solution)/shard_map/ppermute | solution.py:27
  60.5 3.2 %collective-permute-start.8 = (bf16[256,1024]{1,0:T(8,128)(2,1)S(1)}, bf16[256,1024]{1,0:T(8,128)(2,1)S(1)}, u32[]{:S(2)}, u32[]{:S(2)}) collective-permute-start(bf16[256,1024]{1,0:T(8,128)(2,1)S(1)} %shard_map.95), channel_id=1, source_target_pairs={{0,2},{2,0},{4,6},{6,4},{8,10},{10,8},{12,14},{14,12},{16,18},{18,... | collective-permute-start | bytes 1572872 | tf_op jit(solution)/shard_map/ppermute | solution.py:27
  61.0 4.1 %copy-start.9 = (f32[3,16]{1,0:T(4,128)S(1)}, f32[3,16]{1,0:T(4,128)}, u32[]{:S(2)}) copy-start(f32[3,16]{1,0:T(4,128)} %bias_ref.3) | copy-start | bytes 580
  61.0 1.9 %collective-permute-start.1 = (bf16[128,1024]{1,0:T(8,128)(2,1)S(1)}, bf16[128,1024]{1,0:T(8,128)(2,1)S(1)}, u32[]{:S(2)}, u32[]{:S(2)}) collective-permute-start(bf16[128,1024]{1,0:T(8,128)(2,1)S(1)} %get-tuple-element.41), channel_id=1, source_target_pairs={{0,2},{2,0},{4,6},{6,4},{8,10},{10,8},{12,14},{14,12},{16,18},{18,... | collective-permute-start | bytes 786440 | tf_op jit(solution)/shard_map/ppermute | solution.py:27
  61.1 2.2 %collective-permute-start.2 = (bf16[128,1024]{1,0:T(8,128)(2,1)S(1)}, bf16[128,1024]{1,0:T(8,128)(2,1)S(1)}, u32[]{:S(2)}, u32[]{:S(2)}) collective-permute-start(bf16[128,1024]{1,0:T(8,128)(2,1)S(1)} %get-tuple-element.42), channel_id=1, source_target_pairs={{0,2},{2,0},{4,6},{6,4},{8,10},{10,8},{12,14},{14,12},{16,18},{18,... | collective-permute-start | bytes 786440 | tf_op jit(solution)/shard_map/ppermute | solution.py:27
  61.5 2.2 %copy-start.16 = (bf16[128,1024]{1,0:T(8,128)(2,1)}, bf16[128,1024]{1,0:T(8,128)(2,1)S(1)}, u32[]{:S(2)}) copy-start(bf16[128,1024]{1,0:T(8,128)(2,1)S(1)} %collective-permute-done.sq_ref) | copy-start | bytes 786436
  61.6 2.1 %collective-permute-start.3 = (bf16[128,1024]{1,0:T(8,128)(2,1)S(1)}, bf16[128,1024]{1,0:T(8,128)(2,1)S(1)}, u32[]{:S(2)}, u32[]{:S(2)}) collective-permute-start(bf16[128,1024]{1,0:T(8,128)(2,1)S(1)} %get-tuple-element.43), channel_id=1, source_target_pairs={{0,2},{2,0},{4,6},{6,4},{8,10},{10,8},{12,14},{14,12},{16,18},{18,... | collective-permute-start | bytes 786440 | tf_op jit(solution)/shard_map/ppermute | solution.py:27
  62.9 0.8 copy-start.17
  63.3 0.7 copy-start.18
  63.7 0.7 copy-start.19
  64.4 0.8 copy-start.11
  76.4 21.2 %copy-start.10 = (bf16[256,2048]{1,0:T(8,128)(2,1)}, bf16[256,2048]{1,0:T(8,128)(2,1)S(1)}, u32[]{:S(2)}) copy-start(bf16[256,2048]{1,0:T(8,128)(2,1)S(1)} %collective-permute-done.9.q_ref.c_ref) | copy-start | bytes 3145732
  76.4 29.5 %copy-start.27 = (bf16[128,1024]{1,0:T(8,128)(2,1)S(1)}, bf16[128,1024]{1,0:T(8,128)(2,1)}, u32[]{:S(2)}) copy-start(bf16[128,1024]{1,0:T(8,128)(2,1)} %get-tuple-element.57) | copy-start | bytes 786436
  97.6 8.9 %copy-start.25 = (f32[128,1024]{1,0:T(8,128)S(1)}, f32[128,1024]{1,0:T(8,128)}, u32[]{:S(2)}) copy-start(f32[128,1024]{1,0:T(8,128)} %get-tuple-element.61) | copy-start | bytes 1572868
  97.6 11.8 %copy-start.24 = (f32[128,1024]{1,0:T(8,128)S(1)}, f32[128,1024]{1,0:T(8,128)}, u32[]{:S(2)}) copy-start(f32[128,1024]{1,0:T(8,128)} %get-tuple-element.63) | copy-start | bytes 1572868
  98.0 8.4 %copy-start.26 = (bf16[128,1024]{1,0:T(8,128)(2,1)S(1)}, bf16[128,1024]{1,0:T(8,128)(2,1)}, u32[]{:S(2)}) copy-start(bf16[128,1024]{1,0:T(8,128)(2,1)} %get-tuple-element.59) | copy-start | bytes 786436
  98.0 5.7 %collective-permute-start.16 = (f32[5,2,2048]{2,1,0:T(2,128)S(1)}, f32[5,2,2048]{2,1,0:T(2,128)S(1)}, u32[]{:S(2)}, u32[]{:S(2)}) collective-permute-start(f32[5,2,2048]{2,1,0:T(2,128)S(1)} %get-tuple-element.69), channel_id=1, source_target_pairs={{0,192},{2,194},{4,196},{6,198},{8,200},{10,202},{12,204},{14,206}... | collective-permute-start | bytes 245768 | tf_op jit(solution)/shard_map/ppermute | solution.py:27
  103.8 0.6 copy-start.20
  104.4 0.8 slice-start
  105.2 0.7 copy-start.28
  105.2 4.2 %copy-start.21 = (f32[4,2,2048]{2,1,0:T(2,128)S(1)}, f32[4,2,2048]{2,1,0:T(2,128)}, u32[]{:S(2)}) copy-start(f32[4,2,2048]{2,1,0:T(2,128)} %copy-done.20) | copy-start | bytes 196612
  105.2 4.2 %collective-permute-start.17 = (f32[3,2,2048]{2,1,0:T(2,128)S(1)}, f32[3,2,2048]{2,1,0:T(2,128)S(1)}, u32[]{:S(2)}, u32[]{:S(2)}) collective-permute-start(f32[3,2,2048]{2,1,0:T(2,128)S(1)} %pad_maximum_fusion), channel_id=1, source_target_pairs={{0,64},{2,66},{4,68},{6,70},{8,72},{10,74},{12,76},{14,78},{16,80}... | collective-permute-start | bytes 147464 | tf_op jit(solution)/shard_map/ppermute | solution.py:27
  105.9 3.6 %collective-permute-start.10 = (f32[16,128]{1,0:T(8,128)S(1)}, f32[16,128]{1,0:T(8,128)S(1)}, u32[]{:S(2)}, u32[]{:S(2)}) collective-permute-start(f32[16,128]{1,0:T(8,128)S(1)} %copy-done.28), channel_id=1, source_target_pairs={{0,2},{2,0},{4,6},{6,4},{8,10},{10,8},{12,14},{14,12},{16,18},{18,... | collective-permute-start | bytes 24584 | tf_op jit(solution)/shard_map/ppermute | solution.py:27
  105.9 23.5 %collective-permute-start.12 = (bf16[128,1024]{1,0:T(8,128)(2,1)S(1)}, bf16[128,1024]{1,0:T(8,128)(2,1)S(1)}, u32[]{:S(2)}, u32[]{:S(2)}) collective-permute-start(bf16[128,1024]{1,0:T(8,128)(2,1)S(1)} %copy-done.27), channel_id=1, source_target_pairs={{0,2},{2,0},{4,6},{6,4},{8,10},{10,8},{12,14},{14,12},{16,18},{18,... | collective-permute-start | bytes 786440 | tf_op jit(solution)/shard_map/ppermute | solution.py:27
  106.4 23.0 %collective-permute-start.13 = (bf16[128,1024]{1,0:T(8,128)(2,1)S(1)}, bf16[128,1024]{1,0:T(8,128)(2,1)S(1)}, u32[]{:S(2)}, u32[]{:S(2)}) collective-permute-start(bf16[128,1024]{1,0:T(8,128)(2,1)S(1)} %copy-done.26), channel_id=1, source_target_pairs={{0,2},{2,0},{4,6},{6,4},{8,10},{10,8},{12,14},{14,12},{16,18},{18,... | collective-permute-start | bytes 786440 | tf_op jit(solution)/shard_map/ppermute | solution.py:27
  106.5 22.9 %collective-permute-start.14 = (f32[128,1024]{1,0:T(8,128)S(1)}, f32[128,1024]{1,0:T(8,128)S(1)}, u32[]{:S(2)}, u32[]{:S(2)}) collective-permute-start(f32[128,1024]{1,0:T(8,128)S(1)} %copy-done.25), channel_id=1, source_target_pairs={{0,2},{2,0},{4,6},{6,4},{8,10},{10,8},{12,14},{14,12},{16,18},{18,... | collective-permute-start | bytes 1572872 | tf_op jit(solution)/shard_map/ppermute | solution.py:27
  109.4 20.1 %collective-permute-start.15 = (f32[128,1024]{1,0:T(8,128)S(1)}, f32[128,1024]{1,0:T(8,128)S(1)}, u32[]{:S(2)}, u32[]{:S(2)}) collective-permute-start(f32[128,1024]{1,0:T(8,128)S(1)} %copy-done.24), channel_id=1, source_target_pairs={{0,2},{2,0},{4,6},{6,4},{8,10},{10,8},{12,14},{14,12},{16,18},{18,... | collective-permute-start | bytes 1572872 | tf_op jit(solution)/shard_map/ppermute | solution.py:27
  109.4 0.7 copy-start.23
  109.5 5.5 %collective-permute-start.18 = (f32[2,2,2048]{2,1,0:T(2,128)S(1)}, f32[2,2,2048]{2,1,0:T(2,128)S(1)}, u32[]{:S(2)}, u32[]{:S(2)}) collective-permute-start(f32[2,2,2048]{2,1,0:T(2,128)S(1)} %pad_maximum_fusion.1), channel_id=1, source_target_pairs={{0,32},{2,34},{4,36},{6,38},{8,40},{10,42},{12,44},{14,46},{16,48}... | collective-permute-start | bytes 98312 | tf_op jit(solution)/shard_map/ppermute | solution.py:27
  115.0 9.9 %collective-permute-start.11 = (f32[2,16,128]{2,1,0:T(8,128)S(1)}, f32[2,16,128]{2,1,0:T(8,128)S(1)}, u32[]{:S(2)}, u32[]{:S(2)}) collective-permute-start(f32[2,16,128]{2,1,0:T(8,128)S(1)} %maximum_select_fusion), channel_id=1, source_target_pairs={{2,4},{6,8},{10,12},{14,16},{18,20},{22,24},{26,28},{30,32},{34,36... | collective-permute-start | bytes 49160 | tf_op jit(solution)/shard_map/ppermute | solution.py:33
  124.8 4.6 %copy-start.22 = (f32[2,16,128]{2,1,0:T(8,128)}, f32[2,16,128]{2,1,0:T(8,128)S(1)}, u32[]{:S(2)}) copy-start(f32[2,16,128]{2,1,0:T(8,128)S(1)} %collective-permute-done.11.stat_ref) | copy-start | bytes 49156
  124.8 17.5 %collective-permute-start.19 = (f32[1,2,2048]{2,1,0:T(2,128)S(1)}, f32[1,2,2048]{2,1,0:T(2,128)S(1)}, u32[]{:S(2)}, u32[]{:S(2)}) collective-permute-start(f32[1,2,2048]{2,1,0:T(2,128)S(1)} %get-tuple-element.75), channel_id=1, source_target_pairs={{0,1},{1,0},{2,3},{3,2},{4,5},{5,4},{6,7},{7,6},{8,9},{9,8},{10,11... | collective-permute-start | bytes 49160 | tf_op jit(solution)/shard_map/ppermute | solution.py:570
  129.4 0.7 copy-start.14
  129.4 0.8 copy-start.15
  129.4 0.9 copy-start.12
  129.4 1.1 copy-start.13
  138.2 1.2 copy-start.7
  139.4 1.2 copy-start.8

commit v2 on v1

--- a/solution.py
+++ b/solution.py
@@ -14,8 +14,9 @@
 ROWS = 128
 HEAD = 128
 NEGATIVE = -1e30
-LOG1 = math.log(POOL1)
-LOG2 = math.log(POOL2)
+LOG2E = math.log2(math.e)
+LOG1 = math.log2(POOL1)
+LOG2 = math.log2(POOL2)
 
 SIB, Z1, YA, YB = 1, 16, 32, 96
 
@@ -123,10 +124,11 @@
     start = pl.multiple_of((1 - ids_ref[1]) * half, half)
     copies = []
     for n, (ref, out) in enumerate(zip(arrays, halves)):
+        part = ref.at[:, pl.ds(start, half)]
+        copies.append(pltpu.make_async_copy(part, out, sems.at[n]))
+    for n, ref in enumerate(arrays):
         to = wholes[n // 2].at[(n % 2) * ROWS : (n % 2 + 1) * ROWS]
-        copies.append(pltpu.make_async_copy(ref, to, sems.at[2 * n]))
-        part = ref.at[:, pl.ds(start, half)]
-        copies.append(pltpu.make_async_copy(part, out, sems.at[2 * n + 1]))
+        copies.append(pltpu.make_async_copy(ref, to, sems.at[4 + n]))
     for copy in copies:
         copy.start()
     for copy in copies:
@@ -146,29 +148,28 @@
         scratch_shapes=[pltpu.SemaphoreType.DMA((8,))],
         compiler_params=params(),
         cost_estimate=cost(1),
-    )(ids, *arrays)
+    )(ids, *in_hbm(*arrays))
 
 
 def other_kernel(ids_ref, x_ref, out_ref, sem):
     half = out_ref.shape[-1]
     start = pl.multiple_of((1 - ids_ref[1]) * half, half)
-    part = x_ref.at[0 : out_ref.shape[0], pl.ds(start, half)]
-    copy = pltpu.make_async_copy(part, out_ref, sem)
+    copy = pltpu.make_async_copy(x_ref.at[:, pl.ds(start, half)], out_ref, sem)
     copy.start()
     copy.wait()
 
 
-def other_half(ids, x, rows):
+def other_half(ids, x):
     smem = pl.BlockSpec(memory_space=pltpu.SMEM)
     hbm = pl.BlockSpec(memory_space=pltpu.HBM)
     return pl.pallas_call(
         other_kernel,
         in_specs=[smem, hbm],
         out_specs=hbm,
-        out_shape=jax.ShapeDtypeStruct((rows, x.shape[1] // 2), BF),
+        out_shape=jax.ShapeDtypeStruct((x.shape[0], x.shape[1] // 2), BF),
         scratch_shapes=[pltpu.SemaphoreType.DMA],
         compiler_params=params(),
-        cost_estimate=cost(1),
+        cost_estimate=cost(12),
     )(ids, x)
 
 
@@ -231,6 +232,7 @@
     me, core = ids_ref[0], ids_ref[1]
     last = ids_ref[2] - 1
     scale = HEAD**-0.5
+    unit = scale * LOG2E
 
     @pl.when(step == 0)
     def _():
@@ -252,7 +254,7 @@
         cols = slice(j * HEAD, (j + 1) * HEAD)
         head = step * heads + j
         whole_head = core * (steps * heads) + head
-        bias = [bias_ref[n, whole_head] for n in range(3)]
+        bias = [bias_ref[n, whole_head] * LOG2E for n in range(3)]
         q, sq, c, sc = q_ref[:, cols], sq_ref[:, cols], c_ref[:, cols], sc_ref[:, cols]
         k_near = jnp.concatenate([k_ref[:, cols], sk_ref[:, cols]], axis=0)
         v_near = jnp.concatenate([v_ref[:, cols], sv_ref[:, cols]], axis=0)
@@ -266,19 +268,18 @@
         q_both = jnp.concatenate([q, sq], axis=0)
         c_both = jnp.concatenate([c, sc], axis=0)
 
-        s_near = nt(k_near, q_both) * scale + bias[0]
-        s_edge = jnp.concatenate([nt(xk, q), nt(sxk, sq)], axis=1) * scale + (
-            edge_ref[0:1] + bias[0]
-        )
-        s_far = nt(k_far, q_both) * scale
-        s_one = s_far[0:ROWS] + (mask_ref[0:ROWS] + bias[1])
-        s_two = s_far[ROWS:] + (mask_ref[ROWS:] + bias[2])
-        scores = [s_near, s_edge, s_one, s_two]
-        top = functools.reduce(
-            jnp.maximum, [jnp.max(s, axis=0, keepdims=True) for s in scores]
-        )
-        powers = [jnp.exp(s - top) for s in scores]
-        total = sum(jnp.sum(p, axis=0, keepdims=True) for p in powers)
+        near = nt(k_near, q_both)
+        edge = jnp.concatenate([nt(xk, q), nt(sxk, sq)], axis=1)
+        far = nt(k_far, q_both) * unit + mask_ref[...]
+        parts = [near, edge, far[0:ROWS], far[ROWS:]]
+        shifts = [bias[0], bias[0] + edge_ref[0:1], bias[1], bias[2]]
+        tops = [jnp.max(x, axis=0, keepdims=True) for x in parts]
+        tops = [t * unit for t in tops[:2]] + tops[2:]
+        top = functools.reduce(jnp.maximum, [t + s for t, s in zip(tops, shifts)])
+        parts = [x * unit for x in parts[:2]] + parts[2:]
+        powers = [jnp.exp2(x + (s - top)) for x, s in zip(parts, shifts)]
+        masses = [jnp.sum(p, axis=0, keepdims=True) for p in powers]
+        total = sum(masses)
         share = 1.0 / total
         weights = [p * share for p in powers]
 
@@ -289,9 +290,10 @@
             g_far[0:ROWS],
             g_far[ROWS:],
         ]
-        delta = sum(
+        deltas = [
             jnp.sum(w * g, axis=0, keepdims=True) for w, g in zip(weights, grads)
-        )
+        ]
+        delta = sum(deltas)
         score_grads = [w * (g - delta) for w, g in zip(weights, grads)]
         w_near, w_edge, w_one, w_two = [w.astype(BF) for w in weights]
         d_near, d_edge, d_one, d_two = [d.astype(BF) for d in score_grads]
@@ -314,14 +316,14 @@
         dk = nn(d_far, q_both) * scale
         dv = nn(w_far, c_both)
         glevel_ref[:, 0:16, cols] = join_rows(dk[0:ROWS], dv[0:ROWS])
-        sums = [jnp.sum(d, axis=0, keepdims=True) for d in score_grads]
-        level = pieces([sums[0] + sums[1], sums[2], sums[3]])
+        loads = [d - m * (share * delta) for d, m in zip(deltas, masses)]
+        level = pieces([loads[0] + loads[1], loads[2], loads[3]])
         first = lax.broadcasted_iota(jnp.int32, (ROWS, HEAD), 0) % 8 == 0
         glevel_ref[:, 16:32, cols] = join_rows(
             jnp.where(first, level, dk[ROWS:]), dv[ROWS:]
         )
 
-        log_total = top + jnp.log(total)
+        log_total = top + jnp.log(total) * LOG2E
         row = pl.ds(head, 1)
         low = pl.ds(head + 8, 1)
         stat_ref[row] = log_total[:, 0:ROWS]
@@ -373,7 +375,7 @@
         ),
         compiler_params=params(),
         cost_estimate=cost(9),
-    )(ids, bias, *in_hbm(*own, *sib, x, x, sx, sx, level))
+    )(ids, bias, *in_hbm(*own, *sib, x, x, sx, sx), level)
 
 
 def edge_kernel(
@@ -406,12 +408,13 @@
     out_dq_ref[...] = jnp.where(mine, dq_ref[...], sdq_ref[...])
     for j in range(heads):
         cols = slice(j * HEAD, (j + 1) * HEAD)
-        bias = bias_ref[0, step * heads + j]
+        bias = bias_ref[0, step * heads + j] * LOG2E
         row = lax.rem(step, per_half) * heads + j
         log_total = stat_ref[0, pl.ds(row, 1)]
         delta = stat_ref[0, pl.ds(row + 8, 1)]
         q, c = q_ref[:, cols], c_ref[:, cols]
-        weights = jnp.exp(nt(k_ref[:, cols], q) * scale + (bias - log_total))
+        score = nt(k_ref[:, cols], q) * (scale * LOG2E)
+        weights = jnp.exp2(score + (bias - log_total))
         score_grad = weights * (nt(v_ref[:, cols], c) - delta)
         dk = jnp.where(mine, dk_ref[:, cols], sdk_ref[:, cols])
         dv = jnp.where(mine, dv_ref[:, cols], sdv_ref[:, cols])
@@ -421,7 +424,7 @@
 
 def edge(ids, bias, k, v, x, stat, parts):
     rows, width = k.shape
-    heads = 4
+    heads = 8
     block = heads * HEAD
     per_half = width // 2 // block
     whole = pl.BlockSpec((rows, block), lambda i, ids: (0, i))
@@ -442,11 +445,10 @@
             + [part] * 8,
             out_specs=[whole] * 4,
         ),
-        out_shape=out_hbm(
-            [jax.ShapeDtypeStruct((rows, width), t) for t in (BF, BF, F32, F32)]
-        ),
-        compiler_params=params(),
-        cost_estimate=cost(4),
+        out_shape=out_hbm([jax.ShapeDtypeStruct((rows, width), BF)] * 2)
+        + [jax.ShapeDtypeStruct((rows, width), F32)] * 2,
+        compiler_params=params(),
+        cost_estimate=cost(14),
     )(ids, bias, *in_hbm(k, v, x, x, stat, *parts))
 
 
@@ -488,16 +490,38 @@
     )(x)
 
 
-def final_kernel(one_ref, far_ref, dk_ref, dv_ref, out_dk_ref, out_dv_ref):
+def step_kernel(low_ref, got_ref, level_ref, out_low_ref, out_high_ref, out_level_ref):
+    count = low_ref.shape[0]
+    half = count // 2
+    out_low_ref[...] = low_ref[0:half] + got_ref[0:half]
+    out_high_ref[0:half] = low_ref[half:count] + got_ref[half:count]
+    level = level_ref[...] + got_ref[count:]
+    out_level_ref[...] = level
+    out_high_ref[half:] = level
+
+
+def step(low, got, level):
+    half, width = low.shape[0] // 2, low.shape[2]
+    counts = (half, half + 1, 1)
+    return pl.pallas_call(
+        step_kernel,
+        out_shape=[jax.ShapeDtypeStruct((n, 2, width), F32) for n in counts],
+        compiler_params=params(),
+        cost_estimate=cost(1),
+    )(low, got, level)
+
+
+def final_kernel(one_ref, far_ref, got_ref, dk_ref, dv_ref, out_dk_ref, out_dv_ref):
     total = one_ref[...] / POOL1
     for n, (ref, out) in enumerate(((dk_ref, out_dk_ref), (dv_ref, out_dv_ref))):
-        rows = total[8 * n : 8 * n + 8] + far_ref[0, n : n + 1, :] / POOL2
+        far = far_ref[0, n : n + 1, :] + got_ref[0, n : n + 1, :]
+        rows = total[8 * n : 8 * n + 8] + far / POOL2
         for r in range(8):
             at = slice(r * POOL1, (r + 1) * POOL1)
             out[at] = (ref[at] + rows[r : r + 1]).astype(BF)
 
 
-def final(one, far, dk, dv):
+def final(one, far, got, dk, dv):
     rows, width = dk.shape
     block = 512
     whole = pl.BlockSpec((rows, block), lambda i: (0, i))
@@ -507,6 +531,7 @@
         in_specs=[
             pl.BlockSpec((16, block), lambda i: (0, i)),
             pl.BlockSpec((1, 2, block), lambda i: (0, 0, i)),
+            pl.BlockSpec((2, 2, block), lambda i: (0, 0, i)),
             whole,
             whole,
         ],
@@ -514,7 +539,7 @@
         out_shape=[jax.ShapeDtypeStruct((rows, width), BF)] * 2,
         compiler_params=params(),
         cost_estimate=cost(2),
-    )(one, far, dk, dv)
+    )(one, far, got, dk, dv)
 
 
 def body(queries, key_rows, values, cotangent, level_bias):
@@ -525,18 +550,18 @@
     core = me % 2
     ids = jnp.stack([me, core, size]).astype(jnp.int32)
 
+    kv, qc, *sends = prepare(ids, k, v, q, c)
+    x = cross(kv)
     one, far = pool(k, v)
     far = jnp.concatenate([far, swap(far, Z1)], axis=0)
     far = jnp.concatenate([far, swap(far, YA)], axis=0)
     rows = level_rows(one, far, swap(far, YB))
 
-    kv, qc, *sends = prepare(ids, k, v, q, c)
     sk, sv, sq, sc = [swap(s, SIB) for s in sends]
-    x = cross(kv)
-    rows, x = lax.optimization_barrier((rows, x))
+    rows, x, sk, sv, sq, sc = lax.optimization_barrier((rows, x, sk, sv, sq, sc))
     rows = in_group(rows)
-    sx = swap(other_half(ids, x, 2 * ROWS), SIB)
-    late, rows = lax.optimization_barrier((qc, rows))
+    sx = swap(other_half(ids, x), SIB)
+    late, rows, sx = lax.optimization_barrier((qc, rows, sx))
     x_qc = cross(late)
 
     att, satt, dq, sdq, dk, dv, sdk, sdv, grads, stat, sstat = attend(
@@ -544,18 +569,12 @@
     )
 
     grads, x_qc = lax.optimization_barrier((grads, x_qc))
-    one, low, high, level = sums(in_group(grads))
-    for mask in (YB, YA, Z1):
-        got = swap(high, mask)
-        low = low + got[:-1]
-        level = level + got[-1:]
-        half = low.shape[0] // 2
-        high = jnp.concatenate([low[half:], level], axis=0)
-        low = low[:half] if half else low
+    grads = in_group(grads)
 
     rstat = swap(sstat, SIB)
     stats = jnp.where(core == 0, jnp.stack([stat, rstat]), jnp.stack([rstat, stat]))
     x_stats = cross(stats)
+    grads, x_stats = lax.optimization_barrier((grads, x_stats))
     ratt, rdq, rdk, rdv = [swap(s, SIB) for s in (satt, sdq, sdk, sdv)]
     att, dq, dk, dv = edge(
         ids,
@@ -567,8 +586,14 @@
         (att, ratt, dq, rdq, dk, rdk, dv, rdv),
     )
 
+    one, low, high, level = sums(grads)
+    low, high, level = step(low, swap(high, YB), level)
+    low, high, level = step(low, swap(high, YA), level)
+    high, dk, dv = lax.optimization_barrier((high, dk, dv))
+    got = swap(high, Z1)
+    dk, dv = final(one, low, got, dk, dv)
+    level = level + got[1:]
     level = level + lax.ppermute(level, "batch", [(0, 1), (1, 0)])
-    dk, dv = final(one, low, dk, dv)
     level = level[0, 0].reshape(heads, HEAD)[:, :9].reshape(heads, 3, 3).sum(1).T
     return att[None], dq[None], dk[None], dv[None], level
 

time: 144 us -> 123 us (0.85)
  blocking collectives: 40.9 us -> 0 us
  starting transfers between devices: 22.9 us -> 38.8 us
  waiting for transfers between devices: 43.6 us -> 53.8 us
  local copies, waits for them, and re-layouts: 11.3 us -> 4.53 us
  Pallas kernels: 22.5 us -> 24.2 us
    all_to_all x2 -> x0, blocking collectives: 40.9 us -> none  [in_group(): return lax.all_to_all(x, 'seq', 0, 0, axis_index_groups=groups)]
    all_to_all x0 -> x2, waiting for transfers between devices: none -> 13.8 us  [in_group(): return lax.all_to_all(x, 'seq', 0, 0, axis_index_groups=groups)]
    ppermute x16, waiting for transfers between devices: 35.1 us -> 22 us  [swap(): lax.ppermute(x, 'seq', [(i, i ^ mask) for i in range(lax.axis_size('seq'))])]
    ppermute x3, waiting for transfers between devices: 8.47 us -> 17.6 us  [cross(): return lax.ppermute(x, 'seq', pairs + [(j, i) for i, j in pairs])]
    all_to_all x0 -> x2, starting transfers between devices: none -> 7.45 us  [in_group(): return lax.all_to_all(x, 'seq', 0, 0, axis_index_groups=groups)]
    unnamed x61 -> x39, local copies, waits for them, and re-layouts: 10.5 us -> 4.5 us
    ppermute x16, starting transfers between devices: 3.85 us -> 7.98 us  [swap(): lax.ppermute(x, 'seq', [(i, i ^ mask) for i in range(lax.axis_size('seq'))])]
    ppermute x3, starting transfers between devices: 14.5 us -> 17.7 us  [cross(): return lax.ppermute(x, 'seq', pairs + [(j, i) for i, j in pairs])]
  transfers between devices with their start and end apart: 20 -> 22, of which waited for: 11 -> 12; matrix products, arithmetic and copies ran while one was open for 0% -> 0% of each run, Pallas kernels for 15% -> 19%
where the time goes in v2:
time: 123 us
  waiting for transfers between devices  53.8 us (44%)
  starting transfers between devices  38.8 us (32%)
  Pallas kernels  24.2 us (20%)
  local copies, waits for them, and re-layouts  4.53 us (4%)
    ppermute x16, waiting for transfers between devices, swap(): lax.ppermute(x, 'seq', [(i, i ^ mask) for i in range(lax.axis_size('seq'))])  22 us
    ppermute x3, starting transfers between devices, cross(): return lax.ppermute(x, 'seq', pairs + [(j, i) for i, j in pairs])  17.7 us
    ppermute x3, waiting for transfers between devices, cross(): return lax.ppermute(x, 'seq', pairs + [(j, i) for i, j in pairs])  17.6 us
    all_to_all x2, waiting for transfers between devices, in_group(): return lax.all_to_all(x, 'seq', 0, 0, axis_index_groups=groups)  13.8 us
    pallas_call x1, Pallas kernels, attend(): pl.pallas_call(functools.partial(attend_kernel, steps, heads), grid_spec=...  10.6 us
    ppermute x16, starting transfers between devices, swap(): lax.ppermute(x, 'seq', [(i, i ^ mask) for i in range(lax.axis_size('seq'))])  7.98 us
    all_to_all x2, starting transfers between devices, in_group(): return lax.all_to_all(x, 'seq', 0, 0, axis_index_groups=groups)  7.45 us
    pallas_call x1, Pallas kernels, edge(): pl.pallas_call(functools.partial(edge_kernel, per_half, heads), grid_spec...  6.75 us
  transfers between devices with their start and end apart: 22, of which 12 were waited for; matrix products, arithmetic and copies ran while one was open for 0% of the time, Pallas kernels for 19%

profile of v2, /device:TPU:24, one launch (start us, length us, event | category | flops | bytes accessed | tf_op | source)
XLA Modules:
  0.0 122.9 jit_solution(10344840825377793354)
XLA Ops:
  0.6 0.0 copy-start.1
  0.6 1.0 copy-done.1
  1.7 1.0 copy-done.2
  2.7 0.5 shard_map.92
  3.2 3.4 %collective-permute-start = (bf16[1,2,2048]{2,1,0:T(2,128)(2,1)S(1)}, bf16[1,2,2048]{2,1,0:T(2,128)(2,1)S(1)}, u32[]{:S(2)}, u32[]{:S(2)}) collective-permute-start(bf16[1,2,2048]{2,1,0:T(2,128)(2,1)S(1)} %get-tuple-element.57), channel_id=1, source_target_pairs={{0,32},{2,34},{4,36},{6,38},{8,40},{10,42},{12,44},{14,46},{16,48}... | collective-permute-start | bytes 24584 | tf_op jit(solution)/shard_map/ppermute | solution.py:28
  6.6 0.1 pad_add_fusion.ids_ref
  6.7 2.4 %shard_map.94 = (bf16[256,2048]{1,0:T(8,128)(2,1)S(1)}, bf16[256,2048]{1,0:T(8,128)(2,1)S(1)}, bf16[128,1024]{1,0:T(8,128)(2,1)S(1)}, bf16[128,1024]{1,0:T(8,128...) custom-call(s32[3]{0:T(128)S(1)} %pad_add_fusion.ids_ref, bf16[128,2048]{1,0:T(8,128)(2,1)} %bitcast.18, ...), custom_call_target="tpu_custom_call" | custom-call | bytes 3300000 | tf_op jit(solution)/shard_map/pallas_call | solution.py:142
  9.1 5.1 %collective-permute-start.3 = (bf16[256,2048]{1,0:T(8,128)(2,1)S(1)}, bf16[256,2048]{1,0:T(8,128)(2,1)S(1)}, u32[]{:S(2)}, u32[]{:S(2)}) collective-permute-start(bf16[256,2048]{1,0:T(8,128)(2,1)S(1)} %get-tuple-element.58), channel_id=1, source_target_pairs={{2,4},{6,8},{10,12},{14,16},{18,20},{22,24},{26,28},{30,32},{34,36... | collective-permute-start | bytes 3145736 | tf_op jit(solution)/shard_map/ppermute | solution.py:34
  14.3 0.0 collective-permute-done
  14.3 0.5 collective-permute-start.1
  14.9 3.3 %collective-permute-done.1 = bf16[2,2,2048]{2,1,0:T(2,128)(2,1)S(1)} collective-permute-done((bf16[2,2,2048]{2,1,0:T(2,128)(2,1)S(1)}, bf16[2,2,2048]{2,1,0:T(2,128)(2,1)S(1)}, u32[]{:S(2)}, u32[]{:S(2)}) %collective-permute-start.1) | collective-permute-done | bytes 16416 | tf_op jit(solution)/shard_map/ppermute | solution.py:28
  18.2 0.1 collective-permute-start.2
  18.3 0.1 collective-permute-start.4
  18.4 0.5 collective-permute-start.5
  18.9 0.1 collective-permute-start.6
  19.0 4.4 %collective-permute-done.2.b_ref = bf16[4,2,2048]{2,1,0:T(2,128)(2,1)S(1)} collective-permute-done((bf16[4,2,2048]{2,1,0:T(2,128)(2,1)S(1)}, bf16[4,2,2048]{2,1,0:T(2,128)(2,1)S(1)}, u32[]{:S(2)}, u32[]{:S(2)}) %collective-permute-start.2) | collective-permute-done | bytes 32800 | tf_op jit(solution)/shard_map/ppermute | solution.py:28
  23.4 0.0 collective-permute-start.7
  23.4 1.1 shard_map.93
  24.5 0.0 collective-permute-done.4.sk_ref
  24.5 0.0 collective-permute-done.5.sv_ref
  24.5 0.0 collective-permute-done.6.sq_ref
  24.5 0.4 collective-permute-done.7.sc_ref
  24.9 5.1 %collective-permute-done.3.x_ref.xk_ref.xv_ref = bf16[256,2048]{1,0:T(8,128)(2,1)S(1)} collective-permute-done((bf16[256,2048]{1,0:T(8,128)(2,1)S(1)}, bf16[256,2048]{1,0:T(8,128)(2,1)S(1)}, u32[]{:S(2)}, u32[]{:S(2)}) %collective-permute-start.3) | collective-permute-done | bytes 1048608 | tf_op jit(solution)/shard_map/ppermute | solution.py:34
  30.1 3.7 %all-to-all-start = ((bf16[16,32,1024]{2,1,0:T(8,128)(2,1)}), bf16[16,32,1024]{2,1,0:T(8,128)(2,1)S(1)}, u32[]{:S(2)}, u32[]{:S(2)}) async-start(bf16[16,32,1024]{2,1,0:T(8,128)(2,1)} %shard_map.93), calls=%async_computation | async-start | bytes 2097152 | tf_op jit(solution)/shard_map/all_to_all | solution.py:40
  33.7 0.0 copy-start.3
  33.8 0.6 shard_map.95
  34.4 0.4 collective-permute-start.8
  34.8 1.8 %collective-permute-done.8.sxk_ref.sxv_ref = bf16[256,1024]{1,0:T(8,128)(2,1)} collective-permute-done((bf16[256,1024]{1,0:T(8,128)(2,1)S(1)}, bf16[256,1024]{1,0:T(8,128)(2,1)}, u32[]{:S(2)}, u32[]{:S(2)}) %collective-permute-start.8) | collective-permute-done | bytes 524320 | tf_op jit(solution)/shard_map/ppermute | solution.py:28
  36.5 13.8 %all-to-all-done.level_ref = bf16[16,32,1024]{2,1,0:T(8,128)(2,1)S(1)} async-done(((bf16[16,32,1024]{2,1,0:T(8,128)(2,1)}), bf16[16,32,1024]{2,1,0:T(8,128)(2,1)S(1)}, u32[]{:S(2)}, u32[]{:S(2)}) %all-to-all-start) | async-done | bytes 1048608 | tf_op jit(solution)/shard_map/all_to_all | solution.py:40
  50.3 5.5 %collective-permute-start.9 = (bf16[256,2048]{1,0:T(8,128)(2,1)S(1)}, bf16[256,2048]{1,0:T(8,128)(2,1)S(1)}, u32[]{:S(2)}, u32[]{:S(2)}) collective-permute-start(bf16[256,2048]{1,0:T(8,128)(2,1)S(1)} %get-tuple-element.73), channel_id=1, source_target_pairs={{2,4},{6,8},{10,12},{14,16},{18,20},{22,24},{26,28},{30,32},{34,36... | collective-permute-start | bytes 3145736 | tf_op jit(solution)/shard_map/ppermute | solution.py:34
  55.8 10.6 %shard_map.96 = (bf16[128,1024]{1,0:T(8,128)(2,1)}, bf16[128,1024]{1,0:T(8,128)(2,1)}, bf16[128,1024]{1,0:T(8,128)(2,1)}, bf16[128,1024]{1,0:T(8,128)(2,1)}, f32...) custom-call(s32[3]{0:T(128)S(1)} %pad_add_fusion.ids_ref, ...), custom_call_target="tpu_custom_call" | custom-call | bytes 29700000 | tf_op jit(solution)/shard_map/pallas_call | solution.py:354
  66.4 4.8 %collective-permute-done.9.q_ref.c_ref = bf16[256,2048]{1,0:T(8,128)(2,1)S(1)} collective-permute-done((bf16[256,2048]{1,0:T(8,128)(2,1)S(1)}, bf16[256,2048]{1,0:T(8,128)(2,1)S(1)}, u32[]{:S(2)}, u32[]{:S(2)}) %collective-permute-start.9) | collective-permute-done | bytes 1048608 | tf_op jit(solution)/shard_map/ppermute | solution.py:34
  71.2 1.0 copy-done.4
  72.2 3.8 %all-to-all-start.1 = ((bf16[16,32,1024]{2,1,0:T(8,128)(2,1)}), bf16[16,32,1024]{2,1,0:T(8,128)(2,1)S(1)}, u32[]{:S(2)}, u32[]{:S(2)}) async-start(bf16[16,32,1024]{2,1,0:T(8,128)(2,1)} %get-tuple-element.75), calls=%async_computation.1 | async-start | bytes 2097152 | tf_op jit(solution)/shard_map/all_to_all | solution.py:40
  76.0 0.4 collective-permute-start.14
  76.4 0.2 collective-permute-start.15
  76.6 0.3 collective-permute-start.10
  76.9 0.2 collective-permute-start.12
  77.1 0.3 collective-permute-start.13
  77.4 1.6 %collective-permute-done.10 = f32[16,128]{1,0:T(8,128)S(1)} collective-permute-done((f32[16,128]{1,0:T(8,128)S(1)}, f32[16,128]{1,0:T(8,128)S(1)}, u32[]{:S(2)}, u32[]{:S(2)}) %collective-permute-start.10) | collective-permute-done | bytes 8224 | tf_op jit(solution)/shard_map/ppermute | solution.py:28
  79.1 7.1 %collective-permute-start.11 = (f32[2,16,128]{2,1,0:T(8,128)S(1)}, f32[2,16,128]{2,1,0:T(8,128)S(1)}, u32[]{:S(2)}, u32[]{:S(2)}) collective-permute-start(f32[2,16,128]{2,1,0:T(8,128)S(1)} %maximum_select_fusion), channel_id=1, source_target_pairs={{2,4},{6,8},{10,12},{14,16},{18,20},{22,24},{26,28},{30,32},{34,36... | collective-permute-start | bytes 49160 | tf_op jit(solution)/shard_map/ppermute | solution.py:34
  86.2 7.6 %collective-permute-done.11.stat_ref = f32[2,16,128]{2,1,0:T(8,128)S(1)} collective-permute-done((f32[2,16,128]{2,1,0:T(8,128)S(1)}, f32[2,16,128]{2,1,0:T(8,128)S(1)}, u32[]{:S(2)}, u32[]{:S(2)}) %collective-permute-start.11) | collective-permute-done | bytes 16416 | tf_op jit(solution)/shard_map/ppermute | solution.py:34
  93.8 0.0 all-to-all-done.1
  93.8 0.4 shard_map.98
  94.2 0.2 copy-done.13
  94.4 0.0 collective-permute-start.16
  94.4 5.6 %collective-permute-done.16.got_ref = f32[5,2,2048]{2,1,0:T(2,128)S(1)} collective-permute-done((f32[5,2,2048]{2,1,0:T(2,128)S(1)}, f32[5,2,2048]{2,1,0:T(2,128)S(1)}, u32[]{:S(2)}, u32[]{:S(2)}) %collective-permute-start.16) | collective-permute-done | bytes 81952 | tf_op jit(solution)/shard_map/ppermute | solution.py:28
  100.1 1.4 %collective-permute-start.17 = (f32[3,2,2048]{2,1,0:T(2,128)S(1)}, f32[3,2,2048]{2,1,0:T(2,128)S(1)}, u32[]{:S(2)}, u32[]{:S(2)}) collective-permute-start(f32[3,2,2048]{2,1,0:T(2,128)S(1)} %get-tuple-element.95), channel_id=1, source_target_pairs={{0,64},{2,66},{4,68},{6,70},{8,72},{10,74},{12,76},{14,78},{16,80}... | collective-permute-start | bytes 147464 | tf_op jit(solution)/shard_map/ppermute | solution.py:28
  101.5 0.0 collective-permute-done.12.satt_ref
  101.5 0.0 collective-permute-done.13.sdq_ref
  101.5 0.0 collective-permute-done.14.sdk_ref
  101.6 0.7 copy-done.7
  102.3 0.1 copy-done.8
  102.3 0.2 copy-done.5
  102.5 0.2 copy-done.6
  102.7 6.7 %shard_map.97 = (bf16[128,2048]{1,0:T(8,128)(2,1)}, bf16[128,2048]{1,0:T(8,128)(2,1)}, f32[128,2048]{1,0:T(8,128)S(1)}, f32[128,2048]{1,0:T(8,128)S(1)}) custom-call(s32[3]{0:T(128)S(1)} %pad_add_fusion.ids_ref, f32[3,16]{1,0:T(4,128)S(1)} %copy-done.3, bf16[128,2048]{1,0:T(8,128)(2,1)} %bitcast.20, bf16[128,2048]{1,0:T(8,128)(2,1)} %bitcast.24, ...), custom_call_target="tpu_custom_call" | custom-call | bytes 46200000 | tf_op jit(solution)/shard_map/pallas_call | solution.py:432
  109.4 0.0 collective-permute-done.17.got_ref
  109.5 0.1 collective-permute-start.18
  109.6 4.9 %collective-permute-done.18.got_ref = f32[2,2,2048]{2,1,0:T(2,128)S(1)} collective-permute-done((f32[2,2,2048]{2,1,0:T(2,128)S(1)}, f32[2,2,2048]{2,1,0:T(2,128)S(1)}, u32[]{:S(2)}, u32[]{:S(2)}) %collective-permute-start.18) | collective-permute-done | bytes 32800 | tf_op jit(solution)/shard_map/ppermute | solution.py:28
  114.5 5.6 %collective-permute-start.19 = (f32[1,2,2048]{2,1,0:T(2,128)S(1)}, f32[1,2,2048]{2,1,0:T(2,128)S(1)}, u32[]{:S(2)}, u32[]{:S(2)}) collective-permute-start(f32[1,2,2048]{2,1,0:T(2,128)S(1)} %slice_add_fusion), channel_id=1, source_target_pairs={{0,1},{1,0},{2,3},{3,2},{4,5},{5,4},{6,7},{7,6},{8,9},{9,8},{10,11... | collective-permute-start | bytes 49160 | tf_op jit(solution)/shard_map/ppermute | solution.py:596
  120.1 1.7 %shard_map.101 = (bf16[128,2048]{1,0:T(8,128)(2,1)}, bf16[128,2048]{1,0:T(8,128)(2,1)}) custom-call(f32[16,2048]{1,0:T(8,128)S(1)} %get-tuple-element.90.one_ref, f32[1,2,2048]{2,1,0:T(2,128)S(1)} %get-tuple-element.97.far_ref, f32[2,2,2048]{2,1,0:T(2,128)S(1)} %collective-permute-done.18.got_ref, f32[128,2048]{1,0:T(8,128)S(1)} %get-tuple-element.102.dk_ref, ...), custom_call_target="tpu_custom_call" | custom-call | bytes 6600000 | tf_op jit(solution)/shard_map/pallas_call | solution.py:528
  121.8 0.4 collective-permute-done.19
  122.2 0.1 copy.11
  122.3 0.6 reduce_sum.9
  (37 shorter events, 0.2 us)
Async XLA Ops:
  0.6 1.0 copy-start.1
  1.7 1.0 copy-start.2
  3.2 11.0 %collective-permute-start = (bf16[1,2,2048]{2,1,0:T(2,128)(2,1)S(1)}, bf16[1,2,2048]{2,1,0:T(2,128)(2,1)S(1)}, u32[]{:S(2)}, u32[]{:S(2)}) collective-permute-start(bf16[1,2,2048]{2,1,0:T(2,128)(2,1)S(1)} %get-tuple-element.57), channel_id=1, source_target_pairs={{0,32},{2,34},{4,36},{6,38},{8,40},{10,42},{12,44},{14,46},{16,48}... | collective-permute-start | bytes 24584 | tf_op jit(solution)/shard_map/ppermute | solution.py:28
  9.1 20.9 %collective-permute-start.3 = (bf16[256,2048]{1,0:T(8,128)(2,1)S(1)}, bf16[256,2048]{1,0:T(8,128)(2,1)S(1)}, u32[]{:S(2)}, u32[]{:S(2)}) collective-permute-start(bf16[256,2048]{1,0:T(8,128)(2,1)S(1)} %get-tuple-element.58), channel_id=1, source_target_pairs={{2,4},{6,8},{10,12},{14,16},{18,20},{22,24},{26,28},{30,32},{34,36... | collective-permute-start | bytes 3145736 | tf_op jit(solution)/shard_map/ppermute | solution.py:34
  14.3 3.8 %collective-permute-start.1 = (bf16[2,2,2048]{2,1,0:T(2,128)(2,1)S(1)}, bf16[2,2,2048]{2,1,0:T(2,128)(2,1)S(1)}, u32[]{:S(2)}, u32[]{:S(2)}) collective-permute-start(bf16[2,2,2048]{2,1,0:T(2,128)(2,1)S(1)} %pad_maximum_fusion), channel_id=1, source_target_pairs={{0,64},{2,66},{4,68},{6,70},{8,72},{10,74},{12,76},{14,78},{16,80}... | collective-permute-start | bytes 49160 | tf_op jit(solution)/shard_map/ppermute | solution.py:28
  18.2 5.2 %collective-permute-start.2 = (bf16[4,2,2048]{2,1,0:T(2,128)(2,1)S(1)}, bf16[4,2,2048]{2,1,0:T(2,128)(2,1)S(1)}, u32[]{:S(2)}, u32[]{:S(2)}) collective-permute-start(bf16[4,2,2048]{2,1,0:T(2,128)(2,1)S(1)} %constant_dynamic-update-slice_fusion.a_ref), channel_id=1, source_target_pairs={{0,192},{2,194},{4,196},{6,198},{8,200},{10,202},{12,204},{14,206}... | collective-permute-start | bytes 98312 | tf_op jit(solution)/shard_map/ppermute | solution.py:28
  18.3 6.2 %collective-permute-start.4 = (bf16[128,1024]{1,0:T(8,128)(2,1)S(1)}, bf16[128,1024]{1,0:T(8,128)(2,1)S(1)}, u32[]{:S(2)}, u32[]{:S(2)}) collective-permute-start(bf16[128,1024]{1,0:T(8,128)(2,1)S(1)} %get-tuple-element.59), channel_id=1, source_target_pairs={{0,2},{2,0},{4,6},{6,4},{8,10},{10,8},{12,14},{14,12},{16,18},{18,... | collective-permute-start | bytes 786440 | tf_op jit(solution)/shard_map/ppermute | solution.py:28
  18.4 6.1 %collective-permute-start.5 = (bf16[128,1024]{1,0:T(8,128)(2,1)S(1)}, bf16[128,1024]{1,0:T(8,128)(2,1)S(1)}, u32[]{:S(2)}, u32[]{:S(2)}) collective-permute-start(bf16[128,1024]{1,0:T(8,128)(2,1)S(1)} %get-tuple-element.60), channel_id=1, source_target_pairs={{0,2},{2,0},{4,6},{6,4},{8,10},{10,8},{12,14},{14,12},{16,18},{18,... | collective-permute-start | bytes 786440 | tf_op jit(solution)/shard_map/ppermute | solution.py:28
  18.9 5.7 %collective-permute-start.6 = (bf16[128,1024]{1,0:T(8,128)(2,1)S(1)}, bf16[128,1024]{1,0:T(8,128)(2,1)S(1)}, u32[]{:S(2)}, u32[]{:S(2)}) collective-permute-start(bf16[128,1024]{1,0:T(8,128)(2,1)S(1)} %get-tuple-element.61), channel_id=1, source_target_pairs={{0,2},{2,0},{4,6},{6,4},{8,10},{10,8},{12,14},{14,12},{16,18},{18,... | collective-permute-start | bytes 786440 | tf_op jit(solution)/shard_map/ppermute | solution.py:28
  23.4 1.5 %collective-permute-start.7 = (bf16[128,1024]{1,0:T(8,128)(2,1)S(1)}, bf16[128,1024]{1,0:T(8,128)(2,1)S(1)}, u32[]{:S(2)}, u32[]{:S(2)}) collective-permute-start(bf16[128,1024]{1,0:T(8,128)(2,1)S(1)} %get-tuple-element.62), channel_id=1, source_target_pairs={{0,2},{2,0},{4,6},{6,4},{8,10},{10,8},{12,14},{14,12},{16,18},{18,... | collective-permute-start | bytes 786440 | tf_op jit(solution)/shard_map/ppermute | solution.py:28
  24.5 5.6 %copy-start.9 = (bf16[128,1024]{1,0:T(8,128)(2,1)}, bf16[128,1024]{1,0:T(8,128)(2,1)S(1)}, u32[]{:S(2)}) copy-start(bf16[128,1024]{1,0:T(8,128)(2,1)S(1)} %collective-permute-done.4.sk_ref) | copy-start | bytes 786436
  24.5 5.5 %copy-start.10 = (bf16[128,1024]{1,0:T(8,128)(2,1)}, bf16[128,1024]{1,0:T(8,128)(2,1)S(1)}, u32[]{:S(2)}) copy-start(bf16[128,1024]{1,0:T(8,128)(2,1)S(1)} %collective-permute-done.5.sv_ref) | copy-start | bytes 786436
  24.5 5.5 %copy-start.11 = (bf16[128,1024]{1,0:T(8,128)(2,1)}, bf16[128,1024]{1,0:T(8,128)(2,1)S(1)}, u32[]{:S(2)}) copy-start(bf16[128,1024]{1,0:T(8,128)(2,1)S(1)} %collective-permute-done.6.sq_ref) | copy-start | bytes 786436
  24.9 5.1 %copy-start.12 = (bf16[128,1024]{1,0:T(8,128)(2,1)}, bf16[128,1024]{1,0:T(8,128)(2,1)S(1)}, u32[]{:S(2)}) copy-start(bf16[128,1024]{1,0:T(8,128)(2,1)S(1)} %collective-permute-done.7.sc_ref) | copy-start | bytes 786436
  30.1 4.3 %copy-start = (bf16[256,2048]{1,0:T(8,128)(2,1)}, bf16[256,2048]{1,0:T(8,128)(2,1)S(1)}, u32[]{:S(2)}) copy-start(bf16[256,2048]{1,0:T(8,128)(2,1)S(1)} %collective-permute-done.3.x_ref.xk_ref.xv_ref) | copy-start | bytes 3145732
  30.1 20.2 %all-to-all-start = ((bf16[16,32,1024]{2,1,0:T(8,128)(2,1)}), bf16[16,32,1024]{2,1,0:T(8,128)(2,1)S(1)}, u32[]{:S(2)}, u32[]{:S(2)}) async-start(bf16[16,32,1024]{2,1,0:T(8,128)(2,1)} %shard_map.93), calls=%async_computation | async-start | bytes 2097152 | tf_op jit(solution)/shard_map/all_to_all | solution.py:40
  33.7 22.1 %copy-start.3 = (f32[3,16]{1,0:T(4,128)S(1)}, f32[3,16]{1,0:T(4,128)}, u32[]{:S(2)}) copy-start(f32[3,16]{1,0:T(4,128)} %bias_ref.3) | copy-start | bytes 580
  34.4 2.1 %collective-permute-start.8 = (bf16[256,1024]{1,0:T(8,128)(2,1)S(1)}, bf16[256,1024]{1,0:T(8,128)(2,1)}, u32[]{:S(2)}, u32[]{:S(2)}) collective-permute-start(bf16[256,1024]{1,0:T(8,128)(2,1)S(1)} %shard_map.95), channel_id=1, source_target_pairs={{0,2},{2,0},{4,6},{6,4},{8,10},{10,8},{12,14},{14,12},{16,18},{18,... | collective-permute-start | bytes 1572872 | tf_op jit(solution)/shard_map/ppermute | solution.py:28
  50.3 20.9 %collective-permute-start.9 = (bf16[256,2048]{1,0:T(8,128)(2,1)S(1)}, bf16[256,2048]{1,0:T(8,128)(2,1)S(1)}, u32[]{:S(2)}, u32[]{:S(2)}) collective-permute-start(bf16[256,2048]{1,0:T(8,128)(2,1)S(1)} %get-tuple-element.73), channel_id=1, source_target_pairs={{2,4},{6,8},{10,12},{14,16},{18,20},{22,24},{26,28},{30,32},{34,36... | collective-permute-start | bytes 3145736 | tf_op jit(solution)/shard_map/ppermute | solution.py:34
  71.2 1.0 copy-start.4
  72.2 4.2 %copy-start.15 = (f32[128,1024]{1,0:T(8,128)S(1)}, f32[128,1024]{1,0:T(8,128)}, u32[]{:S(2)}) copy-start(f32[128,1024]{1,0:T(8,128)} %get-tuple-element.86) | copy-start | bytes 1572868
  72.2 4.4 %copy-start.17 = (f32[16,128]{1,0:T(8,128)S(1)}, f32[16,128]{1,0:T(8,128)}, u32[]{:S(2)}) copy-start(f32[16,128]{1,0:T(8,128)} %get-tuple-element.77) | copy-start | bytes 24580
  72.2 4.9 %copy-start.16 = (bf16[128,1024]{1,0:T(8,128)(2,1)S(1)}, bf16[128,1024]{1,0:T(8,128)(2,1)}, u32[]{:S(2)}) copy-start(bf16[128,1024]{1,0:T(8,128)(2,1)} %get-tuple-element.82) | copy-start | bytes 786436
  72.2 21.6 %all-to-all-start.1 = ((bf16[16,32,1024]{2,1,0:T(8,128)(2,1)}), bf16[16,32,1024]{2,1,0:T(8,128)(2,1)S(1)}, u32[]{:S(2)}, u32[]{:S(2)}) async-start(bf16[16,32,1024]{2,1,0:T(8,128)(2,1)} %get-tuple-element.75), calls=%async_computation.1 | async-start | bytes 2097152 | tf_op jit(solution)/shard_map/all_to_all | solution.py:40
  76.0 3.1 %copy-start.14 = (f32[16,128]{1,0:T(8,128)S(1)}, f32[16,128]{1,0:T(8,128)}, u32[]{:S(2)}) copy-start(f32[16,128]{1,0:T(8,128)} %get-tuple-element.76) | copy-start | bytes 24580
  76.0 25.5 %collective-permute-start.14 = (f32[128,1024]{1,0:T(8,128)}, f32[128,1024]{1,0:T(8,128)S(1)}, u32[]{:S(2)}, u32[]{:S(2)}) collective-permute-start(f32[128,1024]{1,0:T(8,128)} %get-tuple-element.84), channel_id=1, source_target_pairs={{0,2},{2,0},{4,6},{6,4},{8,10},{10,8},{12,14},{14,12},{16,18},{18,... | collective-permute-start | bytes 1572872 | tf_op jit(solution)/shard_map/ppermute | solution.py:28
  76.4 25.2 %collective-permute-start.15 = (f32[128,1024]{1,0:T(8,128)S(1)}, f32[128,1024]{1,0:T(8,128)S(1)}, u32[]{:S(2)}, u32[]{:S(2)}) collective-permute-start(f32[128,1024]{1,0:T(8,128)S(1)} %copy-done.15), channel_id=1, source_target_pairs={{0,2},{2,0},{4,6},{6,4},{8,10},{10,8},{12,14},{14,12},{16,18},{18,... | collective-permute-start | bytes 1572872 | tf_op jit(solution)/shard_map/ppermute | solution.py:28
  76.6 2.4 %collective-permute-start.10 = (f32[16,128]{1,0:T(8,128)S(1)}, f32[16,128]{1,0:T(8,128)S(1)}, u32[]{:S(2)}, u32[]{:S(2)}) collective-permute-start(f32[16,128]{1,0:T(8,128)S(1)} %copy-done.17), channel_id=1, source_target_pairs={{0,2},{2,0},{4,6},{6,4},{8,10},{10,8},{12,14},{14,12},{16,18},{18,... | collective-permute-start | bytes 24584 | tf_op jit(solution)/shard_map/ppermute | solution.py:28
  76.9 24.6 %collective-permute-start.12 = (bf16[128,1024]{1,0:T(8,128)(2,1)}, bf16[128,1024]{1,0:T(8,128)(2,1)S(1)}, u32[]{:S(2)}, u32[]{:S(2)}) collective-permute-start(bf16[128,1024]{1,0:T(8,128)(2,1)} %get-tuple-element.80), channel_id=1, source_target_pairs={{0,2},{2,0},{4,6},{6,4},{8,10},{10,8},{12,14},{14,12},{16,18},{18,... | collective-permute-start | bytes 786440 | tf_op jit(solution)/shard_map/ppermute | solution.py:28
  77.1 24.4 %collective-permute-start.13 = (bf16[128,1024]{1,0:T(8,128)(2,1)S(1)}, bf16[128,1024]{1,0:T(8,128)(2,1)S(1)}, u32[]{:S(2)}, u32[]{:S(2)}) collective-permute-start(bf16[128,1024]{1,0:T(8,128)(2,1)S(1)} %copy-done.16), channel_id=1, source_target_pairs={{0,2},{2,0},{4,6},{6,4},{8,10},{10,8},{12,14},{14,12},{16,18},{18,... | collective-permute-start | bytes 786440 | tf_op jit(solution)/shard_map/ppermute | solution.py:28
  79.1 14.7 %collective-permute-start.11 = (f32[2,16,128]{2,1,0:T(8,128)S(1)}, f32[2,16,128]{2,1,0:T(8,128)S(1)}, u32[]{:S(2)}, u32[]{:S(2)}) collective-permute-start(f32[2,16,128]{2,1,0:T(8,128)S(1)} %maximum_select_fusion), channel_id=1, source_target_pairs={{2,4},{6,8},{10,12},{14,16},{18,20},{22,24},{26,28},{30,32},{34,36... | collective-permute-start | bytes 49160 | tf_op jit(solution)/shard_map/ppermute | solution.py:34
  93.8 0.6 copy-start.13
  94.4 5.7 %collective-permute-start.16 = (f32[5,2,2048]{2,1,0:T(2,128)S(1)}, f32[5,2,2048]{2,1,0:T(2,128)S(1)}, u32[]{:S(2)}, u32[]{:S(2)}) collective-permute-start(f32[5,2,2048]{2,1,0:T(2,128)S(1)} %get-tuple-element.92), channel_id=1, source_target_pairs={{0,192},{2,194},{4,196},{6,198},{8,200},{10,202},{12,204},{14,206}... | collective-permute-start | bytes 245768 | tf_op jit(solution)/shard_map/ppermute | solution.py:28
  100.1 9.4 %collective-permute-start.17 = (f32[3,2,2048]{2,1,0:T(2,128)S(1)}, f32[3,2,2048]{2,1,0:T(2,128)S(1)}, u32[]{:S(2)}, u32[]{:S(2)}) collective-permute-start(f32[3,2,2048]{2,1,0:T(2,128)S(1)} %get-tuple-element.95), channel_id=1, source_target_pairs={{0,64},{2,66},{4,68},{6,70},{8,72},{10,74},{12,76},{14,78},{16,80}... | collective-permute-start | bytes 147464 | tf_op jit(solution)/shard_map/ppermute | solution.py:28
  101.5 0.7 copy-start.7
  101.5 0.8 copy-start.8
  101.6 0.9 copy-start.5
  101.6 1.1 copy-start.6
  109.5 5.0 %collective-permute-start.18 = (f32[2,2,2048]{2,1,0:T(2,128)S(1)}, f32[2,2,2048]{2,1,0:T(2,128)S(1)}, u32[]{:S(2)}, u32[]{:S(2)}) collective-permute-start(f32[2,2,2048]{2,1,0:T(2,128)S(1)} %get-tuple-element.101), channel_id=1, source_target_pairs={{0,32},{2,34},{4,36},{6,38},{8,40},{10,42},{12,44},{14,46},{16,48}... | collective-permute-start | bytes 98312 | tf_op jit(solution)/shard_map/ppermute | solution.py:28
  114.5 7.7 %collective-permute-start.19 = (f32[1,2,2048]{2,1,0:T(2,128)S(1)}, f32[1,2,2048]{2,1,0:T(2,128)S(1)}, u32[]{:S(2)}, u32[]{:S(2)}) collective-permute-start(f32[1,2,2048]{2,1,0:T(2,128)S(1)} %slice_add_fusion), channel_id=1, source_target_pairs={{0,1},{1,0},{2,3},{3,2},{4,5},{5,4},{6,7},{7,6},{8,9},{9,8},{10,11... | collective-permute-start | bytes 49160 | tf_op jit(solution)/shard_map/ppermute | solution.py:596

commit v3 on v2

--- a/solution.py
+++ b/solution.py
@@ -250,7 +250,7 @@
         block = block[0:8]
         edge_ref[...] = jnp.where((block == 0) | (block == last), NEGATIVE, 0.0)
 
-    for j in range(heads):
+    def one_head(j):
         cols = slice(j * HEAD, (j + 1) * HEAD)
         head = step * heads + j
         whole_head = core * (steps * heads) + head
@@ -271,6 +271,7 @@
         near = nt(k_near, q_both)
         edge = jnp.concatenate([nt(xk, q), nt(sxk, sq)], axis=1)
         far = nt(k_far, q_both) * unit + mask_ref[...]
+        yield
         parts = [near, edge, far[0:ROWS], far[ROWS:]]
         shifts = [bias[0], bias[0] + edge_ref[0:1], bias[1], bias[2]]
         tops = [jnp.max(x, axis=0, keepdims=True) for x in parts]
@@ -283,6 +284,7 @@
         share = 1.0 / total
         weights = [p * share for p in powers]
 
+        yield
         g_far = nt(v_far, c_both)
         grads = [
             nt(v_near, c_both),
@@ -290,6 +292,7 @@
             g_far[0:ROWS],
             g_far[ROWS:],
         ]
+        yield
         deltas = [
             jnp.sum(w * g, axis=0, keepdims=True) for w, g in zip(weights, grads)
         ]
@@ -297,6 +300,7 @@
         score_grads = [w * (g - delta) for w, g in zip(weights, grads)]
         w_near, w_edge, w_one, w_two = [w.astype(BF) for w in weights]
         d_near, d_edge, d_one, d_two = [d.astype(BF) for d in score_grads]
+        yield
         w_far = jnp.concatenate([w_one, w_two], axis=0)
         d_far = jnp.concatenate([d_one, d_two], axis=0)
 
@@ -307,6 +311,7 @@
         dq_ref[:, cols] = ((dq[0:ROWS] + tn(d_edge[:, 0:ROWS], xk)) * scale).astype(BF)
         sdq_ref[:, cols] = ((dq[ROWS:] + tn(d_edge[:, ROWS:], sxk)) * scale).astype(BF)
 
+        yield
         dk = nn(d_near, q_both) * scale
         dk_ref[:, cols] = dk[0:ROWS]
         sdk_ref[:, cols] = dk[ROWS:]
@@ -331,11 +336,17 @@
         stat_ref[low] = delta[:, 0:ROWS]
         sstat_ref[low] = delta[:, ROWS:]
 
+    running = [one_head(j) for j in range(heads)]
+    for turn in range(heads + 5):
+        for j in range(heads):
+            if 0 <= turn - j <= 5:
+                next(running[j], None)
+
 
 def attend(ids, bias, own, sib, x, sx, level):
     width = own[0].shape[1]
     half = width // 2
-    heads = 2
+    heads = 4
     block = heads * HEAD
     steps = half // block
     rows = ROWS
@@ -388,24 +399,16 @@
     q_ref,
     c_ref,
     stat_ref,
-    att_ref,
-    satt_ref,
-    dq_ref,
-    sdq_ref,
     dk_ref,
     sdk_ref,
     dv_ref,
     sdv_ref,
-    out_att_ref,
-    out_dq_ref,
     out_dk_ref,
     out_dv_ref,
 ):
     step = pl.program_id(0)
     mine = step // per_half == ids_ref[1]
     scale = HEAD**-0.5
-    out_att_ref[...] = jnp.where(mine, att_ref[...], satt_ref[...])
-    out_dq_ref[...] = jnp.where(mine, dq_ref[...], sdq_ref[...])
     for j in range(heads):
         cols = slice(j * HEAD, (j + 1) * HEAD)
         bias = bias_ref[0, step * heads + j] * LOG2E
@@ -442,14 +445,36 @@
                 pl.BlockSpec((rows, block), lambda i, ids: (1, i)),
                 pl.BlockSpec((1, 16, rows), lambda i, ids: (i // per_half, 0, 0)),
             ]
-            + [part] * 8,
-            out_specs=[whole] * 4,
+            + [part] * 4,
+            out_specs=[whole] * 2,
         ),
-        out_shape=out_hbm([jax.ShapeDtypeStruct((rows, width), BF)] * 2)
-        + [jax.ShapeDtypeStruct((rows, width), F32)] * 2,
+        out_shape=[jax.ShapeDtypeStruct((rows, width), F32)] * 2,
         compiler_params=params(),
         cost_estimate=cost(14),
-    )(ids, bias, *in_hbm(k, v, x, x, stat, *parts))
+    )(ids, bias, *in_hbm(k, v), x, x, *in_hbm(stat, *parts))
+
+
+def join_kernel(ids_ref, att_ref, satt_ref, dq_ref, sdq_ref, out_att_ref, out_dq_ref):
+    mine = pl.program_id(0) == ids_ref[1]
+    out_att_ref[...] = jnp.where(mine, att_ref[...], satt_ref[...])
+    out_dq_ref[...] = jnp.where(mine, dq_ref[...], sdq_ref[...])
+
+
+def join(ids, *parts):
+    rows, half = parts[0].shape
+    part = pl.BlockSpec((rows, half), lambda i, ids: (0, 0))
+    return pl.pallas_call(
+        join_kernel,
+        grid_spec=pltpu.PrefetchScalarGridSpec(
+            num_scalar_prefetch=1,
+            grid=(2,),
+            in_specs=[part] * 4,
+            out_specs=[pl.BlockSpec((rows, half), lambda i, ids: (0, i))] * 2,
+        ),
+        out_shape=out_hbm([jax.ShapeDtypeStruct((rows, 2 * half), BF)] * 2),
+        compiler_params=params(),
+        cost_estimate=cost(6),
+    )(ids, *in_hbm(*parts))
 
 
 def sums_kernel(x_ref, one_ref, low_ref, high_ref, level_ref):
@@ -576,15 +601,9 @@
     x_stats = cross(stats)
     grads, x_stats = lax.optimization_barrier((grads, x_stats))
     ratt, rdq, rdk, rdv = [swap(s, SIB) for s in (satt, sdq, sdk, sdv)]
-    att, dq, dk, dv = edge(
-        ids,
-        level_bias,
-        k,
-        v,
-        x_qc,
-        x_stats,
-        (att, ratt, dq, rdq, dk, rdk, dv, rdv),
-    )
+    att, dq = join(ids, att, ratt, dq, rdq)
+    grads, att, dq = lax.optimization_barrier((grads, att, dq))
+    dk, dv = edge(ids, level_bias, k, v, x_qc, x_stats, (dk, rdk, dv, rdv))
 
     one, low, high, level = sums(grads)
     low, high, level = step(low, swap(high, YB), level)

time: 123 us -> 121 us (0.984)
  waiting for transfers between devices: 53.8 us -> 51.1 us
    pallas_call x0 -> x1, Pallas kernels: none -> 2.75 us  [join(): pl.pallas_call(join_kernel, grid_spec=pltpu.PrefetchScalarGridSpec(num_sc...]
    ppermute x3, waiting for transfers between devices: 17.6 us -> 15.1 us  [cross(): return lax.ppermute(x, 'seq', pairs + [(j, i) for i, j in pairs])]
    pallas_call x1, Pallas kernels: 10.6 us -> 9.22 us  [attend(): pl.pallas_call(functools.partial(attend_kernel, steps, heads), grid_spec=...]
    pallas_call x1, Pallas kernels: 6.75 us -> 5.5 us  [edge(): pl.pallas_call(functools.partial(edge_kernel, per_half, heads), grid_spec...]
    unnamed x39 -> x31, local copies, waits for them, and re-layouts: 4.5 us -> 4.76 us
  transfers between devices with their start and end apart: 22 -> 22, of which waited for: 12 -> 12; matrix products, arithmetic and copies ran while one was open for 0% -> 0% of each run, Pallas kernels for 19% -> 20%
where the time goes in v3:
time: 121 us; the launch traced here: 120 us
  waiting for transfers between devices  51.1 us (42%)
  starting transfers between devices  38.4 us (32%)
  Pallas kernels  24.2 us (20%)
  local copies, waits for them, and re-layouts  4.79 us (4%)
    ppermute x16, waiting for transfers between devices, swap(): lax.ppermute(x, 'seq', [(i, i ^ mask) for i in range(lax.axis_size('seq'))])  21.8 us
    ppermute x3, starting transfers between devices, cross(): return lax.ppermute(x, 'seq', pairs + [(j, i) for i, j in pairs])  17.6 us
    ppermute x3, waiting for transfers between devices, cross(): return lax.ppermute(x, 'seq', pairs + [(j, i) for i, j in pairs])  15.1 us
    all_to_all x2, waiting for transfers between devices, in_group(): return lax.all_to_all(x, 'seq', 0, 0, axis_index_groups=groups)  13.8 us
    pallas_call x1, Pallas kernels, attend(): pl.pallas_call(functools.partial(attend_kernel, steps, heads), grid_spec=...  9.22 us
    ppermute x16, starting transfers between devices, swap(): lax.ppermute(x, 'seq', [(i, i ^ mask) for i in range(lax.axis_size('seq'))])  7.89 us
    all_to_all x2, starting transfers between devices, in_group(): return lax.all_to_all(x, 'seq', 0, 0, axis_index_groups=groups)  7.32 us
    ppermute x1, starting transfers between devices, body(): level = level + lax.ppermute(level, 'batch', [(0, 1), (1, 0)])  5.66 us
  transfers between devices with their start and end apart: 22, of which 12 were waited for; matrix products, arithmetic and copies ran while one was open for 0% of the time, Pallas kernels for 20%

profile of v3, /device:TPU:24, one launch (start us, length us, event | category | flops | bytes accessed | tf_op | source)
XLA Modules:
  0.0 120.2 jit_solution(16060319062388277824)
XLA Ops:
  0.6 0.0 copy-start.1
  0.6 1.0 copy-done.1
  1.7 1.0 copy-done.2
  2.7 0.5 shard_map.92
  3.2 3.4 %collective-permute-start = (bf16[1,2,2048]{2,1,0:T(2,128)(2,1)S(1)}, bf16[1,2,2048]{2,1,0:T(2,128)(2,1)S(1)}, u32[]{:S(2)}, u32[]{:S(2)}) collective-permute-start(bf16[1,2,2048]{2,1,0:T(2,128)(2,1)S(1)} %get-tuple-element.60), channel_id=1, source_target_pairs={{0,32},{2,34},{4,36},{6,38},{8,40},{10,42},{12,44},{14,46},{16,48}... | collective-permute-start | bytes 24584 | tf_op jit(solution)/shard_map/ppermute | solution.py:28
  6.6 0.1 pad_add_fusion.ids_ref
  6.7 2.4 %shard_map.94 = (bf16[256,2048]{1,0:T(8,128)(2,1)S(1)}, bf16[256,2048]{1,0:T(8,128)(2,1)S(1)}, bf16[128,1024]{1,0:T(8,128)(2,1)S(1)}, bf16[128,1024]{1,0:T(8,128...) custom-call(s32[3]{0:T(128)S(1)} %pad_add_fusion.ids_ref, bf16[128,2048]{1,0:T(8,128)(2,1)} %bitcast.18, ...), custom_call_target="tpu_custom_call" | custom-call | bytes 3300000 | tf_op jit(solution)/shard_map/pallas_call | solution.py:142
  9.1 5.1 %collective-permute-start.3 = (bf16[256,2048]{1,0:T(8,128)(2,1)S(1)}, bf16[256,2048]{1,0:T(8,128)(2,1)S(1)}, u32[]{:S(2)}, u32[]{:S(2)}) collective-permute-start(bf16[256,2048]{1,0:T(8,128)(2,1)S(1)} %get-tuple-element.61), channel_id=1, source_target_pairs={{2,4},{6,8},{10,12},{14,16},{18,20},{22,24},{26,28},{30,32},{34,36... | collective-permute-start | bytes 3145736 | tf_op jit(solution)/shard_map/ppermute | solution.py:34
  14.3 0.0 collective-permute-done
  14.3 0.5 collective-permute-start.1
  14.9 3.3 %collective-permute-done.1 = bf16[2,2,2048]{2,1,0:T(2,128)(2,1)S(1)} collective-permute-done((bf16[2,2,2048]{2,1,0:T(2,128)(2,1)S(1)}, bf16[2,2,2048]{2,1,0:T(2,128)(2,1)S(1)}, u32[]{:S(2)}, u32[]{:S(2)}) %collective-permute-start.1) | collective-permute-done | bytes 16416 | tf_op jit(solution)/shard_map/ppermute | solution.py:28
  18.2 0.1 collective-permute-start.2
  18.3 0.1 collective-permute-start.4
  18.4 0.5 collective-permute-start.5
  18.9 0.1 collective-permute-start.6
  19.0 4.4 %collective-permute-done.2.b_ref = bf16[4,2,2048]{2,1,0:T(2,128)(2,1)S(1)} collective-permute-done((bf16[4,2,2048]{2,1,0:T(2,128)(2,1)S(1)}, bf16[4,2,2048]{2,1,0:T(2,128)(2,1)S(1)}, u32[]{:S(2)}, u32[]{:S(2)}) %collective-permute-start.2) | collective-permute-done | bytes 32800 | tf_op jit(solution)/shard_map/ppermute | solution.py:28
  23.4 0.0 collective-permute-start.7
  23.4 1.1 shard_map.93
  24.5 0.0 collective-permute-done.4.sk_ref
  24.5 0.0 collective-permute-done.5.sv_ref
  24.5 0.0 collective-permute-done.6.sq_ref
  24.5 0.0 copy-start.8
  24.5 0.4 collective-permute-done.7.sc_ref
  24.9 0.7 copy-done.9
  25.6 4.4 %collective-permute-done.3.x_ref.xk_ref.xv_ref = bf16[256,2048]{1,0:T(8,128)(2,1)S(1)} collective-permute-done((bf16[256,2048]{1,0:T(8,128)(2,1)S(1)}, bf16[256,2048]{1,0:T(8,128)(2,1)S(1)}, u32[]{:S(2)}, u32[]{:S(2)}) %collective-permute-start.3) | collective-permute-done | bytes 1048608 | tf_op jit(solution)/shard_map/ppermute | solution.py:34
  30.1 3.7 %all-to-all-start = ((bf16[16,32,1024]{2,1,0:T(8,128)(2,1)}), bf16[16,32,1024]{2,1,0:T(8,128)(2,1)S(1)}, u32[]{:S(2)}, u32[]{:S(2)}) async-start(bf16[16,32,1024]{2,1,0:T(8,128)(2,1)} %shard_map.93), calls=%async_computation | async-start | bytes 2097152 | tf_op jit(solution)/shard_map/all_to_all | solution.py:40
  33.7 0.0 copy-start.3
  33.8 0.6 shard_map.95
  34.4 0.4 collective-permute-start.8
  34.7 1.8 %collective-permute-done.8.sxk_ref.sxv_ref = bf16[256,1024]{1,0:T(8,128)(2,1)} collective-permute-done((bf16[256,1024]{1,0:T(8,128)(2,1)S(1)}, bf16[256,1024]{1,0:T(8,128)(2,1)}, u32[]{:S(2)}, u32[]{:S(2)}) %collective-permute-start.8) | collective-permute-done | bytes 524320 | tf_op jit(solution)/shard_map/ppermute | solution.py:28
  36.5 13.8 %all-to-all-done.level_ref = bf16[16,32,1024]{2,1,0:T(8,128)(2,1)S(1)} async-done(((bf16[16,32,1024]{2,1,0:T(8,128)(2,1)}), bf16[16,32,1024]{2,1,0:T(8,128)(2,1)S(1)}, u32[]{:S(2)}, u32[]{:S(2)}) %all-to-all-start) | async-done | bytes 1048608 | tf_op jit(solution)/shard_map/all_to_all | solution.py:40
  50.3 5.5 %collective-permute-start.9 = (bf16[256,2048]{1,0:T(8,128)(2,1)S(1)}, bf16[256,2048]{1,0:T(8,128)(2,1)S(1)}, u32[]{:S(2)}, u32[]{:S(2)}) collective-permute-start(bf16[256,2048]{1,0:T(8,128)(2,1)S(1)} %get-tuple-element.76), channel_id=1, source_target_pairs={{2,4},{6,8},{10,12},{14,16},{18,20},{22,24},{26,28},{30,32},{34,36... | collective-permute-start | bytes 3145736 | tf_op jit(solution)/shard_map/ppermute | solution.py:34
  55.8 9.2 %shard_map.96 = (bf16[128,1024]{1,0:T(8,128)(2,1)}, bf16[128,1024]{1,0:T(8,128)(2,1)}, bf16[128,1024]{1,0:T(8,128)(2,1)}, bf16[128,1024]{1,0:T(8,128)(2,1)}, f32...) custom-call(s32[3]{0:T(128)S(1)} %pad_add_fusion.ids_ref, ...), custom_call_target="tpu_custom_call" | custom-call | bytes 29700000 | tf_op jit(solution)/shard_map/pallas_call | solution.py:365
  65.0 6.2 %collective-permute-done.9.q_ref.c_ref = bf16[256,2048]{1,0:T(8,128)(2,1)S(1)} collective-permute-done((bf16[256,2048]{1,0:T(8,128)(2,1)S(1)}, bf16[256,2048]{1,0:T(8,128)(2,1)S(1)}, u32[]{:S(2)}, u32[]{:S(2)}) %collective-permute-start.9) | collective-permute-done | bytes 1048608 | tf_op jit(solution)/shard_map/ppermute | solution.py:34
  71.2 3.7 %all-to-all-start.1 = ((bf16[16,32,1024]{2,1,0:T(8,128)(2,1)}), bf16[16,32,1024]{2,1,0:T(8,128)(2,1)S(1)}, u32[]{:S(2)}, u32[]{:S(2)}) async-start(bf16[16,32,1024]{2,1,0:T(8,128)(2,1)} %get-tuple-element.77), calls=%async_computation.1 | async-start | bytes 2097152 | tf_op jit(solution)/shard_map/all_to_all | solution.py:40
  74.9 0.4 collective-permute-start.16
  75.3 0.2 collective-permute-start.17
  75.5 0.3 collective-permute-start.12
  75.8 0.2 collective-permute-start.13
  76.0 0.3 collective-permute-start.10
  76.3 1.4 %collective-permute-done.10 = f32[16,128]{1,0:T(8,128)S(1)} collective-permute-done((f32[16,128]{1,0:T(8,128)S(1)}, f32[16,128]{1,0:T(8,128)S(1)}, u32[]{:S(2)}, u32[]{:S(2)}) %collective-permute-start.10) | collective-permute-done | bytes 8224 | tf_op jit(solution)/shard_map/ppermute | solution.py:28
  77.7 7.0 %collective-permute-start.11 = (f32[2,16,128]{2,1,0:T(8,128)S(1)}, f32[2,16,128]{2,1,0:T(8,128)S(1)}, u32[]{:S(2)}, u32[]{:S(2)}) collective-permute-start(f32[2,16,128]{2,1,0:T(8,128)S(1)} %maximum_select_fusion), channel_id=1, source_target_pairs={{2,4},{6,8},{10,12},{14,16},{18,20},{22,24},{26,28},{30,32},{34,36... | collective-permute-start | bytes 49160 | tf_op jit(solution)/shard_map/ppermute | solution.py:34
  84.7 0.0 collective-permute-done.12.satt_ref
  84.7 0.0 collective-permute-done.13.sdq_ref
  84.7 0.7 copy-done.10
  85.4 2.7 %shard_map.97 = (bf16[128,2048]{1,0:T(8,128)(2,1)}, bf16[128,2048]{1,0:T(8,128)(2,1)}) custom-call(s32[3]{0:T(128)S(1)} %pad_add_fusion.ids_ref, bf16[128,1024]{1,0:T(8,128)(2,1)} %get-tuple-element.81.att_ref, bf16[128,1024]{1,0:T(8,128)(2,1)} %copy-done.10, bf16[128,1024]{1,0:T(8,128)(2,1)} %get-tuple-element.83.dq_ref, ...), custom_call_target="tpu_custom_call" | custom-call | bytes 19800000 | tf_op jit(solution)/shard_map/pallas_call | solution.py:466
  88.1 4.5 %collective-permute-done.11.stat_ref = f32[2,16,128]{2,1,0:T(8,128)S(1)} collective-permute-done((f32[2,16,128]{2,1,0:T(8,128)S(1)}, f32[2,16,128]{2,1,0:T(8,128)S(1)}, u32[]{:S(2)}, u32[]{:S(2)}) %collective-permute-start.11) | collective-permute-done | bytes 16416 | tf_op jit(solution)/shard_map/ppermute | solution.py:34
  92.6 0.0 all-to-all-done.1
  92.6 0.4 shard_map.98
  93.1 0.2 copy-done.11
  93.2 0.0 collective-permute-start.14
  93.2 5.6 %collective-permute-done.14.got_ref = f32[5,2,2048]{2,1,0:T(2,128)S(1)} collective-permute-done((f32[5,2,2048]{2,1,0:T(2,128)S(1)}, f32[5,2,2048]{2,1,0:T(2,128)S(1)}, u32[]{:S(2)}, u32[]{:S(2)}) %collective-permute-start.14) | collective-permute-done | bytes 81952 | tf_op jit(solution)/shard_map/ppermute | solution.py:28
  98.9 1.4 %collective-permute-start.15 = (f32[3,2,2048]{2,1,0:T(2,128)S(1)}, f32[3,2,2048]{2,1,0:T(2,128)S(1)}, u32[]{:S(2)}, u32[]{:S(2)}) collective-permute-start(f32[3,2,2048]{2,1,0:T(2,128)S(1)} %get-tuple-element.95), channel_id=1, source_target_pairs={{0,64},{2,66},{4,68},{6,70},{8,72},{10,74},{12,76},{14,78},{16,80}... | collective-permute-start | bytes 147464 | tf_op jit(solution)/shard_map/ppermute | solution.py:28
  100.3 0.0 collective-permute-done.16.sdk_ref
  100.3 0.8 copy-done.4
  101.1 0.2 copy-done.5
  101.3 5.5 %shard_map.101 = (f32[128,2048]{1,0:T(8,128)S(1)}, f32[128,2048]{1,0:T(8,128)S(1)}) custom-call(s32[3]{0:T(128)S(1)} %pad_add_fusion.ids_ref, f32[3,16]{1,0:T(4,128)S(1)} %copy-done.3, bf16[128,2048]{1,0:T(8,128)(2,1)} %bitcast.20, bf16[128,2048]{1,0:T(8,128)(2,1)} %bitcast.24, bf16[256,2048]{1,0:T(8,128)(2,1)S(1)} %collective-permute-done.9.q_ref.c_ref, ...), custom_call_target="tpu_custom_call" | custom-call | bytes 46200000 | tf_op jit(solution)/shard_map/pallas_call | solution.py:435
  106.8 0.1 collective-permute-start.18
  106.9 4.9 %collective-permute-done.18.got_ref = f32[2,2,2048]{2,1,0:T(2,128)S(1)} collective-permute-done((f32[2,2,2048]{2,1,0:T(2,128)S(1)}, f32[2,2,2048]{2,1,0:T(2,128)S(1)}, u32[]{:S(2)}, u32[]{:S(2)}) %collective-permute-start.18) | collective-permute-done | bytes 32800 | tf_op jit(solution)/shard_map/ppermute | solution.py:28
  111.8 5.7 %collective-permute-start.19 = (f32[1,2,2048]{2,1,0:T(2,128)S(1)}, f32[1,2,2048]{2,1,0:T(2,128)S(1)}, u32[]{:S(2)}, u32[]{:S(2)}) collective-permute-start(f32[1,2,2048]{2,1,0:T(2,128)S(1)} %slice_add_fusion), channel_id=1, source_target_pairs={{0,1},{1,0},{2,3},{3,2},{4,5},{5,4},{6,7},{7,6},{8,9},{9,8},{10,11... | collective-permute-start | bytes 49160 | tf_op jit(solution)/shard_map/ppermute | solution.py:615
  117.4 1.7 %shard_map.102 = (bf16[128,2048]{1,0:T(8,128)(2,1)}, bf16[128,2048]{1,0:T(8,128)(2,1)}) custom-call(f32[16,2048]{1,0:T(8,128)S(1)} %get-tuple-element.90.one_ref, f32[1,2,2048]{2,1,0:T(2,128)S(1)} %get-tuple-element.97.far_ref, f32[2,2,2048]{2,1,0:T(2,128)S(1)} %collective-permute-done.18.got_ref, f32[128,2048]{1,0:T(8,128)S(1)} %get-tuple-element.108.dk_ref, ...), custom_call_target="tpu_custom_call" | custom-call | bytes 6600000 | tf_op jit(solution)/shard_map/pallas_call | solution.py:553
  119.1 0.4 collective-permute-done.19
  119.5 0.1 copy.11
  119.6 0.6 reduce_sum.9
  (30 shorter events, 0.2 us)
Async XLA Ops:
  0.6 1.0 copy-start.1
  1.7 1.0 copy-start.2
  3.2 11.0 %collective-permute-start = (bf16[1,2,2048]{2,1,0:T(2,128)(2,1)S(1)}, bf16[1,2,2048]{2,1,0:T(2,128)(2,1)S(1)}, u32[]{:S(2)}, u32[]{:S(2)}) collective-permute-start(bf16[1,2,2048]{2,1,0:T(2,128)(2,1)S(1)} %get-tuple-element.60), channel_id=1, source_target_pairs={{0,32},{2,34},{4,36},{6,38},{8,40},{10,42},{12,44},{14,46},{16,48}... | collective-permute-start | bytes 24584 | tf_op jit(solution)/shard_map/ppermute | solution.py:28
  9.1 20.9 %collective-permute-start.3 = (bf16[256,2048]{1,0:T(8,128)(2,1)S(1)}, bf16[256,2048]{1,0:T(8,128)(2,1)S(1)}, u32[]{:S(2)}, u32[]{:S(2)}) collective-permute-start(bf16[256,2048]{1,0:T(8,128)(2,1)S(1)} %get-tuple-element.61), channel_id=1, source_target_pairs={{2,4},{6,8},{10,12},{14,16},{18,20},{22,24},{26,28},{30,32},{34,36... | collective-permute-start | bytes 3145736 | tf_op jit(solution)/shard_map/ppermute | solution.py:34
  14.3 3.8 %collective-permute-start.1 = (bf16[2,2,2048]{2,1,0:T(2,128)(2,1)S(1)}, bf16[2,2,2048]{2,1,0:T(2,128)(2,1)S(1)}, u32[]{:S(2)}, u32[]{:S(2)}) collective-permute-start(bf16[2,2,2048]{2,1,0:T(2,128)(2,1)S(1)} %pad_maximum_fusion), channel_id=1, source_target_pairs={{0,64},{2,66},{4,68},{6,70},{8,72},{10,74},{12,76},{14,78},{16,80}... | collective-permute-start | bytes 49160 | tf_op jit(solution)/shard_map/ppermute | solution.py:28
  18.2 5.2 %collective-permute-start.2 = (bf16[4,2,2048]{2,1,0:T(2,128)(2,1)S(1)}, bf16[4,2,2048]{2,1,0:T(2,128)(2,1)S(1)}, u32[]{:S(2)}, u32[]{:S(2)}) collective-permute-start(bf16[4,2,2048]{2,1,0:T(2,128)(2,1)S(1)} %constant_dynamic-update-slice_fusion.a_ref), channel_id=1, source_target_pairs={{0,192},{2,194},{4,196},{6,198},{8,200},{10,202},{12,204},{14,206}... | collective-permute-start | bytes 98312 | tf_op jit(solution)/shard_map/ppermute | solution.py:28
  18.3 6.2 %collective-permute-start.4 = (bf16[128,1024]{1,0:T(8,128)(2,1)S(1)}, bf16[128,1024]{1,0:T(8,128)(2,1)S(1)}, u32[]{:S(2)}, u32[]{:S(2)}) collective-permute-start(bf16[128,1024]{1,0:T(8,128)(2,1)S(1)} %get-tuple-element.62), channel_id=1, source_target_pairs={{0,2},{2,0},{4,6},{6,4},{8,10},{10,8},{12,14},{14,12},{16,18},{18,... | collective-permute-start | bytes 786440 | tf_op jit(solution)/shard_map/ppermute | solution.py:28
  18.4 6.1 %collective-permute-start.5 = (bf16[128,1024]{1,0:T(8,128)(2,1)S(1)}, bf16[128,1024]{1,0:T(8,128)(2,1)S(1)}, u32[]{:S(2)}, u32[]{:S(2)}) collective-permute-start(bf16[128,1024]{1,0:T(8,128)(2,1)S(1)} %get-tuple-element.63), channel_id=1, source_target_pairs={{0,2},{2,0},{4,6},{6,4},{8,10},{10,8},{12,14},{14,12},{16,18},{18,... | collective-permute-start | bytes 786440 | tf_op jit(solution)/shard_map/ppermute | solution.py:28
  18.9 5.6 %collective-permute-start.6 = (bf16[128,1024]{1,0:T(8,128)(2,1)S(1)}, bf16[128,1024]{1,0:T(8,128)(2,1)S(1)}, u32[]{:S(2)}, u32[]{:S(2)}) collective-permute-start(bf16[128,1024]{1,0:T(8,128)(2,1)S(1)} %get-tuple-element.64), channel_id=1, source_target_pairs={{0,2},{2,0},{4,6},{6,4},{8,10},{10,8},{12,14},{14,12},{16,18},{18,... | collective-permute-start | bytes 786440 | tf_op jit(solution)/shard_map/ppermute | solution.py:28
  23.4 1.5 %collective-permute-start.7 = (bf16[128,1024]{1,0:T(8,128)(2,1)S(1)}, bf16[128,1024]{1,0:T(8,128)(2,1)S(1)}, u32[]{:S(2)}, u32[]{:S(2)}) collective-permute-start(bf16[128,1024]{1,0:T(8,128)(2,1)S(1)} %get-tuple-element.65), channel_id=1, source_target_pairs={{0,2},{2,0},{4,6},{6,4},{8,10},{10,8},{12,14},{14,12},{16,18},{18,... | collective-permute-start | bytes 786440 | tf_op jit(solution)/shard_map/ppermute | solution.py:28
  24.5 5.6 %copy-start.6 = (bf16[128,1024]{1,0:T(8,128)(2,1)}, bf16[128,1024]{1,0:T(8,128)(2,1)S(1)}, u32[]{:S(2)}) copy-start(bf16[128,1024]{1,0:T(8,128)(2,1)S(1)} %collective-permute-done.4.sk_ref) | copy-start | bytes 786436
  24.5 5.6 %copy-start.7 = (bf16[128,1024]{1,0:T(8,128)(2,1)}, bf16[128,1024]{1,0:T(8,128)(2,1)S(1)}, u32[]{:S(2)}) copy-start(bf16[128,1024]{1,0:T(8,128)(2,1)S(1)} %collective-permute-done.5.sv_ref) | copy-start | bytes 786436
  24.5 5.6 %copy-start.8 = (bf16[128,1024]{1,0:T(8,128)(2,1)}, bf16[128,1024]{1,0:T(8,128)(2,1)S(1)}, u32[]{:S(2)}) copy-start(bf16[128,1024]{1,0:T(8,128)(2,1)S(1)} %collective-permute-done.6.sq_ref) | copy-start | bytes 786436
  24.9 0.7 copy-start.9
  30.1 4.3 %copy-start = (bf16[256,2048]{1,0:T(8,128)(2,1)}, bf16[256,2048]{1,0:T(8,128)(2,1)S(1)}, u32[]{:S(2)}) copy-start(bf16[256,2048]{1,0:T(8,128)(2,1)S(1)} %collective-permute-done.3.x_ref.xk_ref.xv_ref) | copy-start | bytes 3145732
  30.1 20.2 %all-to-all-start = ((bf16[16,32,1024]{2,1,0:T(8,128)(2,1)}), bf16[16,32,1024]{2,1,0:T(8,128)(2,1)S(1)}, u32[]{:S(2)}, u32[]{:S(2)}) async-start(bf16[16,32,1024]{2,1,0:T(8,128)(2,1)} %shard_map.93), calls=%async_computation | async-start | bytes 2097152 | tf_op jit(solution)/shard_map/all_to_all | solution.py:40
  33.7 22.0 %copy-start.3 = (f32[3,16]{1,0:T(4,128)S(1)}, f32[3,16]{1,0:T(4,128)}, u32[]{:S(2)}) copy-start(f32[3,16]{1,0:T(4,128)} %bias_ref.3) | copy-start | bytes 580
  34.4 2.1 %collective-permute-start.8 = (bf16[256,1024]{1,0:T(8,128)(2,1)S(1)}, bf16[256,1024]{1,0:T(8,128)(2,1)}, u32[]{:S(2)}, u32[]{:S(2)}) collective-permute-start(bf16[256,1024]{1,0:T(8,128)(2,1)S(1)} %shard_map.95), channel_id=1, source_target_pairs={{0,2},{2,0},{4,6},{6,4},{8,10},{10,8},{12,14},{14,12},{16,18},{18,... | collective-permute-start | bytes 1572872 | tf_op jit(solution)/shard_map/ppermute | solution.py:28
  50.3 20.9 %collective-permute-start.9 = (bf16[256,2048]{1,0:T(8,128)(2,1)S(1)}, bf16[256,2048]{1,0:T(8,128)(2,1)S(1)}, u32[]{:S(2)}, u32[]{:S(2)}) collective-permute-start(bf16[256,2048]{1,0:T(8,128)(2,1)S(1)} %get-tuple-element.76), channel_id=1, source_target_pairs={{2,4},{6,8},{10,12},{14,16},{18,20},{22,24},{26,28},{30,32},{34,36... | collective-permute-start | bytes 3145736 | tf_op jit(solution)/shard_map/ppermute | solution.py:34
  71.2 21.4 %all-to-all-start.1 = ((bf16[16,32,1024]{2,1,0:T(8,128)(2,1)}), bf16[16,32,1024]{2,1,0:T(8,128)(2,1)S(1)}, u32[]{:S(2)}, u32[]{:S(2)}) async-start(bf16[16,32,1024]{2,1,0:T(8,128)(2,1)} %get-tuple-element.77), calls=%async_computation.1 | async-start | bytes 2097152 | tf_op jit(solution)/shard_map/all_to_all | solution.py:40
  74.9 1.1 copy-start.13
  74.9 2.8 %copy-start.12 = (f32[16,128]{1,0:T(8,128)S(1)}, f32[16,128]{1,0:T(8,128)}, u32[]{:S(2)}) copy-start(f32[16,128]{1,0:T(8,128)} %get-tuple-element.78) | copy-start | bytes 24580
  74.9 25.4 %collective-permute-start.16 = (f32[128,1024]{1,0:T(8,128)}, f32[128,1024]{1,0:T(8,128)S(1)}, u32[]{:S(2)}, u32[]{:S(2)}) collective-permute-start(f32[128,1024]{1,0:T(8,128)} %get-tuple-element.102), channel_id=1, source_target_pairs={{0,2},{2,0},{4,6},{6,4},{8,10},{10,8},{12,14},{14,12},{16,18},{18,... | collective-permute-start | bytes 1572872 | tf_op jit(solution)/shard_map/ppermute | solution.py:28
  75.3 25.0 %collective-permute-start.17 = (f32[128,1024]{1,0:T(8,128)}, f32[128,1024]{1,0:T(8,128)S(1)}, u32[]{:S(2)}, u32[]{:S(2)}) collective-permute-start(f32[128,1024]{1,0:T(8,128)} %get-tuple-element.104), channel_id=1, source_target_pairs={{0,2},{2,0},{4,6},{6,4},{8,10},{10,8},{12,14},{14,12},{16,18},{18,... | collective-permute-start | bytes 1572872 | tf_op jit(solution)/shard_map/ppermute | solution.py:28
  75.5 9.2 %collective-permute-start.12 = (bf16[128,1024]{1,0:T(8,128)(2,1)}, bf16[128,1024]{1,0:T(8,128)(2,1)S(1)}, u32[]{:S(2)}, u32[]{:S(2)}) collective-permute-start(bf16[128,1024]{1,0:T(8,128)(2,1)} %get-tuple-element.82), channel_id=1, source_target_pairs={{0,2},{2,0},{4,6},{6,4},{8,10},{10,8},{12,14},{14,12},{16,18},{18,... | collective-permute-start | bytes 786440 | tf_op jit(solution)/shard_map/ppermute | solution.py:28
  75.8 8.9 %collective-permute-start.13 = (bf16[128,1024]{1,0:T(8,128)(2,1)}, bf16[128,1024]{1,0:T(8,128)(2,1)}, u32[]{:S(2)}, u32[]{:S(2)}) collective-permute-start(bf16[128,1024]{1,0:T(8,128)(2,1)} %get-tuple-element.84), channel_id=1, source_target_pairs={{0,2},{2,0},{4,6},{6,4},{8,10},{10,8},{12,14},{14,12},{16,18},{18,... | collective-permute-start | bytes 786440 | tf_op jit(solution)/shard_map/ppermute | solution.py:28
  76.0 1.7 %collective-permute-start.10 = (f32[16,128]{1,0:T(8,128)S(1)}, f32[16,128]{1,0:T(8,128)S(1)}, u32[]{:S(2)}, u32[]{:S(2)}) collective-permute-start(f32[16,128]{1,0:T(8,128)S(1)} %copy-done.13), channel_id=1, source_target_pairs={{0,2},{2,0},{4,6},{6,4},{8,10},{10,8},{12,14},{14,12},{16,18},{18,... | collective-permute-start | bytes 24584 | tf_op jit(solution)/shard_map/ppermute | solution.py:28
  77.7 15.0 %collective-permute-start.11 = (f32[2,16,128]{2,1,0:T(8,128)S(1)}, f32[2,16,128]{2,1,0:T(8,128)S(1)}, u32[]{:S(2)}, u32[]{:S(2)}) collective-permute-start(f32[2,16,128]{2,1,0:T(8,128)S(1)} %maximum_select_fusion), channel_id=1, source_target_pairs={{2,4},{6,8},{10,12},{14,16},{18,20},{22,24},{26,28},{30,32},{34,36... | collective-permute-start | bytes 49160 | tf_op jit(solution)/shard_map/ppermute | solution.py:34
  84.7 0.7 copy-start.10
  92.6 0.6 copy-start.11
  93.2 5.7 %collective-permute-start.14 = (f32[5,2,2048]{2,1,0:T(2,128)S(1)}, f32[5,2,2048]{2,1,0:T(2,128)S(1)}, u32[]{:S(2)}, u32[]{:S(2)}) collective-permute-start(f32[5,2,2048]{2,1,0:T(2,128)S(1)} %get-tuple-element.92), channel_id=1, source_target_pairs={{0,192},{2,194},{4,196},{6,198},{8,200},{10,202},{12,204},{14,206}... | collective-permute-start | bytes 245768 | tf_op jit(solution)/shard_map/ppermute | solution.py:28
  98.9 7.9 %collective-permute-start.15 = (f32[3,2,2048]{2,1,0:T(2,128)S(1)}, f32[3,2,2048]{2,1,0:T(2,128)S(1)}, u32[]{:S(2)}, u32[]{:S(2)}) collective-permute-start(f32[3,2,2048]{2,1,0:T(2,128)S(1)} %get-tuple-element.95), channel_id=1, source_target_pairs={{0,64},{2,66},{4,68},{6,70},{8,72},{10,74},{12,76},{14,78},{16,80}... | collective-permute-start | bytes 147464 | tf_op jit(solution)/shard_map/ppermute | solution.py:28
  100.3 0.8 copy-start.4
  100.3 1.0 copy-start.5
  106.8 5.0 %collective-permute-start.18 = (f32[2,2,2048]{2,1,0:T(2,128)S(1)}, f32[2,2,2048]{2,1,0:T(2,128)S(1)}, u32[]{:S(2)}, u32[]{:S(2)}) collective-permute-start(f32[2,2,2048]{2,1,0:T(2,128)S(1)} %get-tuple-element.107), channel_id=1, source_target_pairs={{0,32},{2,34},{4,36},{6,38},{8,40},{10,42},{12,44},{14,46},{16,48}... | collective-permute-start | bytes 98312 | tf_op jit(solution)/shard_map/ppermute | solution.py:28
  111.8 7.7 %collective-permute-start.19 = (f32[1,2,2048]{2,1,0:T(2,128)S(1)}, f32[1,2,2048]{2,1,0:T(2,128)S(1)}, u32[]{:S(2)}, u32[]{:S(2)}) collective-permute-start(f32[1,2,2048]{2,1,0:T(2,128)S(1)} %slice_add_fusion), channel_id=1, source_target_pairs={{0,1},{1,0},{2,3},{3,2},{4,5},{5,4},{6,7},{7,6},{8,9},{9,8},{10,11... | collective-permute-start | bytes 49160 | tf_op jit(solution)/shard_map/ppermute | solution.py:615

commit v4 on v3

--- a/solution.py
+++ b/solution.py
@@ -390,7 +390,7 @@
 
 
 def edge_kernel(
-    per_half,
+    half,
     heads,
     ids_ref,
     bias_ref,
@@ -407,12 +407,12 @@
     out_dv_ref,
 ):
     step = pl.program_id(0)
-    mine = step // per_half == ids_ref[1]
+    mine = half == ids_ref[1]
     scale = HEAD**-0.5
     for j in range(heads):
         cols = slice(j * HEAD, (j + 1) * HEAD)
-        bias = bias_ref[0, step * heads + j] * LOG2E
-        row = lax.rem(step, per_half) * heads + j
+        bias = bias_ref[0, half * 8 + step * heads + j] * LOG2E
+        row = step * heads + j
         log_total = stat_ref[0, pl.ds(row, 1)]
         delta = stat_ref[0, pl.ds(row + 8, 1)]
         q, c = q_ref[:, cols], c_ref[:, cols]
@@ -425,32 +425,32 @@
         out_dv_ref[:, cols] = dv + nn(weights.astype(BF), c)
 
 
-def edge(ids, bias, k, v, x, stat, parts):
+def edge(half, ids, bias, k, v, x, stat, parts):
     rows, width = k.shape
-    heads = 8
+    heads = 4
     block = heads * HEAD
     per_half = width // 2 // block
-    whole = pl.BlockSpec((rows, block), lambda i, ids: (0, i))
-    part = pl.BlockSpec((rows, block), lambda i, ids: (0, lax.rem(i, per_half)))
-    return pl.pallas_call(
-        functools.partial(edge_kernel, per_half, heads),
+    whole = pl.BlockSpec((rows, block), lambda i, ids: (0, half * per_half + i))
+    part = pl.BlockSpec((rows, block), lambda i, ids: (0, i))
+    return pl.pallas_call(
+        functools.partial(edge_kernel, half, heads),
         grid_spec=pltpu.PrefetchScalarGridSpec(
             num_scalar_prefetch=1,
-            grid=(2 * per_half,),
+            grid=(per_half,),
             in_specs=[
                 pl.BlockSpec(memory_space=pltpu.SMEM),
                 whole,
                 whole,
-                pl.BlockSpec((rows, block), lambda i, ids: (0, i)),
-                pl.BlockSpec((rows, block), lambda i, ids: (1, i)),
-                pl.BlockSpec((1, 16, rows), lambda i, ids: (i // per_half, 0, 0)),
+                whole,
+                pl.BlockSpec((rows, block), lambda i, ids: (1, half * per_half + i)),
+                pl.BlockSpec((1, 16, rows), lambda i, ids: (half, 0, 0)),
             ]
             + [part] * 4,
-            out_specs=[whole] * 2,
+            out_specs=[part] * 2,
         ),
-        out_shape=[jax.ShapeDtypeStruct((rows, width), F32)] * 2,
-        compiler_params=params(),
-        cost_estimate=cost(14),
+        out_shape=[jax.ShapeDtypeStruct((rows, width // 2), F32)] * 2,
+        compiler_params=params(),
+        cost_estimate=cost(5),
     )(ids, bias, *in_hbm(k, v), x, x, *in_hbm(stat, *parts))
 
 
@@ -536,35 +536,40 @@
     )(low, got, level)
 
 
-def final_kernel(one_ref, far_ref, got_ref, dk_ref, dv_ref, out_dk_ref, out_dv_ref):
+def final_kernel(
+    one_ref, far_ref, got_ref, dk_ref, dv_ref, dk2_ref, dv2_ref, out_dk_ref, out_dv_ref
+):
+    lower = pl.program_id(0) < pl.num_programs(0) // 2
     total = one_ref[...] / POOL1
-    for n, (ref, out) in enumerate(((dk_ref, out_dk_ref), (dv_ref, out_dv_ref))):
+    triples = (dk_ref, dk2_ref, out_dk_ref), (dv_ref, dv2_ref, out_dv_ref)
+    for n, (ref, ref2, out) in enumerate(triples):
         far = far_ref[0, n : n + 1, :] + got_ref[0, n : n + 1, :]
         rows = total[8 * n : 8 * n + 8] + far / POOL2
         for r in range(8):
             at = slice(r * POOL1, (r + 1) * POOL1)
-            out[at] = (ref[at] + rows[r : r + 1]).astype(BF)
-
-
-def final(one, far, got, dk, dv):
-    rows, width = dk.shape
+            near = jnp.where(lower, ref[at], ref2[at])
+            out[at] = (near + rows[r : r + 1]).astype(BF)
+
+
+def final(one, far, got, *nears):
+    rows, width = nears[0].shape[0], one.shape[1]
     block = 512
+    steps = width // block
     whole = pl.BlockSpec((rows, block), lambda i: (0, i))
     return pl.pallas_call(
         final_kernel,
-        grid=(width // block,),
+        grid=(steps,),
         in_specs=[
             pl.BlockSpec((16, block), lambda i: (0, i)),
             pl.BlockSpec((1, 2, block), lambda i: (0, 0, i)),
             pl.BlockSpec((2, 2, block), lambda i: (0, 0, i)),
-            whole,
-            whole,
-        ],
+        ]
+        + [pl.BlockSpec((rows, block), lambda i: (0, lax.rem(i, steps // 2)))] * 4,
         out_specs=[whole] * 2,
         out_shape=[jax.ShapeDtypeStruct((rows, width), BF)] * 2,
         compiler_params=params(),
         cost_estimate=cost(2),
-    )(one, far, got, dk, dv)
+    )(one, far, got, *nears)
 
 
 def body(queries, key_rows, values, cotangent, level_bias):
@@ -603,14 +608,18 @@
     ratt, rdq, rdk, rdv = [swap(s, SIB) for s in (satt, sdq, sdk, sdv)]
     att, dq = join(ids, att, ratt, dq, rdq)
     grads, att, dq = lax.optimization_barrier((grads, att, dq))
-    dk, dv = edge(ids, level_bias, k, v, x_qc, x_stats, (dk, rdk, dv, rdv))
+    first, second = [
+        edge(half, ids, level_bias, k, v, x_qc, x_stats, (dk, rdk, dv, rdv))
+        for half in range(2)
+    ]
 
     one, low, high, level = sums(grads)
     low, high, level = step(low, swap(high, YB), level)
+    high, first = lax.optimization_barrier((high, first))
     low, high, level = step(low, swap(high, YA), level)
-    high, dk, dv = lax.optimization_barrier((high, dk, dv))
+    high, second = lax.optimization_barrier((high, second))
     got = swap(high, Z1)
-    dk, dv = final(one, low, got, dk, dv)
+    dk, dv = final(one, low, got, *first, *second)
     level = level + got[1:]
     level = level + lax.ppermute(level, "batch", [(0, 1), (1, 0)])
     level = level[0, 0].reshape(heads, HEAD)[:, :9].reshape(heads, 3, 3).sum(1).T

time: 121 us -> 119 us (0.983)
  waiting for transfers between devices: 51.1 us -> 44.9 us
  Pallas kernels: 24.2 us -> 26.4 us
  starting transfers between devices: 38.4 us -> 40 us
    ppermute x16, waiting for transfers between devices: 21.8 us -> 15.7 us  [swap(): lax.ppermute(x, 'seq', [(i, i ^ mask) for i in range(lax.axis_size('seq'))])]
    pallas_call x2 -> x3, Pallas kernels: 7.18 us -> 9.31 us  [the longest x2 7.44 us: edge(): pl.pallas_call(functools.partial(edge_kernel, half, heads), grid_spec=plt...]
    ppermute x16, starting transfers between devices: 7.89 us -> 9.49 us  [swap(): lax.ppermute(x, 'seq', [(i, i ^ mask) for i in range(lax.axis_size('seq'))])]
  transfers between devices with their start and end apart: 22 -> 22, of which waited for: 12 -> 12; matrix products, arithmetic and copies ran while one was open for 0% -> 0% of each run, Pallas kernels for 20% -> 22%
where the time goes in v4:
time: 119 us; the launch traced here: 118 us
  waiting for transfers between devices  44.9 us (38%)
  starting transfers between devices  40 us (34%)
  Pallas kernels  26.4 us (22%)
  local copies, waits for them, and re-layouts  4.78 us (4%)
    ppermute x3, starting transfers between devices, cross(): return lax.ppermute(x, 'seq', pairs + [(j, i) for i, j in pairs])  17.6 us
    ppermute x16, waiting for transfers between devices, swap(): lax.ppermute(x, 'seq', [(i, i ^ mask) for i in range(lax.axis_size('seq'))])  15.7 us
    ppermute x3, waiting for transfers between devices, cross(): return lax.ppermute(x, 'seq', pairs + [(j, i) for i, j in pairs])  15.1 us
    all_to_all x2, waiting for transfers between devices, in_group(): return lax.all_to_all(x, 'seq', 0, 0, axis_index_groups=groups)  13.8 us
    ppermute x16, starting transfers between devices, swap(): lax.ppermute(x, 'seq', [(i, i ^ mask) for i in range(lax.axis_size('seq'))])  9.49 us
    pallas_call x1, Pallas kernels, attend(): pl.pallas_call(functools.partial(attend_kernel, steps, heads), grid_spec=...  9.26 us
    pallas_call x2, Pallas kernels, edge(): pl.pallas_call(functools.partial(edge_kernel, half, heads), grid_spec=plt...  7.44 us
    all_to_all x2, starting transfers between devices, in_group(): return lax.all_to_all(x, 'seq', 0, 0, axis_index_groups=groups)  7.32 us
  transfers between devices with their start and end apart: 22, of which 12 were waited for; matrix products, arithmetic and copies ran while one was open for 0% of the time, Pallas kernels for 22%

profile of v4, /device:TPU:24, one launch (start us, length us, event | category | flops | bytes accessed | tf_op | source)
XLA Modules:
  0.0 117.8 jit_solution(6022110689399382450)
XLA Ops:
  0.6 0.0 copy-start
  0.6 1.0 copy-done
  1.7 1.0 copy-done.1
  2.7 0.5 shard_map.92
  3.2 3.4 %collective-permute-start = (bf16[1,2,2048]{2,1,0:T(2,128)(2,1)S(1)}, bf16[1,2,2048]{2,1,0:T(2,128)(2,1)S(1)}, u32[]{:S(2)}, u32[]{:S(2)}) collective-permute-start(bf16[1,2,2048]{2,1,0:T(2,128)(2,1)S(1)} %get-tuple-element.65), channel_id=1, source_target_pairs={{0,32},{2,34},{4,36},{6,38},{8,40},{10,42},{12,44},{14,46},{16,48}... | collective-permute-start | bytes 24584 | tf_op jit(solution)/shard_map/ppermute | solution.py:28
  6.6 0.1 pad_add_fusion.ids_ref
  6.7 2.4 %shard_map.94 = (bf16[256,2048]{1,0:T(8,128)(2,1)S(1)}, bf16[256,2048]{1,0:T(8,128)(2,1)S(1)}, bf16[128,1024]{1,0:T(8,128)(2,1)S(1)}, bf16[128,1024]{1,0:T(8,128...) custom-call(s32[3]{0:T(128)S(1)} %pad_add_fusion.ids_ref, bf16[128,2048]{1,0:T(8,128)(2,1)} %bitcast.18, ...), custom_call_target="tpu_custom_call" | custom-call | bytes 3300000 | tf_op jit(solution)/shard_map/pallas_call | solution.py:142
  9.1 5.1 %collective-permute-start.3 = (bf16[256,2048]{1,0:T(8,128)(2,1)S(1)}, bf16[256,2048]{1,0:T(8,128)(2,1)S(1)}, u32[]{:S(2)}, u32[]{:S(2)}) collective-permute-start(bf16[256,2048]{1,0:T(8,128)(2,1)S(1)} %get-tuple-element.66), channel_id=1, source_target_pairs={{2,4},{6,8},{10,12},{14,16},{18,20},{22,24},{26,28},{30,32},{34,36... | collective-permute-start | bytes 3145736 | tf_op jit(solution)/shard_map/ppermute | solution.py:34
  14.3 0.0 collective-permute-done
  14.3 0.5 collective-permute-start.1
  14.9 3.3 %collective-permute-done.1 = bf16[2,2,2048]{2,1,0:T(2,128)(2,1)S(1)} collective-permute-done((bf16[2,2,2048]{2,1,0:T(2,128)(2,1)S(1)}, bf16[2,2,2048]{2,1,0:T(2,128)(2,1)S(1)}, u32[]{:S(2)}, u32[]{:S(2)}) %collective-permute-start.1) | collective-permute-done | bytes 16416 | tf_op jit(solution)/shard_map/ppermute | solution.py:28
  18.2 0.1 collective-permute-start.2
  18.3 0.1 collective-permute-start.4
  18.4 0.5 collective-permute-start.5
  18.9 0.1 collective-permute-start.6
  19.0 4.4 %collective-permute-done.2.b_ref = bf16[4,2,2048]{2,1,0:T(2,128)(2,1)S(1)} collective-permute-done((bf16[4,2,2048]{2,1,0:T(2,128)(2,1)S(1)}, bf16[4,2,2048]{2,1,0:T(2,128)(2,1)S(1)}, u32[]{:S(2)}, u32[]{:S(2)}) %collective-permute-start.2) | collective-permute-done | bytes 32800 | tf_op jit(solution)/shard_map/ppermute | solution.py:28
  23.4 0.0 collective-permute-start.7
  23.4 1.1 shard_map.93
  24.5 0.0 collective-permute-done.4.sk_ref
  24.5 0.0 collective-permute-done.5.sv_ref
  24.5 0.0 collective-permute-done.6.sq_ref
  24.5 0.0 copy-start.8
  24.5 0.4 collective-permute-done.7.sc_ref
  24.9 0.7 copy-done.9
  25.6 4.4 %collective-permute-done.3.x_ref.xk_ref.xv_ref = bf16[256,2048]{1,0:T(8,128)(2,1)S(1)} collective-permute-done((bf16[256,2048]{1,0:T(8,128)(2,1)S(1)}, bf16[256,2048]{1,0:T(8,128)(2,1)S(1)}, u32[]{:S(2)}, u32[]{:S(2)}) %collective-permute-start.3) | collective-permute-done | bytes 1048608 | tf_op jit(solution)/shard_map/ppermute | solution.py:34
  30.1 3.7 %all-to-all-start = ((bf16[16,32,1024]{2,1,0:T(8,128)(2,1)}), bf16[16,32,1024]{2,1,0:T(8,128)(2,1)S(1)}, u32[]{:S(2)}, u32[]{:S(2)}) async-start(bf16[16,32,1024]{2,1,0:T(8,128)(2,1)} %shard_map.93), calls=%async_computation | async-start | bytes 2097152 | tf_op jit(solution)/shard_map/all_to_all | solution.py:40
  33.7 0.0 copy-start.3
  33.7 0.6 shard_map.95
  34.4 0.4 collective-permute-start.8
  34.7 1.8 %collective-permute-done.8.sxk_ref.sxv_ref = bf16[256,1024]{1,0:T(8,128)(2,1)} collective-permute-done((bf16[256,1024]{1,0:T(8,128)(2,1)S(1)}, bf16[256,1024]{1,0:T(8,128)(2,1)}, u32[]{:S(2)}, u32[]{:S(2)}) %collective-permute-start.8) | collective-permute-done | bytes 524320 | tf_op jit(solution)/shard_map/ppermute | solution.py:28
  36.5 13.8 %all-to-all-done.level_ref = bf16[16,32,1024]{2,1,0:T(8,128)(2,1)S(1)} async-done(((bf16[16,32,1024]{2,1,0:T(8,128)(2,1)}), bf16[16,32,1024]{2,1,0:T(8,128)(2,1)S(1)}, u32[]{:S(2)}, u32[]{:S(2)}) %all-to-all-start) | async-done | bytes 1048608 | tf_op jit(solution)/shard_map/all_to_all | solution.py:40
  50.3 5.5 %collective-permute-start.9 = (bf16[256,2048]{1,0:T(8,128)(2,1)S(1)}, bf16[256,2048]{1,0:T(8,128)(2,1)S(1)}, u32[]{:S(2)}, u32[]{:S(2)}) collective-permute-start(bf16[256,2048]{1,0:T(8,128)(2,1)S(1)} %get-tuple-element.81), channel_id=1, source_target_pairs={{2,4},{6,8},{10,12},{14,16},{18,20},{22,24},{26,28},{30,32},{34,36... | collective-permute-start | bytes 3145736 | tf_op jit(solution)/shard_map/ppermute | solution.py:34
  55.8 9.3 %shard_map.96 = (bf16[128,1024]{1,0:T(8,128)(2,1)}, bf16[128,1024]{1,0:T(8,128)(2,1)}, bf16[128,1024]{1,0:T(8,128)(2,1)}, bf16[128,1024]{1,0:T(8,128)(2,1)}, f32...) custom-call(s32[3]{0:T(128)S(1)} %pad_add_fusion.ids_ref, ...), custom_call_target="tpu_custom_call" | custom-call | bytes 29700000 | tf_op jit(solution)/shard_map/pallas_call | solution.py:365
  65.1 6.2 %collective-permute-done.9.q_ref.c_ref = bf16[256,2048]{1,0:T(8,128)(2,1)S(1)} collective-permute-done((bf16[256,2048]{1,0:T(8,128)(2,1)S(1)}, bf16[256,2048]{1,0:T(8,128)(2,1)S(1)}, u32[]{:S(2)}, u32[]{:S(2)}) %collective-permute-start.9) | collective-permute-done | bytes 1048608 | tf_op jit(solution)/shard_map/ppermute | solution.py:34
  71.2 3.7 %all-to-all-start.1 = ((bf16[16,32,1024]{2,1,0:T(8,128)(2,1)}), bf16[16,32,1024]{2,1,0:T(8,128)(2,1)S(1)}, u32[]{:S(2)}, u32[]{:S(2)}) async-start(bf16[16,32,1024]{2,1,0:T(8,128)(2,1)} %get-tuple-element.82), calls=%async_computation.1 | async-start | bytes 2097152 | tf_op jit(solution)/shard_map/all_to_all | solution.py:40
  74.9 0.4 collective-permute-start.15
  75.3 0.2 collective-permute-start.16
  75.5 0.3 collective-permute-start.12
  75.8 0.2 collective-permute-start.13
  76.0 0.3 collective-permute-start.10
  76.3 1.4 %collective-permute-done.10 = f32[16,128]{1,0:T(8,128)S(1)} collective-permute-done((f32[16,128]{1,0:T(8,128)S(1)}, f32[16,128]{1,0:T(8,128)S(1)}, u32[]{:S(2)}, u32[]{:S(2)}) %collective-permute-start.10) | collective-permute-done | bytes 8224 | tf_op jit(solution)/shard_map/ppermute | solution.py:28
  77.7 7.0 %collective-permute-start.11 = (f32[2,16,128]{2,1,0:T(8,128)S(1)}, f32[2,16,128]{2,1,0:T(8,128)S(1)}, u32[]{:S(2)}, u32[]{:S(2)}) collective-permute-start(f32[2,16,128]{2,1,0:T(8,128)S(1)} %maximum_select_fusion), channel_id=1, source_target_pairs={{2,4},{6,8},{10,12},{14,16},{18,20},{22,24},{26,28},{30,32},{34,36... | collective-permute-start | bytes 49160 | tf_op jit(solution)/shard_map/ppermute | solution.py:34
  84.7 0.0 collective-permute-done.12.satt_ref
  84.7 0.0 collective-permute-done.13.sdq_ref
  84.7 0.7 copy-done.10
  85.4 2.7 %shard_map.97 = (bf16[128,2048]{1,0:T(8,128)(2,1)}, bf16[128,2048]{1,0:T(8,128)(2,1)}) custom-call(s32[3]{0:T(128)S(1)} %pad_add_fusion.ids_ref, bf16[128,1024]{1,0:T(8,128)(2,1)} %get-tuple-element.86.att_ref, bf16[128,1024]{1,0:T(8,128)(2,1)} %copy-done.10, bf16[128,1024]{1,0:T(8,128)(2,1)} %get-tuple-element.88.dq_ref, ...), custom_call_target="tpu_custom_call" | custom-call | bytes 19800000 | tf_op jit(solution)/shard_map/pallas_call | solution.py:466
  88.1 4.5 %collective-permute-done.11.stat_ref = f32[2,16,128]{2,1,0:T(8,128)S(1)} collective-permute-done((f32[2,16,128]{2,1,0:T(8,128)S(1)}, f32[2,16,128]{2,1,0:T(8,128)S(1)}, u32[]{:S(2)}, u32[]{:S(2)}) %collective-permute-start.11) | collective-permute-done | bytes 16416 | tf_op jit(solution)/shard_map/ppermute | solution.py:34
  92.7 0.0 all-to-all-done.1
  92.7 0.4 shard_map.98
  93.1 0.2 copy-done.11
  93.3 0.8 copy-done.4
  94.1 0.2 copy-done.5
  94.3 3.7 %shard_map.100 = (f32[128,1024]{1,0:T(8,128)S(1)}, f32[128,1024]{1,0:T(8,128)S(1)}) custom-call(s32[3]{0:T(128)S(1)} %pad_add_fusion.ids_ref, f32[3,16]{1,0:T(4,128)S(1)} %copy-done.3, bf16[128,2048]{1,0:T(8,128)(2,1)} %bitcast.20, bf16[128,2048]{1,0:T(8,128)(2,1)} %bitcast.25, bf16[256,2048]{1,0:T(8,128)(2,1)S(1)} %collective-permute-done.9.q_ref.c_ref, ...), custom_call_target="tpu_custom_call" | custom-call | bytes 16500000 | tf_op jit(solution)/shard_map/pallas_call | solution.py:435
  98.0 0.9 collective-permute-done.14.got_ref
  98.9 1.6 %collective-permute-start.17 = (f32[3,2,2048]{2,1,0:T(2,128)S(1)}, f32[3,2,2048]{2,1,0:T(2,128)S(1)}, u32[]{:S(2)}, u32[]{:S(2)}) collective-permute-start(f32[3,2,2048]{2,1,0:T(2,128)S(1)} %get-tuple-element.109), channel_id=1, source_target_pairs={{0,64},{2,66},{4,68},{6,70},{8,72},{10,74},{12,76},{14,78},{16,80}... | collective-permute-start | bytes 147464 | tf_op jit(solution)/shard_map/ppermute | solution.py:28
  100.5 3.7 %shard_map.102 = (f32[128,1024]{1,0:T(8,128)S(1)}, f32[128,1024]{1,0:T(8,128)S(1)}) custom-call(s32[3]{0:T(128)S(1)} %pad_add_fusion.ids_ref, f32[3,16]{1,0:T(4,128)S(1)} %copy-done.3, bf16[128,2048]{1,0:T(8,128)(2,1)} %bitcast.21, bf16[128,2048]{1,0:T(8,128)(2,1)} %bitcast.26, bf16[256,2048]{1,0:T(8,128)(2,1)S(1)} %collective-permute-done.9.q_ref.c_ref, ...), custom_call_target="tpu_custom_call" | custom-call | bytes 16500000 | tf_op jit(solution)/shard_map/pallas_call | solution.py:435
  104.3 0.0 collective-permute-done.17.got_ref
  104.3 1.4 %collective-permute-start.18 = (f32[2,2,2048]{2,1,0:T(2,128)S(1)}, f32[2,2,2048]{2,1,0:T(2,128)S(1)}, u32[]{:S(2)}, u32[]{:S(2)}) collective-permute-start(f32[2,2,2048]{2,1,0:T(2,128)S(1)} %get-tuple-element.115), channel_id=1, source_target_pairs={{0,32},{2,34},{4,36},{6,38},{8,40},{10,42},{12,44},{14,46},{16,48}... | collective-permute-start | bytes 98312 | tf_op jit(solution)/shard_map/ppermute | solution.py:28
  105.7 3.6 %collective-permute-done.18.got_ref = f32[2,2,2048]{2,1,0:T(2,128)S(1)} collective-permute-done((f32[2,2,2048]{2,1,0:T(2,128)S(1)}, f32[2,2,2048]{2,1,0:T(2,128)S(1)}, u32[]{:S(2)}, u32[]{:S(2)}) %collective-permute-start.18) | collective-permute-done | bytes 32800 | tf_op jit(solution)/shard_map/ppermute | solution.py:28
  109.3 5.6 %collective-permute-start.19 = (f32[1,2,2048]{2,1,0:T(2,128)S(1)}, f32[1,2,2048]{2,1,0:T(2,128)S(1)}, u32[]{:S(2)}, u32[]{:S(2)}) collective-permute-start(f32[1,2,2048]{2,1,0:T(2,128)S(1)} %slice_add_fusion), channel_id=1, source_target_pairs={{0,1},{1,0},{2,3},{3,2},{4,5},{5,4},{6,7},{7,6},{8,9},{9,8},{10,11... | collective-permute-start | bytes 49160 | tf_op jit(solution)/shard_map/ppermute | solution.py:624
  115.0 1.9 %shard_map.103 = (bf16[128,2048]{1,0:T(8,128)(2,1)}, bf16[128,2048]{1,0:T(8,128)(2,1)}) custom-call(f32[16,2048]{1,0:T(8,128)S(1)} %get-tuple-element.95.one_ref, f32[1,2,2048]{2,1,0:T(2,128)S(1)} %get-tuple-element.111.far_ref, f32[2,2,2048]{2,1,0:T(2,128)S(1)} %collective-permute-done.18.got_ref, f32[128,1024]{1,0:T(8,128)S(1)} %get-tuple-element.116.dk_ref, ...), custom_call_target="tpu_custom_call" | custom-call | bytes 6600000 | tf_op jit(solution)/shard_map/pallas_call | solution.py:559
  116.8 0.2 collective-permute-done.19
  117.1 0.1 copy.11
  117.2 0.6 reduce_sum.9
  (31 shorter events, 0.2 us)
Async XLA Ops:
  0.6 1.0 copy-start
  1.7 1.0 copy-start.1
  3.2 11.0 %collective-permute-start = (bf16[1,2,2048]{2,1,0:T(2,128)(2,1)S(1)}, bf16[1,2,2048]{2,1,0:T(2,128)(2,1)S(1)}, u32[]{:S(2)}, u32[]{:S(2)}) collective-permute-start(bf16[1,2,2048]{2,1,0:T(2,128)(2,1)S(1)} %get-tuple-element.65), channel_id=1, source_target_pairs={{0,32},{2,34},{4,36},{6,38},{8,40},{10,42},{12,44},{14,46},{16,48}... | collective-permute-start | bytes 24584 | tf_op jit(solution)/shard_map/ppermute | solution.py:28
  9.1 20.9 %collective-permute-start.3 = (bf16[256,2048]{1,0:T(8,128)(2,1)S(1)}, bf16[256,2048]{1,0:T(8,128)(2,1)S(1)}, u32[]{:S(2)}, u32[]{:S(2)}) collective-permute-start(bf16[256,2048]{1,0:T(8,128)(2,1)S(1)} %get-tuple-element.66), channel_id=1, source_target_pairs={{2,4},{6,8},{10,12},{14,16},{18,20},{22,24},{26,28},{30,32},{34,36... | collective-permute-start | bytes 3145736 | tf_op jit(solution)/shard_map/ppermute | solution.py:34
  14.3 3.8 %collective-permute-start.1 = (bf16[2,2,2048]{2,1,0:T(2,128)(2,1)S(1)}, bf16[2,2,2048]{2,1,0:T(2,128)(2,1)S(1)}, u32[]{:S(2)}, u32[]{:S(2)}) collective-permute-start(bf16[2,2,2048]{2,1,0:T(2,128)(2,1)S(1)} %pad_maximum_fusion), channel_id=1, source_target_pairs={{0,64},{2,66},{4,68},{6,70},{8,72},{10,74},{12,76},{14,78},{16,80}... | collective-permute-start | bytes 49160 | tf_op jit(solution)/shard_map/ppermute | solution.py:28
  18.2 5.2 %collective-permute-start.2 = (bf16[4,2,2048]{2,1,0:T(2,128)(2,1)S(1)}, bf16[4,2,2048]{2,1,0:T(2,128)(2,1)S(1)}, u32[]{:S(2)}, u32[]{:S(2)}) collective-permute-start(bf16[4,2,2048]{2,1,0:T(2,128)(2,1)S(1)} %constant_dynamic-update-slice_fusion.a_ref), channel_id=1, source_target_pairs={{0,192},{2,194},{4,196},{6,198},{8,200},{10,202},{12,204},{14,206}... | collective-permute-start | bytes 98312 | tf_op jit(solution)/shard_map/ppermute | solution.py:28
  18.3 6.2 %collective-permute-start.4 = (bf16[128,1024]{1,0:T(8,128)(2,1)S(1)}, bf16[128,1024]{1,0:T(8,128)(2,1)S(1)}, u32[]{:S(2)}, u32[]{:S(2)}) collective-permute-start(bf16[128,1024]{1,0:T(8,128)(2,1)S(1)} %get-tuple-element.67), channel_id=1, source_target_pairs={{0,2},{2,0},{4,6},{6,4},{8,10},{10,8},{12,14},{14,12},{16,18},{18,... | collective-permute-start | bytes 786440 | tf_op jit(solution)/shard_map/ppermute | solution.py:28
  18.4 6.1 %collective-permute-start.5 = (bf16[128,1024]{1,0:T(8,128)(2,1)S(1)}, bf16[128,1024]{1,0:T(8,128)(2,1)S(1)}, u32[]{:S(2)}, u32[]{:S(2)}) collective-permute-start(bf16[128,1024]{1,0:T(8,128)(2,1)S(1)} %get-tuple-element.68), channel_id=1, source_target_pairs={{0,2},{2,0},{4,6},{6,4},{8,10},{10,8},{12,14},{14,12},{16,18},{18,... | collective-permute-start | bytes 786440 | tf_op jit(solution)/shard_map/ppermute | solution.py:28
  18.9 5.6 %collective-permute-start.6 = (bf16[128,1024]{1,0:T(8,128)(2,1)S(1)}, bf16[128,1024]{1,0:T(8,128)(2,1)S(1)}, u32[]{:S(2)}, u32[]{:S(2)}) collective-permute-start(bf16[128,1024]{1,0:T(8,128)(2,1)S(1)} %get-tuple-element.69), channel_id=1, source_target_pairs={{0,2},{2,0},{4,6},{6,4},{8,10},{10,8},{12,14},{14,12},{16,18},{18,... | collective-permute-start | bytes 786440 | tf_op jit(solution)/shard_map/ppermute | solution.py:28
  23.4 1.5 %collective-permute-start.7 = (bf16[128,1024]{1,0:T(8,128)(2,1)S(1)}, bf16[128,1024]{1,0:T(8,128)(2,1)S(1)}, u32[]{:S(2)}, u32[]{:S(2)}) collective-permute-start(bf16[128,1024]{1,0:T(8,128)(2,1)S(1)} %get-tuple-element.70), channel_id=1, source_target_pairs={{0,2},{2,0},{4,6},{6,4},{8,10},{10,8},{12,14},{14,12},{16,18},{18,... | collective-permute-start | bytes 786440 | tf_op jit(solution)/shard_map/ppermute | solution.py:28
  24.5 5.6 %copy-start.6 = (bf16[128,1024]{1,0:T(8,128)(2,1)}, bf16[128,1024]{1,0:T(8,128)(2,1)S(1)}, u32[]{:S(2)}) copy-start(bf16[128,1024]{1,0:T(8,128)(2,1)S(1)} %collective-permute-done.4.sk_ref) | copy-start | bytes 786436
  24.5 5.6 %copy-start.7 = (bf16[128,1024]{1,0:T(8,128)(2,1)}, bf16[128,1024]{1,0:T(8,128)(2,1)S(1)}, u32[]{:S(2)}) copy-start(bf16[128,1024]{1,0:T(8,128)(2,1)S(1)} %collective-permute-done.5.sv_ref) | copy-start | bytes 786436
  24.5 5.5 %copy-start.8 = (bf16[128,1024]{1,0:T(8,128)(2,1)}, bf16[128,1024]{1,0:T(8,128)(2,1)S(1)}, u32[]{:S(2)}) copy-start(bf16[128,1024]{1,0:T(8,128)(2,1)S(1)} %collective-permute-done.6.sq_ref) | copy-start | bytes 786436
  24.9 0.7 copy-start.9
  30.1 4.3 %copy-start.2 = (bf16[256,2048]{1,0:T(8,128)(2,1)}, bf16[256,2048]{1,0:T(8,128)(2,1)S(1)}, u32[]{:S(2)}) copy-start(bf16[256,2048]{1,0:T(8,128)(2,1)S(1)} %collective-permute-done.3.x_ref.xk_ref.xv_ref) | copy-start | bytes 3145732
  30.1 20.2 %all-to-all-start = ((bf16[16,32,1024]{2,1,0:T(8,128)(2,1)}), bf16[16,32,1024]{2,1,0:T(8,128)(2,1)S(1)}, u32[]{:S(2)}, u32[]{:S(2)}) async-start(bf16[16,32,1024]{2,1,0:T(8,128)(2,1)} %shard_map.93), calls=%async_computation | async-start | bytes 2097152 | tf_op jit(solution)/shard_map/all_to_all | solution.py:40
  33.7 22.0 %copy-start.3 = (f32[3,16]{1,0:T(4,128)S(1)}, f32[3,16]{1,0:T(4,128)}, u32[]{:S(2)}) copy-start(f32[3,16]{1,0:T(4,128)} %bias_ref.5) | copy-start | bytes 580
  34.4 2.1 %collective-permute-start.8 = (bf16[256,1024]{1,0:T(8,128)(2,1)S(1)}, bf16[256,1024]{1,0:T(8,128)(2,1)}, u32[]{:S(2)}, u32[]{:S(2)}) collective-permute-start(bf16[256,1024]{1,0:T(8,128)(2,1)S(1)} %shard_map.95), channel_id=1, source_target_pairs={{0,2},{2,0},{4,6},{6,4},{8,10},{10,8},{12,14},{14,12},{16,18},{18,... | collective-permute-start | bytes 1572872 | tf_op jit(solution)/shard_map/ppermute | solution.py:28
  50.3 20.9 %collective-permute-start.9 = (bf16[256,2048]{1,0:T(8,128)(2,1)S(1)}, bf16[256,2048]{1,0:T(8,128)(2,1)S(1)}, u32[]{:S(2)}, u32[]{:S(2)}) collective-permute-start(bf16[256,2048]{1,0:T(8,128)(2,1)S(1)} %get-tuple-element.81), channel_id=1, source_target_pairs={{2,4},{6,8},{10,12},{14,16},{18,20},{22,24},{26,28},{30,32},{34,36... | collective-permute-start | bytes 3145736 | tf_op jit(solution)/shard_map/ppermute | solution.py:34
  71.2 21.4 %all-to-all-start.1 = ((bf16[16,32,1024]{2,1,0:T(8,128)(2,1)}), bf16[16,32,1024]{2,1,0:T(8,128)(2,1)S(1)}, u32[]{:S(2)}, u32[]{:S(2)}) async-start(bf16[16,32,1024]{2,1,0:T(8,128)(2,1)} %get-tuple-element.82), calls=%async_computation.1 | async-start | bytes 2097152 | tf_op jit(solution)/shard_map/all_to_all | solution.py:40
  74.9 1.1 copy-start.13
  74.9 2.8 %copy-start.12 = (f32[16,128]{1,0:T(8,128)S(1)}, f32[16,128]{1,0:T(8,128)}, u32[]{:S(2)}) copy-start(f32[16,128]{1,0:T(8,128)} %get-tuple-element.83) | copy-start | bytes 24580
  74.9 18.4 %collective-permute-start.15 = (f32[128,1024]{1,0:T(8,128)}, f32[128,1024]{1,0:T(8,128)S(1)}, u32[]{:S(2)}, u32[]{:S(2)}) collective-permute-start(f32[128,1024]{1,0:T(8,128)} %get-tuple-element.104), channel_id=1, source_target_pairs={{0,2},{2,0},{4,6},{6,4},{8,10},{10,8},{12,14},{14,12},{16,18},{18,... | collective-permute-start | bytes 1572872 | tf_op jit(solution)/shard_map/ppermute | solution.py:28
  75.3 18.0 %collective-permute-start.16 = (f32[128,1024]{1,0:T(8,128)}, f32[128,1024]{1,0:T(8,128)S(1)}, u32[]{:S(2)}, u32[]{:S(2)}) collective-permute-start(f32[128,1024]{1,0:T(8,128)} %get-tuple-element.106), channel_id=1, source_target_pairs={{0,2},{2,0},{4,6},{6,4},{8,10},{10,8},{12,14},{14,12},{16,18},{18,... | collective-permute-start | bytes 1572872 | tf_op jit(solution)/shard_map/ppermute | solution.py:28
  75.5 9.2 %collective-permute-start.12 = (bf16[128,1024]{1,0:T(8,128)(2,1)}, bf16[128,1024]{1,0:T(8,128)(2,1)S(1)}, u32[]{:S(2)}, u32[]{:S(2)}) collective-permute-start(bf16[128,1024]{1,0:T(8,128)(2,1)} %get-tuple-element.87), channel_id=1, source_target_pairs={{0,2},{2,0},{4,6},{6,4},{8,10},{10,8},{12,14},{14,12},{16,18},{18,... | collective-permute-start | bytes 786440 | tf_op jit(solution)/shard_map/ppermute | solution.py:28
  75.8 8.9 %collective-permute-start.13 = (bf16[128,1024]{1,0:T(8,128)(2,1)}, bf16[128,1024]{1,0:T(8,128)(2,1)}, u32[]{:S(2)}, u32[]{:S(2)}) collective-permute-start(bf16[128,1024]{1,0:T(8,128)(2,1)} %get-tuple-element.89), channel_id=1, source_target_pairs={{0,2},{2,0},{4,6},{6,4},{8,10},{10,8},{12,14},{14,12},{16,18},{18,... | collective-permute-start | bytes 786440 | tf_op jit(solution)/shard_map/ppermute | solution.py:28
  76.0 1.7 %collective-permute-start.10 = (f32[16,128]{1,0:T(8,128)S(1)}, f32[16,128]{1,0:T(8,128)S(1)}, u32[]{:S(2)}, u32[]{:S(2)}) collective-permute-start(f32[16,128]{1,0:T(8,128)S(1)} %copy-done.13), channel_id=1, source_target_pairs={{0,2},{2,0},{4,6},{6,4},{8,10},{10,8},{12,14},{14,12},{16,18},{18,... | collective-permute-start | bytes 24584 | tf_op jit(solution)/shard_map/ppermute | solution.py:28
  77.7 15.0 %collective-permute-start.11 = (f32[2,16,128]{2,1,0:T(8,128)S(1)}, f32[2,16,128]{2,1,0:T(8,128)S(1)}, u32[]{:S(2)}, u32[]{:S(2)}) collective-permute-start(f32[2,16,128]{2,1,0:T(8,128)S(1)} %maximum_select_fusion), channel_id=1, source_target_pairs={{2,4},{6,8},{10,12},{14,16},{18,20},{22,24},{26,28},{30,32},{34,36... | collective-permute-start | bytes 49160 | tf_op jit(solution)/shard_map/ppermute | solution.py:34
  84.7 0.7 copy-start.10
  92.7 0.6 copy-start.11
  93.3 5.7 %collective-permute-start.14 = (f32[5,2,2048]{2,1,0:T(2,128)S(1)}, f32[5,2,2048]{2,1,0:T(2,128)S(1)}, u32[]{:S(2)}, u32[]{:S(2)}) collective-permute-start(f32[5,2,2048]{2,1,0:T(2,128)S(1)} %get-tuple-element.97), channel_id=1, source_target_pairs={{0,192},{2,194},{4,196},{6,198},{8,200},{10,202},{12,204},{14,206}... | collective-permute-start | bytes 245768 | tf_op jit(solution)/shard_map/ppermute | solution.py:28
  93.3 0.8 copy-start.4
  93.3 1.0 copy-start.5
  98.9 5.4 %collective-permute-start.17 = (f32[3,2,2048]{2,1,0:T(2,128)S(1)}, f32[3,2,2048]{2,1,0:T(2,128)S(1)}, u32[]{:S(2)}, u32[]{:S(2)}) collective-permute-start(f32[3,2,2048]{2,1,0:T(2,128)S(1)} %get-tuple-element.109), channel_id=1, source_target_pairs={{0,64},{2,66},{4,68},{6,70},{8,72},{10,74},{12,76},{14,78},{16,80}... | collective-permute-start | bytes 147464 | tf_op jit(solution)/shard_map/ppermute | solution.py:28
  104.3 5.0 %collective-permute-start.18 = (f32[2,2,2048]{2,1,0:T(2,128)S(1)}, f32[2,2,2048]{2,1,0:T(2,128)S(1)}, u32[]{:S(2)}, u32[]{:S(2)}) collective-permute-start(f32[2,2,2048]{2,1,0:T(2,128)S(1)} %get-tuple-element.115), channel_id=1, source_target_pairs={{0,32},{2,34},{4,36},{6,38},{8,40},{10,42},{12,44},{14,46},{16,48}... | collective-permute-start | bytes 98312 | tf_op jit(solution)/shard_map/ppermute | solution.py:28
  109.3 7.7 %collective-permute-start.19 = (f32[1,2,2048]{2,1,0:T(2,128)S(1)}, f32[1,2,2048]{2,1,0:T(2,128)S(1)}, u32[]{:S(2)}, u32[]{:S(2)}) collective-permute-start(f32[1,2,2048]{2,1,0:T(2,128)S(1)} %slice_add_fusion), channel_id=1, source_target_pairs={{0,1},{1,0},{2,3},{3,2},{4,5},{5,4},{6,7},{7,6},{8,9},{9,8},{10,11... | collective-permute-start | bytes 49160 | tf_op jit(solution)/shard_map/ppermute | solution.py:624

commit v5 on v4

--- a/solution.py
+++ b/solution.py
@@ -598,10 +598,10 @@
         ids, level_bias, (q, k, v, c), (sq, sk, sv, sc), x, sx, rows
     )
 
-    grads, x_qc = lax.optimization_barrier((grads, x_qc))
+    rstat = swap(sstat, SIB)
+    grads, x_qc, rstat = lax.optimization_barrier((grads, x_qc, rstat))
     grads = in_group(grads)
 
-    rstat = swap(sstat, SIB)
     stats = jnp.where(core == 0, jnp.stack([stat, rstat]), jnp.stack([rstat, stat]))
     x_stats = cross(stats)
     grads, x_stats = lax.optimization_barrier((grads, x_stats))

time: 119 us -> 119 us (level)
    unnamed x31 -> x29, local copies, waits for them, and re-layouts: 4.75 us -> 4.75 us
where the time goes in v5:
time: 119 us; the launch traced here: 118 us
  waiting for transfers between devices  45.1 us (38%)
  starting transfers between devices  39.8 us (33%)
  Pallas kernels  26.4 us (22%)
  local copies, waits for them, and re-layouts  4.78 us (4%)
    ppermute x3, starting transfers between devices, cross(): return lax.ppermute(x, 'seq', pairs + [(j, i) for i, j in pairs])  17.6 us
    ppermute x16, waiting for transfers between devices, swap(): lax.ppermute(x, 'seq', [(i, i ^ mask) for i in range(lax.axis_size('seq'))])  15.7 us
    ppermute x3, waiting for transfers between devices, cross(): return lax.ppermute(x, 'seq', pairs + [(j, i) for i, j in pairs])  15.4 us
    all_to_all x2, waiting for transfers between devices, in_group(): return lax.all_to_all(x, 'seq', 0, 0, axis_index_groups=groups)  13.8 us
    ppermute x16, starting transfers between devices, swap(): lax.ppermute(x, 'seq', [(i, i ^ mask) for i in range(lax.axis_size('seq'))])  9.31 us
    pallas_call x1, Pallas kernels, attend(): pl.pallas_call(functools.partial(attend_kernel, steps, heads), grid_spec=...  9.22 us
    pallas_call x2, Pallas kernels, edge(): pl.pallas_call(functools.partial(edge_kernel, half, heads), grid_spec=plt...  7.44 us
    all_to_all x2, starting transfers between devices, in_group(): return lax.all_to_all(x, 'seq', 0, 0, axis_index_groups=groups)  7.32 us
  transfers between devices with their start and end apart: 22, of which 12 were waited for; matrix products, arithmetic and copies ran while one was open for 0% of the time, Pallas kernels for 22%

profile of v5, /device:TPU:24, one launch (start us, length us, event | category | flops | bytes accessed | tf_op | source)
XLA Modules:
  0.0 117.8 jit_solution(2820091548305391108)
XLA Ops:
  0.6 0.0 copy-start
  0.6 1.0 copy-done
  1.7 1.0 copy-done.1
  2.7 0.5 shard_map.92
  3.2 3.4 %collective-permute-start = (bf16[1,2,2048]{2,1,0:T(2,128)(2,1)S(1)}, bf16[1,2,2048]{2,1,0:T(2,128)(2,1)S(1)}, u32[]{:S(2)}, u32[]{:S(2)}) collective-permute-start(bf16[1,2,2048]{2,1,0:T(2,128)(2,1)S(1)} %get-tuple-element.66), channel_id=1, source_target_pairs={{0,32},{2,34},{4,36},{6,38},{8,40},{10,42},{12,44},{14,46},{16,48}... | collective-permute-start | bytes 24584 | tf_op jit(solution)/shard_map/ppermute | solution.py:28
  6.6 0.1 pad_add_fusion.ids_ref
  6.7 2.4 %shard_map.94 = (bf16[256,2048]{1,0:T(8,128)(2,1)S(1)}, bf16[256,2048]{1,0:T(8,128)(2,1)S(1)}, bf16[128,1024]{1,0:T(8,128)(2,1)S(1)}, bf16[128,1024]{1,0:T(8,128...) custom-call(s32[3]{0:T(128)S(1)} %pad_add_fusion.ids_ref, bf16[128,2048]{1,0:T(8,128)(2,1)} %bitcast.18, ...), custom_call_target="tpu_custom_call" | custom-call | bytes 3300000 | tf_op jit(solution)/shard_map/pallas_call | solution.py:142
  9.1 5.1 %collective-permute-start.3 = (bf16[256,2048]{1,0:T(8,128)(2,1)S(1)}, bf16[256,2048]{1,0:T(8,128)(2,1)S(1)}, u32[]{:S(2)}, u32[]{:S(2)}) collective-permute-start(bf16[256,2048]{1,0:T(8,128)(2,1)S(1)} %get-tuple-element.67), channel_id=1, source_target_pairs={{2,4},{6,8},{10,12},{14,16},{18,20},{22,24},{26,28},{30,32},{34,36... | collective-permute-start | bytes 3145736 | tf_op jit(solution)/shard_map/ppermute | solution.py:34
  14.3 0.0 collective-permute-done
  14.3 0.5 collective-permute-start.1
  14.9 3.3 %collective-permute-done.1 = bf16[2,2,2048]{2,1,0:T(2,128)(2,1)S(1)} collective-permute-done((bf16[2,2,2048]{2,1,0:T(2,128)(2,1)S(1)}, bf16[2,2,2048]{2,1,0:T(2,128)(2,1)S(1)}, u32[]{:S(2)}, u32[]{:S(2)}) %collective-permute-start.1) | collective-permute-done | bytes 16416 | tf_op jit(solution)/shard_map/ppermute | solution.py:28
  18.2 0.1 collective-permute-start.2
  18.3 0.1 collective-permute-start.4
  18.4 0.5 collective-permute-start.5
  18.9 0.1 collective-permute-start.6
  19.0 4.4 %collective-permute-done.2.b_ref = bf16[4,2,2048]{2,1,0:T(2,128)(2,1)S(1)} collective-permute-done((bf16[4,2,2048]{2,1,0:T(2,128)(2,1)S(1)}, bf16[4,2,2048]{2,1,0:T(2,128)(2,1)S(1)}, u32[]{:S(2)}, u32[]{:S(2)}) %collective-permute-start.2) | collective-permute-done | bytes 32800 | tf_op jit(solution)/shard_map/ppermute | solution.py:28
  23.4 0.0 collective-permute-start.7
  23.4 1.1 shard_map.93
  24.5 0.0 collective-permute-done.4.sk_ref
  24.5 0.0 collective-permute-done.5.sv_ref
  24.5 0.0 collective-permute-done.6.sq_ref
  24.5 0.0 copy-start.8
  24.5 0.4 collective-permute-done.7.sc_ref
  24.9 0.7 copy-done.9
  25.6 4.4 %collective-permute-done.3.x_ref.xk_ref.xv_ref = bf16[256,2048]{1,0:T(8,128)(2,1)S(1)} collective-permute-done((bf16[256,2048]{1,0:T(8,128)(2,1)S(1)}, bf16[256,2048]{1,0:T(8,128)(2,1)S(1)}, u32[]{:S(2)}, u32[]{:S(2)}) %collective-permute-start.3) | collective-permute-done | bytes 1048608 | tf_op jit(solution)/shard_map/ppermute | solution.py:34
  30.1 3.7 %all-to-all-start = ((bf16[16,32,1024]{2,1,0:T(8,128)(2,1)}), bf16[16,32,1024]{2,1,0:T(8,128)(2,1)S(1)}, u32[]{:S(2)}, u32[]{:S(2)}) async-start(bf16[16,32,1024]{2,1,0:T(8,128)(2,1)} %shard_map.93), calls=%async_computation | async-start | bytes 2097152 | tf_op jit(solution)/shard_map/all_to_all | solution.py:40
  33.7 0.0 copy-start.3
  33.7 0.6 shard_map.95
  34.4 0.4 collective-permute-start.8
  34.7 1.8 %collective-permute-done.8.sxk_ref.sxv_ref = bf16[256,1024]{1,0:T(8,128)(2,1)} collective-permute-done((bf16[256,1024]{1,0:T(8,128)(2,1)S(1)}, bf16[256,1024]{1,0:T(8,128)(2,1)}, u32[]{:S(2)}, u32[]{:S(2)}) %collective-permute-start.8) | collective-permute-done | bytes 524320 | tf_op jit(solution)/shard_map/ppermute | solution.py:28
  36.5 13.8 %all-to-all-done.level_ref = bf16[16,32,1024]{2,1,0:T(8,128)(2,1)S(1)} async-done(((bf16[16,32,1024]{2,1,0:T(8,128)(2,1)}), bf16[16,32,1024]{2,1,0:T(8,128)(2,1)S(1)}, u32[]{:S(2)}, u32[]{:S(2)}) %all-to-all-start) | async-done | bytes 1048608 | tf_op jit(solution)/shard_map/all_to_all | solution.py:40
  50.3 5.5 %collective-permute-start.9 = (bf16[256,2048]{1,0:T(8,128)(2,1)S(1)}, bf16[256,2048]{1,0:T(8,128)(2,1)S(1)}, u32[]{:S(2)}, u32[]{:S(2)}) collective-permute-start(bf16[256,2048]{1,0:T(8,128)(2,1)S(1)} %get-tuple-element.82), channel_id=1, source_target_pairs={{2,4},{6,8},{10,12},{14,16},{18,20},{22,24},{26,28},{30,32},{34,36... | collective-permute-start | bytes 3145736 | tf_op jit(solution)/shard_map/ppermute | solution.py:34
  55.8 9.2 %shard_map.96 = (bf16[128,1024]{1,0:T(8,128)(2,1)}, bf16[128,1024]{1,0:T(8,128)(2,1)}, bf16[128,1024]{1,0:T(8,128)(2,1)}, bf16[128,1024]{1,0:T(8,128)(2,1)}, f32...) custom-call(s32[3]{0:T(128)S(1)} %pad_add_fusion.ids_ref, ...), custom_call_target="tpu_custom_call" | custom-call | bytes 29700000 | tf_op jit(solution)/shard_map/pallas_call | solution.py:365
  65.0 0.1 collective-permute-start.10
  65.1 1.4 %collective-permute-done.10 = f32[16,128]{1,0:T(8,128)S(1)} collective-permute-done((f32[16,128]{1,0:T(8,128)}, f32[16,128]{1,0:T(8,128)S(1)}, u32[]{:S(2)}, u32[]{:S(2)}) %collective-permute-start.10) | collective-permute-done | bytes 8224 | tf_op jit(solution)/shard_map/ppermute | solution.py:28
  66.5 4.7 %collective-permute-done.9.q_ref.c_ref = bf16[256,2048]{1,0:T(8,128)(2,1)S(1)} collective-permute-done((bf16[256,2048]{1,0:T(8,128)(2,1)S(1)}, bf16[256,2048]{1,0:T(8,128)(2,1)S(1)}, u32[]{:S(2)}, u32[]{:S(2)}) %collective-permute-start.9) | collective-permute-done | bytes 1048608 | tf_op jit(solution)/shard_map/ppermute | solution.py:34
  71.2 3.7 %all-to-all-start.1 = ((bf16[16,32,1024]{2,1,0:T(8,128)(2,1)}), bf16[16,32,1024]{2,1,0:T(8,128)(2,1)S(1)}, u32[]{:S(2)}, u32[]{:S(2)}) async-start(bf16[16,32,1024]{2,1,0:T(8,128)(2,1)} %get-tuple-element.84), calls=%async_computation.1 | async-start | bytes 2097152 | tf_op jit(solution)/shard_map/all_to_all | solution.py:40
  74.9 0.4 collective-permute-start.15
  75.3 0.2 collective-permute-start.16
  75.5 0.3 collective-permute-start.12
  75.8 0.2 collective-permute-start.13
  76.0 7.0 %collective-permute-start.11 = (f32[2,16,128]{2,1,0:T(8,128)S(1)}, f32[2,16,128]{2,1,0:T(8,128)S(1)}, u32[]{:S(2)}, u32[]{:S(2)}) collective-permute-start(f32[2,16,128]{2,1,0:T(8,128)S(1)} %maximum_select_fusion), channel_id=1, source_target_pairs={{2,4},{6,8},{10,12},{14,16},{18,20},{22,24},{26,28},{30,32},{34,36... | collective-permute-start | bytes 49160 | tf_op jit(solution)/shard_map/ppermute | solution.py:34
  83.0 0.0 collective-permute-done.12.satt_ref
  83.0 0.0 collective-permute-done.13.sdq_ref
  83.0 0.7 copy-done.10
  83.7 2.7 %shard_map.97 = (bf16[128,2048]{1,0:T(8,128)(2,1)}, bf16[128,2048]{1,0:T(8,128)(2,1)}) custom-call(s32[3]{0:T(128)S(1)} %pad_add_fusion.ids_ref, bf16[128,1024]{1,0:T(8,128)(2,1)} %get-tuple-element.88.att_ref, bf16[128,1024]{1,0:T(8,128)(2,1)} %copy-done.10, bf16[128,1024]{1,0:T(8,128)(2,1)} %get-tuple-element.90.dq_ref, ...), custom_call_target="tpu_custom_call" | custom-call | bytes 19800000 | tf_op jit(solution)/shard_map/pallas_call | solution.py:466
  86.4 6.2 %collective-permute-done.11.stat_ref = f32[2,16,128]{2,1,0:T(8,128)S(1)} collective-permute-done((f32[2,16,128]{2,1,0:T(8,128)S(1)}, f32[2,16,128]{2,1,0:T(8,128)S(1)}, u32[]{:S(2)}, u32[]{:S(2)}) %collective-permute-start.11) | collective-permute-done | bytes 16416 | tf_op jit(solution)/shard_map/ppermute | solution.py:34
  92.6 0.0 all-to-all-done.1
  92.6 0.4 shard_map.98
  93.1 0.2 copy-done.11
  93.3 0.8 copy-done.4
  94.0 0.2 copy-done.5
  94.2 3.7 %shard_map.100 = (f32[128,1024]{1,0:T(8,128)S(1)}, f32[128,1024]{1,0:T(8,128)S(1)}) custom-call(s32[3]{0:T(128)S(1)} %pad_add_fusion.ids_ref, f32[3,16]{1,0:T(4,128)S(1)} %copy-done.3, bf16[128,2048]{1,0:T(8,128)(2,1)} %bitcast.20, bf16[128,2048]{1,0:T(8,128)(2,1)} %bitcast.25, bf16[256,2048]{1,0:T(8,128)(2,1)S(1)} %collective-permute-done.9.q_ref.c_ref, ...), custom_call_target="tpu_custom_call" | custom-call | bytes 16500000 | tf_op jit(solution)/shard_map/pallas_call | solution.py:435
  98.0 0.9 collective-permute-done.14.got_ref
  98.9 1.6 %collective-permute-start.17 = (f32[3,2,2048]{2,1,0:T(2,128)S(1)}, f32[3,2,2048]{2,1,0:T(2,128)S(1)}, u32[]{:S(2)}, u32[]{:S(2)}) collective-permute-start(f32[3,2,2048]{2,1,0:T(2,128)S(1)} %get-tuple-element.111), channel_id=1, source_target_pairs={{0,64},{2,66},{4,68},{6,70},{8,72},{10,74},{12,76},{14,78},{16,80}... | collective-permute-start | bytes 147464 | tf_op jit(solution)/shard_map/ppermute | solution.py:28
  100.5 3.7 %shard_map.102 = (f32[128,1024]{1,0:T(8,128)S(1)}, f32[128,1024]{1,0:T(8,128)S(1)}) custom-call(s32[3]{0:T(128)S(1)} %pad_add_fusion.ids_ref, f32[3,16]{1,0:T(4,128)S(1)} %copy-done.3, bf16[128,2048]{1,0:T(8,128)(2,1)} %bitcast.21, bf16[128,2048]{1,0:T(8,128)(2,1)} %bitcast.26, bf16[256,2048]{1,0:T(8,128)(2,1)S(1)} %collective-permute-done.9.q_ref.c_ref, ...), custom_call_target="tpu_custom_call" | custom-call | bytes 16500000 | tf_op jit(solution)/shard_map/pallas_call | solution.py:435
  104.3 0.0 collective-permute-done.17.got_ref
  104.3 1.4 %collective-permute-start.18 = (f32[2,2,2048]{2,1,0:T(2,128)S(1)}, f32[2,2,2048]{2,1,0:T(2,128)S(1)}, u32[]{:S(2)}, u32[]{:S(2)}) collective-permute-start(f32[2,2,2048]{2,1,0:T(2,128)S(1)} %get-tuple-element.117), channel_id=1, source_target_pairs={{0,32},{2,34},{4,36},{6,38},{8,40},{10,42},{12,44},{14,46},{16,48}... | collective-permute-start | bytes 98312 | tf_op jit(solution)/shard_map/ppermute | solution.py:28
  105.7 3.6 %collective-permute-done.18.got_ref = f32[2,2,2048]{2,1,0:T(2,128)S(1)} collective-permute-done((f32[2,2,2048]{2,1,0:T(2,128)S(1)}, f32[2,2,2048]{2,1,0:T(2,128)S(1)}, u32[]{:S(2)}, u32[]{:S(2)}) %collective-permute-start.18) | collective-permute-done | bytes 32800 | tf_op jit(solution)/shard_map/ppermute | solution.py:28
  109.3 5.6 %collective-permute-start.19 = (f32[1,2,2048]{2,1,0:T(2,128)S(1)}, f32[1,2,2048]{2,1,0:T(2,128)S(1)}, u32[]{:S(2)}, u32[]{:S(2)}) collective-permute-start(f32[1,2,2048]{2,1,0:T(2,128)S(1)} %slice_add_fusion), channel_id=1, source_target_pairs={{0,1},{1,0},{2,3},{3,2},{4,5},{5,4},{6,7},{7,6},{8,9},{9,8},{10,11... | collective-permute-start | bytes 49160 | tf_op jit(solution)/shard_map/ppermute | solution.py:624
  115.0 1.9 %shard_map.103 = (bf16[128,2048]{1,0:T(8,128)(2,1)}, bf16[128,2048]{1,0:T(8,128)(2,1)}) custom-call(f32[16,2048]{1,0:T(8,128)S(1)} %get-tuple-element.97.one_ref, f32[1,2,2048]{2,1,0:T(2,128)S(1)} %get-tuple-element.113.far_ref, f32[2,2,2048]{2,1,0:T(2,128)S(1)} %collective-permute-done.18.got_ref, f32[128,1024]{1,0:T(8,128)S(1)} %get-tuple-element.118.dk_ref, ...), custom_call_target="tpu_custom_call" | custom-call | bytes 6600000 | tf_op jit(solution)/shard_map/pallas_call | solution.py:559
  116.8 0.2 collective-permute-done.19
  117.1 0.1 copy.11
  117.2 0.6 reduce_sum.9
  (29 shorter events, 0.2 us)
Async XLA Ops:
  0.6 1.0 copy-start
  1.7 1.0 copy-start.1
  3.2 11.0 %collective-permute-start = (bf16[1,2,2048]{2,1,0:T(2,128)(2,1)S(1)}, bf16[1,2,2048]{2,1,0:T(2,128)(2,1)S(1)}, u32[]{:S(2)}, u32[]{:S(2)}) collective-permute-start(bf16[1,2,2048]{2,1,0:T(2,128)(2,1)S(1)} %get-tuple-element.66), channel_id=1, source_target_pairs={{0,32},{2,34},{4,36},{6,38},{8,40},{10,42},{12,44},{14,46},{16,48}... | collective-permute-start | bytes 24584 | tf_op jit(solution)/shard_map/ppermute | solution.py:28
  9.1 20.9 %collective-permute-start.3 = (bf16[256,2048]{1,0:T(8,128)(2,1)S(1)}, bf16[256,2048]{1,0:T(8,128)(2,1)S(1)}, u32[]{:S(2)}, u32[]{:S(2)}) collective-permute-start(bf16[256,2048]{1,0:T(8,128)(2,1)S(1)} %get-tuple-element.67), channel_id=1, source_target_pairs={{2,4},{6,8},{10,12},{14,16},{18,20},{22,24},{26,28},{30,32},{34,36... | collective-permute-start | bytes 3145736 | tf_op jit(solution)/shard_map/ppermute | solution.py:34
  14.3 3.8 %collective-permute-start.1 = (bf16[2,2,2048]{2,1,0:T(2,128)(2,1)S(1)}, bf16[2,2,2048]{2,1,0:T(2,128)(2,1)S(1)}, u32[]{:S(2)}, u32[]{:S(2)}) collective-permute-start(bf16[2,2,2048]{2,1,0:T(2,128)(2,1)S(1)} %pad_maximum_fusion), channel_id=1, source_target_pairs={{0,64},{2,66},{4,68},{6,70},{8,72},{10,74},{12,76},{14,78},{16,80}... | collective-permute-start | bytes 49160 | tf_op jit(solution)/shard_map/ppermute | solution.py:28
  18.2 5.2 %collective-permute-start.2 = (bf16[4,2,2048]{2,1,0:T(2,128)(2,1)S(1)}, bf16[4,2,2048]{2,1,0:T(2,128)(2,1)S(1)}, u32[]{:S(2)}, u32[]{:S(2)}) collective-permute-start(bf16[4,2,2048]{2,1,0:T(2,128)(2,1)S(1)} %constant_dynamic-update-slice_fusion.a_ref), channel_id=1, source_target_pairs={{0,192},{2,194},{4,196},{6,198},{8,200},{10,202},{12,204},{14,206}... | collective-permute-start | bytes 98312 | tf_op jit(solution)/shard_map/ppermute | solution.py:28
  18.3 6.2 %collective-permute-start.4 = (bf16[128,1024]{1,0:T(8,128)(2,1)S(1)}, bf16[128,1024]{1,0:T(8,128)(2,1)S(1)}, u32[]{:S(2)}, u32[]{:S(2)}) collective-permute-start(bf16[128,1024]{1,0:T(8,128)(2,1)S(1)} %get-tuple-element.68), channel_id=1, source_target_pairs={{0,2},{2,0},{4,6},{6,4},{8,10},{10,8},{12,14},{14,12},{16,18},{18,... | collective-permute-start | bytes 786440 | tf_op jit(solution)/shard_map/ppermute | solution.py:28
  18.4 6.1 %collective-permute-start.5 = (bf16[128,1024]{1,0:T(8,128)(2,1)S(1)}, bf16[128,1024]{1,0:T(8,128)(2,1)S(1)}, u32[]{:S(2)}, u32[]{:S(2)}) collective-permute-start(bf16[128,1024]{1,0:T(8,128)(2,1)S(1)} %get-tuple-element.69), channel_id=1, source_target_pairs={{0,2},{2,0},{4,6},{6,4},{8,10},{10,8},{12,14},{14,12},{16,18},{18,... | collective-permute-start | bytes 786440 | tf_op jit(solution)/shard_map/ppermute | solution.py:28
  18.9 5.6 %collective-permute-start.6 = (bf16[128,1024]{1,0:T(8,128)(2,1)S(1)}, bf16[128,1024]{1,0:T(8,128)(2,1)S(1)}, u32[]{:S(2)}, u32[]{:S(2)}) collective-permute-start(bf16[128,1024]{1,0:T(8,128)(2,1)S(1)} %get-tuple-element.70), channel_id=1, source_target_pairs={{0,2},{2,0},{4,6},{6,4},{8,10},{10,8},{12,14},{14,12},{16,18},{18,... | collective-permute-start | bytes 786440 | tf_op jit(solution)/shard_map/ppermute | solution.py:28
  23.4 1.5 %collective-permute-start.7 = (bf16[128,1024]{1,0:T(8,128)(2,1)S(1)}, bf16[128,1024]{1,0:T(8,128)(2,1)S(1)}, u32[]{:S(2)}, u32[]{:S(2)}) collective-permute-start(bf16[128,1024]{1,0:T(8,128)(2,1)S(1)} %get-tuple-element.71), channel_id=1, source_target_pairs={{0,2},{2,0},{4,6},{6,4},{8,10},{10,8},{12,14},{14,12},{16,18},{18,... | collective-permute-start | bytes 786440 | tf_op jit(solution)/shard_map/ppermute | solution.py:28
  24.5 5.6 %copy-start.6 = (bf16[128,1024]{1,0:T(8,128)(2,1)}, bf16[128,1024]{1,0:T(8,128)(2,1)S(1)}, u32[]{:S(2)}) copy-start(bf16[128,1024]{1,0:T(8,128)(2,1)S(1)} %collective-permute-done.4.sk_ref) | copy-start | bytes 786436
  24.5 5.6 %copy-start.7 = (bf16[128,1024]{1,0:T(8,128)(2,1)}, bf16[128,1024]{1,0:T(8,128)(2,1)S(1)}, u32[]{:S(2)}) copy-start(bf16[128,1024]{1,0:T(8,128)(2,1)S(1)} %collective-permute-done.5.sv_ref) | copy-start | bytes 786436
  24.5 5.6 %copy-start.8 = (bf16[128,1024]{1,0:T(8,128)(2,1)}, bf16[128,1024]{1,0:T(8,128)(2,1)S(1)}, u32[]{:S(2)}) copy-start(bf16[128,1024]{1,0:T(8,128)(2,1)S(1)} %collective-permute-done.6.sq_ref) | copy-start | bytes 786436
  24.9 0.7 copy-start.9
  30.1 4.3 %copy-start.2 = (bf16[256,2048]{1,0:T(8,128)(2,1)}, bf16[256,2048]{1,0:T(8,128)(2,1)S(1)}, u32[]{:S(2)}) copy-start(bf16[256,2048]{1,0:T(8,128)(2,1)S(1)} %collective-permute-done.3.x_ref.xk_ref.xv_ref) | copy-start | bytes 3145732
  30.1 20.2 %all-to-all-start = ((bf16[16,32,1024]{2,1,0:T(8,128)(2,1)}), bf16[16,32,1024]{2,1,0:T(8,128)(2,1)S(1)}, u32[]{:S(2)}, u32[]{:S(2)}) async-start(bf16[16,32,1024]{2,1,0:T(8,128)(2,1)} %shard_map.93), calls=%async_computation | async-start | bytes 2097152 | tf_op jit(solution)/shard_map/all_to_all | solution.py:40
  33.7 22.0 %copy-start.3 = (f32[3,16]{1,0:T(4,128)S(1)}, f32[3,16]{1,0:T(4,128)}, u32[]{:S(2)}) copy-start(f32[3,16]{1,0:T(4,128)} %bias_ref.5) | copy-start | bytes 580
  34.4 2.1 %collective-permute-start.8 = (bf16[256,1024]{1,0:T(8,128)(2,1)S(1)}, bf16[256,1024]{1,0:T(8,128)(2,1)}, u32[]{:S(2)}, u32[]{:S(2)}) collective-permute-start(bf16[256,1024]{1,0:T(8,128)(2,1)S(1)} %shard_map.95), channel_id=1, source_target_pairs={{0,2},{2,0},{4,6},{6,4},{8,10},{10,8},{12,14},{14,12},{16,18},{18,... | collective-permute-start | bytes 1572872 | tf_op jit(solution)/shard_map/ppermute | solution.py:28
  50.3 20.9 %collective-permute-start.9 = (bf16[256,2048]{1,0:T(8,128)(2,1)S(1)}, bf16[256,2048]{1,0:T(8,128)(2,1)S(1)}, u32[]{:S(2)}, u32[]{:S(2)}) collective-permute-start(bf16[256,2048]{1,0:T(8,128)(2,1)S(1)} %get-tuple-element.82), channel_id=1, source_target_pairs={{2,4},{6,8},{10,12},{14,16},{18,20},{22,24},{26,28},{30,32},{34,36... | collective-permute-start | bytes 3145736 | tf_op jit(solution)/shard_map/ppermute | solution.py:34
  65.0 1.5 %collective-permute-start.10 = (f32[16,128]{1,0:T(8,128)}, f32[16,128]{1,0:T(8,128)S(1)}, u32[]{:S(2)}, u32[]{:S(2)}) collective-permute-start(f32[16,128]{1,0:T(8,128)} %get-tuple-element.83), channel_id=1, source_target_pairs={{0,2},{2,0},{4,6},{6,4},{8,10},{10,8},{12,14},{14,12},{16,18},{18,... | collective-permute-start | bytes 24584 | tf_op jit(solution)/shard_map/ppermute | solution.py:28
  71.2 21.4 %all-to-all-start.1 = ((bf16[16,32,1024]{2,1,0:T(8,128)(2,1)}), bf16[16,32,1024]{2,1,0:T(8,128)(2,1)S(1)}, u32[]{:S(2)}, u32[]{:S(2)}) async-start(bf16[16,32,1024]{2,1,0:T(8,128)(2,1)} %get-tuple-element.84), calls=%async_computation.1 | async-start | bytes 2097152 | tf_op jit(solution)/shard_map/all_to_all | solution.py:40
  74.9 1.1 copy-start.12
  74.9 18.4 %collective-permute-start.15 = (f32[128,1024]{1,0:T(8,128)}, f32[128,1024]{1,0:T(8,128)S(1)}, u32[]{:S(2)}, u32[]{:S(2)}) collective-permute-start(f32[128,1024]{1,0:T(8,128)} %get-tuple-element.106), channel_id=1, source_target_pairs={{0,2},{2,0},{4,6},{6,4},{8,10},{10,8},{12,14},{14,12},{16,18},{18,... | collective-permute-start | bytes 1572872 | tf_op jit(solution)/shard_map/ppermute | solution.py:28
  75.3 18.0 %collective-permute-start.16 = (f32[128,1024]{1,0:T(8,128)}, f32[128,1024]{1,0:T(8,128)S(1)}, u32[]{:S(2)}, u32[]{:S(2)}) collective-permute-start(f32[128,1024]{1,0:T(8,128)} %get-tuple-element.108), channel_id=1, source_target_pairs={{0,2},{2,0},{4,6},{6,4},{8,10},{10,8},{12,14},{14,12},{16,18},{18,... | collective-permute-start | bytes 1572872 | tf_op jit(solution)/shard_map/ppermute | solution.py:28
  75.5 7.5 %collective-permute-start.12 = (bf16[128,1024]{1,0:T(8,128)(2,1)}, bf16[128,1024]{1,0:T(8,128)(2,1)S(1)}, u32[]{:S(2)}, u32[]{:S(2)}) collective-permute-start(bf16[128,1024]{1,0:T(8,128)(2,1)} %get-tuple-element.89), channel_id=1, source_target_pairs={{0,2},{2,0},{4,6},{6,4},{8,10},{10,8},{12,14},{14,12},{16,18},{18,... | collective-permute-start | bytes 786440 | tf_op jit(solution)/shard_map/ppermute | solution.py:28
  75.8 7.2 %collective-permute-start.13 = (bf16[128,1024]{1,0:T(8,128)(2,1)}, bf16[128,1024]{1,0:T(8,128)(2,1)}, u32[]{:S(2)}, u32[]{:S(2)}) collective-permute-start(bf16[128,1024]{1,0:T(8,128)(2,1)} %get-tuple-element.91), channel_id=1, source_target_pairs={{0,2},{2,0},{4,6},{6,4},{8,10},{10,8},{12,14},{14,12},{16,18},{18,... | collective-permute-start | bytes 786440 | tf_op jit(solution)/shard_map/ppermute | solution.py:28
  76.0 16.6 %collective-permute-start.11 = (f32[2,16,128]{2,1,0:T(8,128)S(1)}, f32[2,16,128]{2,1,0:T(8,128)S(1)}, u32[]{:S(2)}, u32[]{:S(2)}) collective-permute-start(f32[2,16,128]{2,1,0:T(8,128)S(1)} %maximum_select_fusion), channel_id=1, source_target_pairs={{2,4},{6,8},{10,12},{14,16},{18,20},{22,24},{26,28},{30,32},{34,36... | collective-permute-start | bytes 49160 | tf_op jit(solution)/shard_map/ppermute | solution.py:34
  83.0 0.7 copy-start.10
  92.6 0.6 copy-start.11
  93.2 5.7 %collective-permute-start.14 = (f32[5,2,2048]{2,1,0:T(2,128)S(1)}, f32[5,2,2048]{2,1,0:T(2,128)S(1)}, u32[]{:S(2)}, u32[]{:S(2)}) collective-permute-start(f32[5,2,2048]{2,1,0:T(2,128)S(1)} %get-tuple-element.99), channel_id=1, source_target_pairs={{0,192},{2,194},{4,196},{6,198},{8,200},{10,202},{12,204},{14,206}... | collective-permute-start | bytes 245768 | tf_op jit(solution)/shard_map/ppermute | solution.py:28
  93.2 0.8 copy-start.4
  93.3 1.0 copy-start.5
  98.9 5.4 %collective-permute-start.17 = (f32[3,2,2048]{2,1,0:T(2,128)S(1)}, f32[3,2,2048]{2,1,0:T(2,128)S(1)}, u32[]{:S(2)}, u32[]{:S(2)}) collective-permute-start(f32[3,2,2048]{2,1,0:T(2,128)S(1)} %get-tuple-element.111), channel_id=1, source_target_pairs={{0,64},{2,66},{4,68},{6,70},{8,72},{10,74},{12,76},{14,78},{16,80}... | collective-permute-start | bytes 147464 | tf_op jit(solution)/shard_map/ppermute | solution.py:28
  104.3 5.0 %collective-permute-start.18 = (f32[2,2,2048]{2,1,0:T(2,128)S(1)}, f32[2,2,2048]{2,1,0:T(2,128)S(1)}, u32[]{:S(2)}, u32[]{:S(2)}) collective-permute-start(f32[2,2,2048]{2,1,0:T(2,128)S(1)} %get-tuple-element.117), channel_id=1, source_target_pairs={{0,32},{2,34},{4,36},{6,38},{8,40},{10,42},{12,44},{14,46},{16,48}... | collective-permute-start | bytes 98312 | tf_op jit(solution)/shard_map/ppermute | solution.py:28
  109.3 7.7 %collective-permute-start.19 = (f32[1,2,2048]{2,1,0:T(2,128)S(1)}, f32[1,2,2048]{2,1,0:T(2,128)S(1)}, u32[]{:S(2)}, u32[]{:S(2)}) collective-permute-start(f32[1,2,2048]{2,1,0:T(2,128)S(1)} %slice_add_fusion), channel_id=1, source_target_pairs={{0,1},{1,0},{2,3},{3,2},{4,5},{5,4},{6,7},{7,6},{8,9},{9,8},{10,11... | collective-permute-start | bytes 49160 | tf_op jit(solution)/shard_map/ppermute | solution.py:624
